TPU v7x, 32 devices: a whole 2x2x4 slice. The times are simulated.
32 devices in a mesh: groups: 2 (over y), expert: 4 (over z), dp: 4 (over x, core).
Axes of the slice: x: 2, y: 2, z: 4, core: 2. Of those that a mesh axis runs over, the one named last changes fastest.
Arguments:
- norm_input: bfloat16 [512, 1792], P(('groups', 'expert', 'dp')), parts along dimension 0, may hold values from -6 to 6
- out_grad: bfloat16 [512, 1792], P(('groups', 'expert', 'dp')), parts along dimension 0, may hold values from -6 to 6
- shared_out: bfloat16 [512, 1792], P(('groups', 'expert', 'dp')), parts along dimension 0, may hold values from -1.1953125 to 1.1953125
- expert_ids: int32 [512, 8], P(('groups', 'expert', 'dp')), parts along dimension 0, may hold values from 0 to 63, all different within a row; in each aligned block of 64 rows (0 to 63, 64 to 127, ...) at most 12 rows name the same one
- route_weight: bfloat16 [512, 8], P(('groups', 'expert', 'dp')), parts along dimension 0, may hold values from 0.019897461 to 0.5
- shared_gate: bfloat16 [1792], replicated, may hold values from -0.125 to 0.125
- w_gate: bfloat16 [64, 1792, 1536], P('expert', None, 'dp'), may hold values from -0.125 to 0.125
- w_up: bfloat16 [64, 1792, 1536], P('expert', None, 'dp'), may hold values from -0.125 to 0.125
- w_down: bfloat16 [64, 1536, 1792], P('expert', 'dp'), may hold values from -0.15625 to 0.15625
Outputs:
- input_grad: bfloat16 [512, 1792], P(('groups', 'expert', 'dp')), parts along dimension 0
- route_grad: float32 [512, 8], P(('groups', 'expert', 'dp')), parts along dimension 0
- gate_grad: float32 [3584], P('groups'), parts along dimension 0
There are 2 independent parts, one for each index of `groups`. A program takes and returns all parts, laid end to end along the dimension named above; an argument that names none is the same for every part. Nothing has to cross between parts.
Inputs may be any that keep to these rules, and one draw needn't show every extreme that they name: `expert_ids`: each token names 8 different experts. Tokens come in aligned blocks of 64 (rows 0 to 63, and so on); within a block no expert is named by more than 12 rows, and in some block one expert is named by exactly 12 rows.
All inputs are finite; a program needn't handle non-finite values.
Results may differ from a plain program's by a relative error of at most 0.013.
Values may be sent and summed in bfloat16 or wider, within the bound.
No kernel may reach another device: no remote copies, remote signals or barrier semaphores. Data moves between devices by JAX's collectives and lax.ppermute only.
A program may use at most 192 MiB of HBM per device.

v0:
```python
import jax
import jax.numpy as jnp
from jax import lax
from jax.sharding import PartitionSpec as P

EXPERTS = 64
TOPK = 8
CAP = 12


def slot_targets(group_ids):
    flat_ids = group_ids.reshape(-1)
    one_hot = (flat_ids[:, None] == jnp.arange(EXPERTS, dtype=jnp.int32)[None, :]).astype(jnp.int32)
    before = jnp.cumsum(one_hot, axis=0) - one_hot
    position = jnp.sum(before * one_hot, axis=1)
    return flat_ids * CAP + position


def on_device(
    norm_input, out_grad, shared_out, expert_ids, route_weight, shared_gate, w_gate, w_up, w_down
):
    features = norm_input.shape[1]
    group_norm, group_grad, group_codes, group_weight = (
        lax.all_gather(norm_input, "dp", axis=0, tiled=True),
        lax.all_gather(out_grad, "dp", axis=0, tiled=True),
        lax.all_gather(expert_ids.astype(jnp.bfloat16), "dp", axis=0, tiled=True),
        lax.all_gather(route_weight, "dp", axis=0, tiled=True),
    )
    group_ids = group_codes.astype(jnp.int32)
    group_tokens = group_norm.shape[0]
    target = slot_targets(group_ids)
    slots = jnp.arange(EXPERTS * CAP, dtype=jnp.int32)
    hits = (target[None, :] == slots[:, None]).astype(jnp.bfloat16)
    dispatch = hits.reshape(EXPERTS * CAP, group_tokens, TOPK).sum(axis=2)
    slot_norm = jnp.dot(dispatch, group_norm, preferred_element_type=jnp.float32).astype(
        jnp.bfloat16
    )
    slot_grad = jnp.dot(dispatch, group_grad, preferred_element_type=jnp.float32).astype(
        jnp.bfloat16
    )
    slot_norm = slot_norm.reshape(EXPERTS, CAP, features)
    slot_grad = slot_grad.reshape(EXPERTS, CAP, features)
    local_experts = w_gate.shape[0]
    quarter = CAP // lax.axis_size("dp")
    offset = lax.axis_index("dp") * quarter
    norm_share = lax.dynamic_slice_in_dim(slot_norm, offset, quarter, 1)
    grad_share = lax.dynamic_slice_in_dim(slot_grad, offset, quarter, 1)
    arrived_norm, arrived_grad = (
        lax.all_to_all(norm_share, "expert", split_axis=0, concat_axis=0, tiled=True),
        lax.all_to_all(grad_share, "expert", split_axis=0, concat_axis=0, tiled=True),
    )
    rows_in = lax.all_gather(arrived_norm, "dp", axis=1, tiled=True)
    grads_in = lax.all_gather(arrived_grad, "dp", axis=1, tiled=True)
    item_count = rows_in.shape[1]
    sources = rows_in.shape[0] // local_experts
    rows_four = rows_in.reshape(sources, local_experts, item_count, features)
    grads_four = grads_in.reshape(sources, local_experts, item_count, features)
    gate_pre = jnp.einsum("sxcd,xdf->sxcf", rows_four, w_gate, preferred_element_type=jnp.float32)
    up_pre = jnp.einsum("sxcd,xdf->sxcf", rows_four, w_up, preferred_element_type=jnp.float32)
    hidden_grad = jnp.einsum(
        "sxcd,xfd->sxcf", grads_four, w_down, preferred_element_type=jnp.float32
    )
    logistic = jax.nn.sigmoid(gate_pre)
    swish = gate_pre * logistic
    act = swish * up_pre
    gate_diff = (hidden_grad * up_pre * logistic * (1.0 + gate_pre * (1.0 - logistic))).astype(
        jnp.bfloat16
    )
    up_diff = (hidden_grad * swish).astype(jnp.bfloat16)
    row_part = jnp.einsum("sxcf,xdf->sxcd", gate_diff, w_gate, preferred_element_type=jnp.float32)
    row_part = row_part + jnp.einsum(
        "sxcf,xdf->sxcd", up_diff, w_up, preferred_element_type=jnp.float32
    )
    row_back = row_part.astype(jnp.bfloat16).reshape(sources * local_experts, item_count, features)
    score_back = jnp.sum(act * hidden_grad, axis=3).astype(jnp.bfloat16)
    score_back = score_back.reshape(sources * local_experts, item_count, 1)
    back_rows = lax.all_to_all(row_back, "expert", split_axis=0, concat_axis=0, tiled=True)
    back_scores = lax.all_to_all(score_back, "expert", split_axis=0, concat_axis=0, tiled=True)
    columns = back_rows.shape[2]
    back_flat = back_rows.reshape(EXPERTS * CAP, columns)
    score_flat = back_scores.reshape(EXPERTS * CAP)
    picked = jnp.take(back_flat, target, axis=0).reshape(group_tokens, TOPK, columns)
    token_part = jnp.einsum(
        "tk,tkd->td", group_weight.astype(jnp.float32), picked.astype(jnp.float32)
    )
    score_part = (
        jnp.take(score_flat, target, axis=0).astype(jnp.float32).reshape(group_tokens, TOPK)
    )
    routed, route_grad = (
        lax.psum_scatter(
            token_part.astype(jnp.bfloat16), "dp", scatter_dimension=0, tiled=True
        ).astype(jnp.float32),
        lax.psum_scatter(
            score_part.astype(jnp.bfloat16), "dp", scatter_dimension=0, tiled=True
        ).astype(jnp.float32),
    )
    gate_value = jax.nn.sigmoid(
        jnp.dot(norm_input, shared_gate, preferred_element_type=jnp.float32)
    )
    inner = jnp.sum(out_grad.astype(jnp.float32) * shared_out.astype(jnp.float32), axis=1)
    gate_delta = inner * gate_value * (1.0 - gate_value)
    input_grad = (routed + gate_delta[:, None] * shared_gate.astype(jnp.float32)[None, :]).astype(
        jnp.bfloat16
    )
    gate_local = jnp.dot(
        gate_delta, norm_input.astype(jnp.float32), precision=lax.Precision.HIGHEST
    )
    gate_grad = lax.psum(gate_local, ("expert", "dp"))
    return (input_grad, route_grad, gate_grad)


def solution(mesh):
    return jax.shard_map(
        on_device,
        mesh=mesh,
        in_specs=(
            P(("groups", "expert", "dp"), None),
            P(("groups", "expert", "dp"), None),
            P(("groups", "expert", "dp"), None),
            P(("groups", "expert", "dp"), None),
            P(("groups", "expert", "dp"), None),
            P(),
            P("expert", None, "dp"),
            P("expert", None, "dp"),
            P("expert", "dp", None),
        ),
        out_specs=(
            P(("groups", "expert", "dp"), None),
            P(("groups", "expert", "dp"), None),
            P("groups"),
        ),
        check_vma=False,
    )
```

profile of v0, /device:TPU:0, one launch (start us, length us, event | category | flops | bytes accessed | tf_op | source)
XLA Modules:
  0.0 326.7 jit_solution(10846611834491723466)
XLA Ops:
  7.9 6.1 %all-gather = bf16[4,16,8]{1,2,0:T(8,128)(2,1)S(1)} all-gather(bf16[1,16,8]{1,2,0:T(8,128)(2,1)S(1)} %convert_bitcast_fusion), channel_id=1, replica_groups=mesh['groups'=2,'expert'=4,'dp'=4] {'dp'}, dimensions={0}, use_global_device_ids=true | all-gather | bytes 1280 | tf_op jit(solution)/shard_map/all_gather | solution.py:26
  14.3 1.2 reduce-window.6
  16.8 6.3 %all_gather.21 = bf16[64,1792]{1,0:T(8,128)(2,1)S(1)} all-gather(bf16[16,1792]{1,0:T(8,128)(2,1)} %param.9), channel_id=1, replica_groups=mesh['groups'=2,'expert'=4,'dp'=4] {'dp'}, dimensions={0}, use_global_device_ids=true | all-gather | bytes 286720 | tf_op jit(solution)/shard_map/all_gather | solution.py:24
  23.1 0.9 convolution_convert_fusion
  24.0 2.5 reshape.127
  26.5 2.6 constant_dynamic-slice_fusion
  29.2 28.4 %all_to_all.20 = bf16[64,3,1792]{2,1,0:T(4,128)(2,1)S(1)} all-to-all(bf16[64,3,1792]{2,1,0:T(4,128)(2,1)S(1)} %constant_dynamic-slice_fusion), channel_id=1, replica_groups=mesh['groups'=2,'expert'=4,'dp'=4] {'expert'}, dimensions={0} | all-to-all | bytes 1376256 | tf_op jit(solution)/shard_map/all_to_all | solution.py:49
  57.5 0.9 copy.95
  58.5 5.7 %all_gather.19 = bf16[64,1792]{1,0:T(8,128)(2,1)S(1)} all-gather(bf16[16,1792]{1,0:T(8,128)(2,1)S(1)} %copy-done.1), channel_id=1, replica_groups=mesh['groups'=2,'expert'=4,'dp'=4] {'dp'}, dimensions={0}, use_global_device_ids=true | all-gather | bytes 286720 | tf_op jit(solution)/shard_map/all_gather | solution.py:25
  64.2 0.9 convolution_convert_fusion.1
  65.1 2.5 reshape.125
  67.7 2.6 constant_dynamic-slice_fusion.1
  70.3 26.1 %all_to_all.21 = bf16[64,3,1792]{2,1,0:T(4,128)(2,1)S(1)} all-to-all(bf16[64,3,1792]{2,1,0:T(4,128)(2,1)S(1)} %constant_dynamic-slice_fusion.1), channel_id=1, replica_groups=mesh['groups'=2,'expert'=4,'dp'=4] {'expert'}, dimensions={0} | all-to-all | bytes 1376256 | tf_op jit(solution)/shard_map/all_to_all | solution.py:50
  96.4 0.9 copy.93
  97.4 13.7 %fusion.2 = f32[16,4,12,384]{3,2,1,0:T(8,128)S(1)} fusion(bf16[16,1792,384]{2,1,0:T(8,128)(2,1)} %param.15, bf16[4,16,12,1792]{3,1,0,2:T(8,128)(2,1)} %bitcast.136), kind=kOutput, calls=%fused_computation.4 | convolution fusion | flops 1056964608 | bytes 25952256 | tf_op jit(solution)/shard_map/sxcd,xdf->sxcf/dot_general | solution.py:58
  111.1 10.9 %all-gather.5.cloned.1.call-done = bf16[64,12,1792]{2,0,1:T(8,128)(2,1)} async-done(((bf16[64,3,1792]{2,0,1:T(8,128)(2,1)}), bf16[64,12,1792]{2,0,1:T(8,128)(2,1)}) %all-gather.5.cloned.1.call-update) | async-done | bytes 2752528 | tf_op jit(solution)/shard_map/all_gather | solution.py:53
  122.0 12.3 %fusion.4 = f32[16,4,12,384]{3,2,1,0:T(8,128)S(1)} fusion(bf16[16,384,1792]{2,1,0:T(8,128)(2,1)} %param.17, bf16[4,16,12,1792]{3,1,0,2:T(8,128)(2,1)} %bitcast.139), kind=kOutput, calls=%fused_computation.6 | convolution fusion | flops 1056964608 | bytes 25952256 | tf_op jit(solution)/shard_map/sxcd,xfd->sxcf/dot_general | solution.py:60
  134.3 14.1 %fusion.28 = (bf16[4,16,12]{2,0,1:T(4,128)(2,1)S(1)}, f32[16,4,12,384]{3,2,1,0:T(8,128)}) fusion(f32[16,4,12,384]{3,2,1,0:T(8,128)S(1)} %fusion.4, f32[16,4,12,384]{3,2,1,0:T(8,128)S(1)} %fusion.2, bf16[16,1792,384]{2,1,0:T(8,128)(2,1)} %param.16, bf16[4,16,12,1792]{3,1,0,2:T(8,128)(2,1)S(1)} %bitcast.137), kind=kOutput, calls=%fused_computation.35 | convolution fusion | flops 1059028224 | bytes 28313088 | tf_op jit(solution)/shard_map/sxcd,xdf->sxcf/dot_general | solution.py:59
  148.5 13.9 %fusion = f32[16,4,12,1792]{3,2,1,0:T(8,128)} fusion(bf16[16,1792,384]{2,1,0:T(8,128)(2,1)} %param.15, f32[16,4,12,384]{3,2,1,0:T(8,128)S(1)} %fusion.2, f32[16,4,12,384]{3,2,1,0:T(8,128)} %get-tuple-element.6, f32[16,4,12,384]{3,2,1,0:T(8,128)S(1)} %fusion.4), kind=kOutput, calls=%fused_computation.2 | convolution fusion | flops 1059913728 | bytes 31064064 | tf_op jit(solution)/shard_map/sxcf,xdf->sxcd/dot_general | solution.py:70
  163.3 4.6 %all-to-all-start.3 = ((bf16[64,12,1]{1,2,0:T(2,128)(2,1)}), bf16[64,12,1]{1,2,0:T(2,128)(2,1)S(1)}, u32[]{:S(2)}, u32[]{:S(2)}) async-start(bf16[64,12,1]{1,2,0:T(2,128)(2,1)} %copy.103), calls=%async_computation.4 | async-start | bytes 65536 | tf_op jit(solution)/shard_map/all_to_all | solution.py:78
  167.9 14.2 %fusion.15 = bf16[4,16,12,1792]{3,2,0,1:T(8,128)(2,1)} fusion(f32[16,4,12,1792]{3,2,1,0:T(8,128)} %fusion, bf16[16,1792,384]{2,1,0:T(8,128)(2,1)} %param.16, f32[16,4,12,384]{3,2,1,0:T(8,128)S(1)} %fusion.4, f32[16,4,12,384]{3,2,1,0:T(8,128)S(1)} %fusion.2), kind=kOutput, calls=%fused_computation.18 | convolution fusion | flops 1061486592 | bytes 32636928 | tf_op jit(solution)/shard_map/sxcf,xdf->sxcd/dot_general | solution.py:71
  182.1 3.5 %copy.98 = bf16[4,16,12,1792]{3,1,0,2:T(8,128)(2,1)S(1)} copy(bf16[4,16,12,1792]{3,2,0,1:T(8,128)(2,1)} %fusion.15) | data formatting | bytes 5505024 | tf_op jit(solution)/shard_map/convert_element_type | solution.py:74
  185.6 3.4 %copy.99 = bf16[64,12,1792]{2,1,0:T(8,128)(2,1)} copy(bf16[64,12,1792]{2,0,1:T(8,128)(2,1)S(1)} %bitcast.138) | data formatting | bytes 5505024 | tf_op jit(solution)/shard_map/reshape | solution.py:74
  189.0 5.2 %all-to-all-start.2 = ((bf16[64,12,1792]{2,1,0:T(8,128)(2,1)}), bf16[64,12,1792]{2,1,0:T(8,128)(2,1)}, u32[]{:S(2)}, u32[]{:S(2)}) async-start(bf16[64,12,1792]{2,1,0:T(8,128)(2,1)} %copy.99), calls=%async_computation.2 | async-start | bytes 7340032 | tf_op jit(solution)/shard_map/all_to_all | solution.py:77
  194.4 5.2 %all-gather.1 = bf16[4,16,8]{1,2,0:T(8,128)(2,1)S(1)} all-gather(bf16[1,16,8]{1,2,0:T(8,128)(2,1)S(1)} %bitcast.143), channel_id=1, replica_groups=mesh['groups'=2,'expert'=4,'dp'=4] {'dp'}, dimensions={0}, use_global_device_ids=true | all-gather | bytes 1280 | tf_op jit(solution)/shard_map/all_gather | solution.py:27
  200.0 3.5 %gather_fusion.1 = bf16[512]{0:T(512)(128)(2,1)S(1)} fusion(bf16[768]{0:T(1024)(128)(2,1)S(1)} %reshape.131, s32[1024]{0:T(1024)S(1)} %pad_clamp_fusion), kind=kCustom, calls=%fused_computation.1 | custom fusion | bytes 4096 | tf_op jit(solution)/shard_map/jit(_take)/gather | solution.py:87
  204.6 71.6 %all-to-all-done.2 = bf16[64,12,1792]{2,1,0:T(8,128)(2,1)} async-done(((bf16[64,12,1792]{2,1,0:T(8,128)(2,1)}), bf16[64,12,1792]{2,1,0:T(8,128)(2,1)}, u32[]{:S(2)}, u32[]{:S(2)}) %all-to-all-start.2) | async-done | bytes 2752544 | tf_op jit(solution)/shard_map/all_to_all | solution.py:77
  276.3 3.8 %reshape.130 = bf16[768,1792]{1,0:T(8,128)(2,1)S(1)} reshape(bf16[64,12,1792]{2,1,0:T(8,128)(2,1)} %all-to-all-done.2) | data formatting | bytes 5505024 | tf_op jit(solution)/shard_map/reshape | solution.py:80
  280.1 3.2 gather_fusion
  283.3 2.2 fusion.18
  286.7 30.6 %psum.7 = f32[1792]{0:T(1024)} all-reduce(f32[1792]{0:T(1024)S(1)} %convolution_reduce_fusion), channel_id=1, replica_groups=mesh['groups'=2,'expert'=4,'dp'=4] {'expert','dp'}, use_global_device_ids=true, to_apply=%region_8.9 | all-reduce | flops 1792 | bytes 14336 | tf_op jit(solution)/shard_map/psum | solution.py:108
  318.6 1.5 add_convert_fusion.1
  (67 shorter events, 7.5 us)
Async XLA Ops:
  7.2 90.2 %all-gather.7.cloned.1.call-start = ((), (), s32[]{:S(2)}) async-start(), calls=%async_computation.7 | async-start | bytes 3440640 | tf_op jit(solution)/shard_map/all_gather | solution.py:52
  29.1 29.4 %copy-start.1 = (bf16[16,1792]{1,0:T(8,128)(2,1)S(1)}, bf16[16,1792]{1,0:T(8,128)(2,1)}, u32[]{:S(2)}) copy-start(bf16[16,1792]{1,0:T(8,128)(2,1)} %param.10) | copy-start | bytes 172036
  58.5 63.5 %all-gather.5.cloned.1.call-start = ((), (), s32[]{:S(2)}) async-start(), calls=%async_computation.6 | async-start | bytes 3440640 | tf_op jit(solution)/shard_map/all_gather | solution.py:53
  122.0 12.3 %copy-start = (bf16[64,12,1792]{2,0,1:T(8,128)(2,1)S(1)}, bf16[64,12,1792]{2,0,1:T(8,128)(2,1)}, u32[]{:S(2)}) copy-start(bf16[64,12,1792]{2,0,1:T(8,128)(2,1)} %all-gather.7.cloned.1.call-done) | copy-start | bytes 8257540
  163.3 25.7 %all-to-all-start.3 = ((bf16[64,12,1]{1,2,0:T(2,128)(2,1)}), bf16[64,12,1]{1,2,0:T(2,128)(2,1)S(1)}, u32[]{:S(2)}, u32[]{:S(2)}) async-start(bf16[64,12,1]{1,2,0:T(2,128)(2,1)} %copy.103), calls=%async_computation.4 | async-start | bytes 65536 | tf_op jit(solution)/shard_map/all_to_all | solution.py:78
  189.0 5.3 %copy-start.4 = (bf16[1792]{0:T(1024)(128)(2,1)S(1)}, bf16[1792]{0:T(1024)(128)(2,1)}, u32[]{:S(2)}) copy-start(bf16[1792]{0:T(1024)(128)(2,1)} %param.14) | copy-start | bytes 10756
  189.0 5.4 %copy-start.5 = (bf16[16,8]{0,1:T(8,128)(2,1)S(1)}, bf16[16,8]{0,1:T(8,128)(2,1)}, u32[]{:S(2)}) copy-start(bf16[16,8]{0,1:T(8,128)(2,1)} %param.13) | copy-start | bytes 772
  189.0 87.3 %all-to-all-start.2 = ((bf16[64,12,1792]{2,1,0:T(8,128)(2,1)}), bf16[64,12,1792]{2,1,0:T(8,128)(2,1)}, u32[]{:S(2)}, u32[]{:S(2)}) async-start(bf16[64,12,1792]{2,1,0:T(8,128)(2,1)} %copy.99), calls=%async_computation.2 | async-start | bytes 7340032 | tf_op jit(solution)/shard_map/all_to_all | solution.py:77
  194.2 123.0 %reduce-scatter.7.cloned.1.call-start = ((), (), s32[]{:S(2)}) async-start(), calls=%async_computation.9 | async-start | bytes 20480
  204.6 114.0 %reduce-scatter.5.cloned.1.call-start = ((), (), s32[]{:S(2)}) async-start(), calls=%async_computation.8 | async-start | bytes 286720 | tf_op jit(solution)/shard_map/reduce_scatter | solution.py:90
  283.3 2.9 copy-start.3
  283.3 3.1 copy-start.2
Sparse Core Ops, SparseCore 0:
  58.6 24.8 all-gather.6
  97.5 24.4 all-gather.4
  204.7 19.8 reduce-scatter.6
  286.3 18.0 reduce-scatter.4
where the time goes:
time: 328 us; the launch traced here: 327 us
  blocking collectives  108 us (33%)
  waiting for transfers between devices  82.6 us (25%)
  matrix products  72.5 us (22%)
  local copies, waits for them, and re-layouts  34.3 us (10%)
  between operations  14 us (4%)
  starting transfers between devices  9.94 us (3%)
  other arithmetic  5.01 us (2%)
    all_to_all x1, waiting for transfers between devices, on_device(): lax.all_to_all(row_back, 'expert', split_axis=0, concat_axis=0, tiled=True)  71.6 us
    psum x1, blocking collectives, on_device(): gate_grad = lax.psum(gate_local, ('expert', 'dp'))  30.6 us
    all_to_all x1, blocking collectives, on_device(): lax.all_to_all(norm_share, 'expert', split_axis=0, concat_axis=0, tiled=T...  28.4 us
    all_to_all x1, blocking collectives, on_device(): lax.all_to_all(grad_share, 'expert', split_axis=0, concat_axis=0, tiled=T...  26.1 us
    dot_general x1, matrix products, on_device(): jnp.einsum('sxcf,xdf->sxcd', up_diff, w_up, preferred_element_type=jnp.fl...  14.2 us
    dot_general x1, matrix products, on_device(): jnp.einsum('sxcd,xdf->sxcf', rows_four, w_up, preferred_element_type=jnp....  14.1 us
    dot_general x1, matrix products, on_device(): jnp.einsum('sxcf,xdf->sxcd', gate_diff, w_gate, preferred_element_type=jn...  13.9 us
    dot_general x1, matrix products, on_device(): jnp.einsum('sxcd,xdf->sxcf', rows_four, w_gate, preferred_element_type=jn...  13.7 us
  transfers between devices with their start and end apart: 6, of which 2 were waited for; matrix products, arithmetic and copies ran while one was open for 18% of the time, Pallas kernels for 0%

commit v1 on v0

--- a/solution.py
+++ b/solution.py
@@ -1,11 +1,20 @@
+import functools
+
 import jax
 import jax.numpy as jnp
 from jax import lax
+from jax.experimental import pallas as pl
+from jax.experimental.pallas import tpu as pltpu
 from jax.sharding import PartitionSpec as P
 
 EXPERTS = 64
 TOPK = 8
 CAP = 12
+LANES = 128
+BF16 = jnp.bfloat16
+F32 = jnp.float32
+NT = (((1,), (1,)), ((), ()))
+TN = (((0,), (0,)), ((), ()))
 
 
 def slot_targets(group_ids):
@@ -16,7 +25,7 @@
     return flat_ids * CAP + position
 
 
-def on_device(
+def general_device(
     norm_input, out_grad, shared_out, expert_ids, route_weight, shared_gate, w_gate, w_up, w_down
 ):
     features = norm_input.shape[1]
@@ -109,7 +118,164 @@
     return (input_grad, route_grad, gate_grad)
 
 
+def dot(a, b, dims=(((1,), (0,)), ((), ()))):
+    return lax.dot_general(a, b, dims, preferred_element_type=F32)
+
+
+def swap(value, axis, distance):
+    size = lax.axis_size(axis)
+    return lax.ppermute(value, axis, [(i, i ^ distance) for i in range(size)])
+
+
+def experts_kernel(features, rows, blocks, *refs):
+    token_refs, refs = refs[:blocks], refs[blocks:]
+    tail_ref, w_gate, w_up, w_down, keep_ref, send_ref, tokens, copied, spread, weighted, norms, grads, backs, hits, routes = refs
+    step, steps = pl.program_id(0), pl.num_programs(0)
+    each = token_refs[0].shape[0]
+    count = each * blocks
+
+    @pl.when(step == 0)
+    def _():
+        copies = [
+            pltpu.make_async_copy(ref, tokens.at[pl.ds(j * each, each)], copied.at[j])
+            for j, ref in enumerate(token_refs)
+        ]
+        for copy in copies:
+            copy.start()
+        for copy in copies:
+            copy.wait()
+        codes = tokens[:, 2 * features :].astype(F32).T
+        named = codes[:TOPK]
+        weights = codes[TOPK : 2 * TOPK]
+        first = (lax.axis_index("expert") * steps).astype(F32)
+        hits[...] = named - first
+        local = named - first
+        earlier = (
+            lax.broadcasted_iota(jnp.int32, (count, count), 0)
+            < lax.broadcasted_iota(jnp.int32, (count, count), 1)
+        ).astype(BF16)
+        number = spread.shape[0] // rows
+        masks = [local == float(e) for e in range(number)]
+        member = jnp.concatenate(
+            [jnp.sum(m.astype(F32), axis=0, keepdims=True) for m in masks], axis=0
+        )
+        position = dot(member.astype(BF16), earlier)
+        slot = lax.broadcasted_iota(jnp.int32, (rows, count), 0).astype(F32)
+        for e in range(number):
+            weight = jnp.sum(jnp.where(masks[e], weights, 0.0), axis=0, keepdims=True)
+            chosen = (slot == position[e : e + 1]) & (member[e : e + 1] > 0.0)
+            spread[e * rows : (e + 1) * rows] = jnp.where(chosen, 1.0, 0.0).astype(BF16)
+            weighted[e * rows : (e + 1) * rows] = jnp.where(chosen, weight, 0.0).astype(BF16)
+        norms[...] = dot(spread[...], tokens[:, :features]).astype(BF16)
+        grads[...] = dot(spread[...], tokens[:, features : 2 * features]).astype(BF16)
+        routes[...] = jnp.zeros_like(routes)
+
+    here = pl.ds(pl.multiple_of(step * rows, rows), rows)
+    x, dy = norms[here], grads[here]
+    gate_pre = dot(x, w_gate[0])
+    up_pre = dot(x, w_up[0])
+    hidden_grad = dot(dy, w_down[0], NT)
+    logistic = jax.nn.sigmoid(gate_pre)
+    swish = gate_pre * logistic
+    gate_diff = (hidden_grad * up_pre * logistic * (1.0 + gate_pre * (1.0 - logistic))).astype(BF16)
+    up_diff = (hidden_grad * swish).astype(BF16)
+    backs[here] = (dot(gate_diff, w_gate[0], NT) + dot(up_diff, w_up[0], NT)).astype(BF16)
+    score = jnp.sum(swish * up_pre * hidden_grad, axis=1, keepdims=True)
+    by_token = jnp.sum(spread[here].astype(F32) * score, axis=0, keepdims=True)
+    routes[...] += jnp.where(hits[...] == step.astype(F32), by_token, 0.0)
+
+    @pl.when(step == steps - 1)
+    def _():
+        half = count // 2
+        result = dot(weighted[...], backs[...], TN).astype(BF16)
+        scores = jnp.concatenate([routes[...], jnp.zeros((LANES - TOPK, count), F32)], axis=0).T
+        tail = jnp.concatenate([tail_ref[...]] * blocks, axis=0)
+        last = (scores + tail).astype(BF16)
+        keep_ref[:, :features] = result[:half]
+        send_ref[:, :features] = result[half:]
+        keep_ref[:, features:] = last[:half]
+        send_ref[:, features:] = last[half:]
+
+
+def run_experts(token_blocks, tail, w_gate, w_up, w_down, sources):
+    local, features, hidden = w_gate.shape
+    blocks = len(token_blocks)
+    count = blocks * token_blocks[0].shape[0]
+    rows = sources * CAP
+    width = features + LANES
+    return pl.pallas_call(
+        functools.partial(experts_kernel, features, rows, blocks),
+        grid=(local,),
+        in_specs=[pl.BlockSpec(memory_space=pl.ANY)] * blocks
+        + [
+            pl.BlockSpec(tail.shape, lambda i: (0, 0)),
+            pl.BlockSpec((1, features, hidden), lambda i: (i, 0, 0)),
+            pl.BlockSpec((1, features, hidden), lambda i: (i, 0, 0)),
+            pl.BlockSpec((1, hidden, features), lambda i: (i, 0, 0)),
+        ],
+        out_specs=[pl.BlockSpec((count // 2, width), lambda i: (0, 0))] * 2,
+        out_shape=[jax.ShapeDtypeStruct((count // 2, width), BF16)] * 2,
+        scratch_shapes=[
+            pltpu.VMEM((count, 2 * features + LANES), BF16),
+            pltpu.SemaphoreType.DMA((blocks,)),
+            pltpu.VMEM((local * rows, count), BF16),
+            pltpu.VMEM((local * rows, count), BF16),
+            pltpu.VMEM((local * rows, features), BF16),
+            pltpu.VMEM((local * rows, features), BF16),
+            pltpu.VMEM((local * rows, features), BF16),
+            pltpu.VMEM((TOPK, count), F32),
+            pltpu.VMEM((TOPK, count), F32),
+        ],
+        compiler_params=pltpu.CompilerParams(vmem_limit_bytes=48 << 20),
+        name="experts",
+    )(*token_blocks, tail, w_gate, w_up, w_down)
+
+
+def square_device(
+    norm_input, out_grad, shared_out, expert_ids, route_weight, shared_gate, w_gate, w_up, w_down
+):
+    tokens, features = norm_input.shape
+    sources = lax.axis_size("expert")
+    codes = jnp.concatenate(
+        [
+            expert_ids.astype(BF16),
+            route_weight,
+            jnp.zeros((tokens, LANES - 2 * TOPK), BF16),
+        ],
+        axis=1,
+    )
+    mine = jnp.concatenate([norm_input, out_grad, codes], axis=1)
+    held = [mine] + [swap(mine, "expert", d) for d in range(1, sources)]
+    held = held + [swap(block, "dp", 2) for block in held]
+    held = held + [swap(block, "dp", 1) for block in held]
+
+    gate_value = jax.nn.sigmoid(
+        jnp.dot(norm_input, shared_gate, preferred_element_type=F32)
+    )
+    inner = jnp.sum(out_grad.astype(F32) * shared_out.astype(F32), axis=1)
+    gate_delta = inner * gate_value * (1.0 - gate_value)
+    gate_local = jnp.sum(gate_delta[:, None] * norm_input.astype(F32), axis=0)
+    share = features // tokens
+    tail = jnp.pad(gate_local.reshape(tokens, share), ((0, 0), (TOPK, LANES - TOPK - share)))
+
+    kept, sent = run_experts(held, tail, w_gate, w_up, w_down, sources)
+    total = (kept.astype(F32) + swap(sent, "dp", 1).astype(F32)).astype(BF16)
+    half = total.shape[0] // 2
+    total = (total[:half].astype(F32) + swap(total[half:], "dp", 2).astype(F32)).astype(BF16)
+    final = total[:tokens].astype(F32)
+    for d in range(1, sources):
+        final = final + swap(total[d * tokens : (d + 1) * tokens], "expert", d).astype(F32)
+    input_grad = (
+        final[:, :features] + gate_delta[:, None] * shared_gate.astype(F32)[None, :]
+    ).astype(BF16)
+    route_grad = final[:, features : features + TOPK]
+    gate_grad = final[:, features + TOPK : features + TOPK + share].reshape(features)
+    return (input_grad, route_grad, gate_grad)
+
+
 def solution(mesh):
+    square = mesh.shape["expert"] == 4 and mesh.shape["dp"] == 4
+    on_device = square_device if square else general_device
     return jax.shard_map(
         on_device,
         mesh=mesh,

time: 328 us -> 90.6 us (0.28)
  blocking collectives: 108 us -> 0 us
  matrix products: 72.5 us -> 0.94 us
  waiting for transfers between devices: 82.6 us -> 21.1 us
  Pallas kernels: 0 us -> 41.1 us
  local copies, waits for them, and re-layouts: 34.3 us -> 4.08 us
  between operations: 14 us -> 0.73 us
  starting transfers between devices: 9.94 us -> 18.6 us
    all_to_all x2 -> x0, waiting for transfers between devices: 71.6 us -> none  [the longest x1 71.6 us: on_device(): lax.all_to_all(row_back, 'expert', split_axis=0, concat_axis=0, tiled=True)]
    dot_general x10 -> x1, matrix products: 72.5 us -> 0.94 us  [square_device(): jnp.dot(norm_input, shared_gate, preferred_element_type=F32)]
    all_to_all x2 -> x0, blocking collectives: 54.5 us -> none  [the longest x1 28.4 us: on_device(): lax.all_to_all(norm_share, 'expert', split_axis=0, concat_axis=0, tiled=T...]
    pallas_call x0 -> x1, Pallas kernels: none -> 41.1 us  [run_experts(): pl.pallas_call(functools.partial(experts_kernel, features, rows, blocks),...]
    psum x1 -> x0, blocking collectives: 30.6 us -> none  [on_device(): gate_grad = lax.psum(gate_local, ('expert', 'dp'))]
    all_gather x4 -> x0, blocking collectives: 23.2 us -> none  [the longest x1 6.28 us: on_device(): lax.all_gather(norm_input, 'dp', axis=0, tiled=True)]
    ppermute x0 -> x20, waiting for transfers between devices: none -> 21.1 us  [swap(): return lax.ppermute(value, axis, [(i, i ^ distance) for i in range(size)])]
    ppermute x0 -> x20, starting transfers between devices: none -> 18.6 us  [swap(): return lax.ppermute(value, axis, [(i, i ^ distance) for i in range(size)])]
  transfers between devices with their start and end apart: 6 -> 20, of which waited for: 2 -> 9; matrix products, arithmetic and copies ran while one was open for 18% -> 4% of each run, Pallas kernels for 0% -> 0%
where the time goes in v1:
time: 90.6 us; the launch traced here: 90.1 us
  Pallas kernels  41.1 us (45%)
  waiting for transfers between devices  21.1 us (23%)
  starting transfers between devices  18.6 us (21%)
  local copies, waits for them, and re-layouts  4.08 us (5%)
  other arithmetic  3.51 us (4%)
  matrix products  0.94 us (1%)
    pallas_call x1, Pallas kernels, run_experts(): pl.pallas_call(functools.partial(experts_kernel, features, rows, blocks),...  41.1 us
    ppermute x20, waiting for transfers between devices, swap(): return lax.ppermute(value, axis, [(i, i ^ distance) for i in range(size)])  21.1 us
    ppermute x20, starting transfers between devices, swap(): return lax.ppermute(value, axis, [(i, i ^ distance) for i in range(size)])  18.6 us
    unnamed x5, local copies, waits for them, and re-layouts  2.12 us
  transfers between devices with their start and end apart: 20, of which 9 were waited for; matrix products, arithmetic and copies ran while one was open for 4% of the time, Pallas kernels for 0%

profile of v1, /device:TPU:0, one launch (start us, length us, event | category | flops | bytes accessed | tf_op | source)
XLA Modules:
  0.0 90.1 jit_solution(8176137218137761484)
XLA Ops:
  0.6 0.7 convert_element_type.50
  1.4 0.8 copy.16
  2.2 0.9 %concatenate.3.refs_0_ = bf16[16,3712]{1,0:T(8,128)(2,1)S(1)} concatenate(bf16[16,1792]{1,0:T(8,128)(2,1)} %param.9, bf16[16,1792]{1,0:T(8,128)(2,1)} %param.10, bf16[16,8]{1,0:T(8,128)(2,1)S(1)} %copy.15, bf16[16,8]{1,0:T(8,128)(2,1)S(1)} %copy.16, bf16[16,112]{1,0:T(8,128)(2,1)S(1)} %broadcast_in_dim.2), dimensions={1} | concatenate | bytes 237568 | tf_op jit(solution)/shard_map/concatenate | solution.py:247
  3.1 3.0 %collective-permute-start = (bf16[16,3712]{1,0:T(8,128)(2,1)S(1)}, bf16[16,3712]{1,0:T(8,128)(2,1)S(1)}, u32[]{:S(2)}, u32[]{:S(2)}) collective-permute-start(bf16[16,3712]{1,0:T(8,128)(2,1)S(1)} %concatenate.3.refs_0_), channel_id=1, source_target_pairs={{0,4},{4,0},{8,12},{12,8},{1,5},{5,1},{9,13},{13,9},{2,6},{6,2},{1... | collective-permute-start | bytes 356360 | tf_op jit(solution)/shard_map/ppermute | solution.py:127
  6.1 2.6 %collective-permute-start.1 = (bf16[16,3712]{1,0:T(8,128)(2,1)S(1)}, bf16[16,3712]{1,0:T(8,128)(2,1)S(1)}, u32[]{:S(2)}, u32[]{:S(2)}) collective-permute-start(bf16[16,3712]{1,0:T(8,128)(2,1)S(1)} %concatenate.3.refs_0_), channel_id=1, source_target_pairs={{0,8},{4,12},{8,0},{12,4},{1,9},{5,13},{9,1},{13,5},{2,10},{6,14},... | collective-permute-start | bytes 356360 | tf_op jit(solution)/shard_map/ppermute | solution.py:127
  8.7 1.7 %collective-permute-start.3 = (bf16[16,3712]{1,0:T(8,128)(2,1)S(1)}, bf16[16,3712]{1,0:T(8,128)(2,1)S(1)}, u32[]{:S(2)}, u32[]{:S(2)}) collective-permute-start(bf16[16,3712]{1,0:T(8,128)(2,1)S(1)} %concatenate.3.refs_0_), channel_id=1, source_target_pairs={{0,2},{1,3},{2,0},{3,1},{4,6},{5,7},{6,4},{7,5},{8,10},{9,11},{10,... | collective-permute-start | bytes 356360 | tf_op jit(solution)/shard_map/ppermute | solution.py:127
  10.4 0.2 collective-permute-done.refs_1_
  10.6 1.7 %collective-permute-start.4 = (bf16[16,3712]{1,0:T(8,128)(2,1)S(1)}, bf16[16,3712]{1,0:T(8,128)(2,1)S(1)}, u32[]{:S(2)}, u32[]{:S(2)}) collective-permute-start(bf16[16,3712]{1,0:T(8,128)(2,1)S(1)} %collective-permute-done.refs_1_), channel_id=1, source_target_pairs={{0,2},{1,3},{2,0},{3,1},{4,6},{5,7},{6,4},{7,5},{8,10},{9,11},{10,... | collective-permute-start | bytes 356360 | tf_op jit(solution)/shard_map/ppermute | solution.py:127
  12.3 5.8 %collective-permute-done.1.refs_2_ = bf16[16,3712]{1,0:T(8,128)(2,1)S(1)} collective-permute-done((bf16[16,3712]{1,0:T(8,128)(2,1)S(1)}, bf16[16,3712]{1,0:T(8,128)(2,1)S(1)}, u32[]{:S(2)}, u32[]{:S(2)}) %collective-permute-start.1) | collective-permute-done | bytes 118816 | tf_op jit(solution)/shard_map/ppermute | solution.py:127
  18.1 1.5 %collective-permute-start.5 = (bf16[16,3712]{1,0:T(8,128)(2,1)S(1)}, bf16[16,3712]{1,0:T(8,128)(2,1)S(1)}, u32[]{:S(2)}, u32[]{:S(2)}) collective-permute-start(bf16[16,3712]{1,0:T(8,128)(2,1)S(1)} %collective-permute-done.1.refs_2_), channel_id=1, source_target_pairs={{0,2},{1,3},{2,0},{3,1},{4,6},{5,7},{6,4},{7,5},{8,10},{9,11},{10,... | collective-permute-start | bytes 356360 | tf_op jit(solution)/shard_map/ppermute | solution.py:127
  19.6 0.5 collective-permute-start.6
  20.2 0.5 collective-permute-start.8
  20.7 0.7 reshape.16
  21.4 1.0 %multiply_reduce_fusion.1 = f32[16]{0:T(128)S(1)} fusion(bf16[16,1792]{1,0:T(8,128)(2,1)} %param.11, bf16[16,1792]{1,0:T(8,128)(2,1)} %param.10), kind=kLoop, calls=%fused_computation.11 | loop fusion | flops 114672 | bytes 114752 | tf_op jit(solution)/shard_map/reduce_sum | solution.py:255
  22.5 0.5 collective-permute-done.5.refs_6_
  23.0 1.5 %collective-permute-done.6.refs_7_ = bf16[16,3712]{1,0:T(8,128)(2,1)S(1)} collective-permute-done((bf16[16,3712]{1,0:T(8,128)(2,1)S(1)}, bf16[16,3712]{1,0:T(8,128)(2,1)S(1)}, u32[]{:S(2)}, u32[]{:S(2)}) %collective-permute-start.6) | collective-permute-done | bytes 118816 | tf_op jit(solution)/shard_map/ppermute | solution.py:127
  24.5 0.5 collective-permute-start.13
  25.1 0.9 %subtract_multiply_fusion = f32[16]{0:T(128)S(1)} fusion(f32[16]{0:T(128)S(1)} %multiply_reduce_fusion.1, bf16[16,1792]{1,0:T(8,128)(2,1)} %param.9, bf16[1792,1]{0,1:T(2,128)(2,1)S(1)} %reshape.16), kind=kOutput, calls=%fused_computation.12 | convolution fusion | flops 57440 | bytes 61056 | tf_op jit(solution)/shard_map/dot_general | solution.py:253
  26.0 0.9 %multiply_reduce_fusion = f32[1792]{0:T(1024)S(1)} fusion(bf16[16,1792]{1,0:T(8,128)(2,1)} %param.9, f32[16]{0:T(128)S(1)} %subtract_multiply_fusion), kind=kLoop, calls=%fused_computation.10 | loop fusion | flops 84224 | bytes 64576 | tf_op jit(solution)/shard_map/reduce_sum | solution.py:257
  27.1 41.1 %experts.1 = (bf16[128,1920]{1,0:T(8,128)(2,1)S(1)}, bf16[128,1920]{1,0:T(8,128)(2,1)S(1)}) custom-call(bf16[16,3712]{1,0:T(8,128)(2,1)S(1)} %concatenate.3.refs_0_, bf16[16,3712]{1,0:T(8,128)(2,1)S(1)} %collective-permute-done.refs_1_, bf16[16,3712]{1,0:T(8,128)(2,1)S(1)} %collective-permute-done.1.refs_2_, ...), custom_call_target="tpu_custom_call" | custom-call | tf_op jit(solution)/shard_map/experts/pallas_call | solution.py:206
  68.3 0.5 collective-permute-start.15
  68.8 1.5 %collective-permute-done.15 = bf16[128,1920]{1,0:T(8,128)(2,1)S(1)} collective-permute-done((bf16[128,1920]{1,0:T(8,128)(2,1)S(1)}, bf16[128,1920]{1,0:T(8,128)(2,1)S(1)}, u32[]{:S(2)}, u32[]{:S(2)}) %collective-permute-start.15) | collective-permute-done | bytes 491552 | tf_op jit(solution)/shard_map/ppermute | solution.py:127
  70.4 1.3 %collective-permute-start.16 = (bf16[64,1920]{1,0:T(8,128)(2,1)S(1)}, bf16[64,1920]{1,0:T(8,128)(2,1)S(1)}, u32[]{:S(2)}, u32[]{:S(2)}) collective-permute-start(bf16[64,1920]{1,0:T(8,128)(2,1)S(1)} %slice.37), channel_id=1, source_target_pairs={{0,2},{1,3},{2,0},{3,1},{4,6},{5,7},{6,4},{7,5},{8,10},{9,11},{10,... | collective-permute-start | bytes 737288 | tf_op jit(solution)/shard_map/ppermute | solution.py:127
  71.8 7.0 %collective-permute-done.16 = bf16[64,1920]{1,0:T(8,128)(2,1)S(1)} collective-permute-done((bf16[64,1920]{1,0:T(8,128)(2,1)S(1)}, bf16[64,1920]{1,0:T(8,128)(2,1)S(1)}, u32[]{:S(2)}, u32[]{:S(2)}) %collective-permute-start.16) | collective-permute-done | bytes 245792 | tf_op jit(solution)/shard_map/ppermute | solution.py:127
  78.8 0.5 collective-permute-start.17
  79.3 2.6 %collective-permute-start.18 = (bf16[16,1920]{1,0:T(8,128)(2,1)S(1)}, bf16[16,1920]{1,0:T(8,128)(2,1)S(1)}, u32[]{:S(2)}, u32[]{:S(2)}) collective-permute-start(bf16[16,1920]{1,0:T(8,128)(2,1)S(1)} %get-tuple-element.15), channel_id=1, source_target_pairs={{0,8},{4,12},{8,0},{12,4},{1,9},{5,13},{9,1},{13,5},{2,10},{6,14},... | collective-permute-start | bytes 184328 | tf_op jit(solution)/shard_map/ppermute | solution.py:127
  81.9 1.4 %collective-permute-start.19 = (bf16[16,1920]{1,0:T(8,128)(2,1)S(1)}, bf16[16,1920]{1,0:T(8,128)(2,1)S(1)}, u32[]{:S(2)}, u32[]{:S(2)}) collective-permute-start(bf16[16,1920]{1,0:T(8,128)(2,1)S(1)} %get-tuple-element.14), channel_id=1, source_target_pairs={{0,12},{4,8},{8,4},{12,0},{1,13},{5,9},{9,5},{13,1},{2,14},{6,10},... | collective-permute-start | bytes 184328 | tf_op jit(solution)/shard_map/ppermute | solution.py:127
  83.4 3.1 %collective-permute-done.18 = bf16[16,1920]{1,0:T(8,128)(2,1)S(1)} collective-permute-done((bf16[16,1920]{1,0:T(8,128)(2,1)S(1)}, bf16[16,1920]{1,0:T(8,128)(2,1)S(1)}, u32[]{:S(2)}, u32[]{:S(2)}) %collective-permute-start.18) | collective-permute-done | bytes 61472 | tf_op jit(solution)/shard_map/ppermute | solution.py:127
  86.4 1.5 %collective-permute-done.19 = bf16[16,1920]{1,0:T(8,128)(2,1)S(1)} collective-permute-done((bf16[16,1920]{1,0:T(8,128)(2,1)S(1)}, bf16[16,1920]{1,0:T(8,128)(2,1)S(1)}, u32[]{:S(2)}, u32[]{:S(2)}) %collective-permute-start.19) | collective-permute-done | bytes 61472 | tf_op jit(solution)/shard_map/ppermute | solution.py:127
  88.0 0.7 fusion.4
  88.7 0.7 reshape.15
  89.4 0.7 copy.17
  (33 shorter events, 0.9 us)
Async XLA Ops:
  3.1 7.5 %collective-permute-start = (bf16[16,3712]{1,0:T(8,128)(2,1)S(1)}, bf16[16,3712]{1,0:T(8,128)(2,1)S(1)}, u32[]{:S(2)}, u32[]{:S(2)}) collective-permute-start(bf16[16,3712]{1,0:T(8,128)(2,1)S(1)} %concatenate.3.refs_0_), channel_id=1, source_target_pairs={{0,4},{4,0},{8,12},{12,8},{1,5},{5,1},{9,13},{13,9},{2,6},{6,2},{1... | collective-permute-start | bytes 356360 | tf_op jit(solution)/shard_map/ppermute | solution.py:127
  6.1 12.0 %collective-permute-start.1 = (bf16[16,3712]{1,0:T(8,128)(2,1)S(1)}, bf16[16,3712]{1,0:T(8,128)(2,1)S(1)}, u32[]{:S(2)}, u32[]{:S(2)}) collective-permute-start(bf16[16,3712]{1,0:T(8,128)(2,1)S(1)} %concatenate.3.refs_0_), channel_id=1, source_target_pairs={{0,8},{4,12},{8,0},{12,4},{1,9},{5,13},{9,1},{13,5},{2,10},{6,14},... | collective-permute-start | bytes 356360 | tf_op jit(solution)/shard_map/ppermute | solution.py:127
  8.7 10.9 %collective-permute-start.2 = (bf16[16,3712]{1,0:T(8,128)(2,1)S(1)}, bf16[16,3712]{1,0:T(8,128)(2,1)S(1)}, u32[]{:S(2)}, u32[]{:S(2)}) collective-permute-start(bf16[16,3712]{1,0:T(8,128)(2,1)S(1)} %concatenate.3.refs_0_), channel_id=1, source_target_pairs={{0,12},{4,8},{8,4},{12,0},{1,13},{5,9},{9,5},{13,1},{2,14},{6,10},... | collective-permute-start | bytes 356360 | tf_op jit(solution)/shard_map/ppermute | solution.py:127
  8.7 11.4 %collective-permute-start.3 = (bf16[16,3712]{1,0:T(8,128)(2,1)S(1)}, bf16[16,3712]{1,0:T(8,128)(2,1)S(1)}, u32[]{:S(2)}, u32[]{:S(2)}) collective-permute-start(bf16[16,3712]{1,0:T(8,128)(2,1)S(1)} %concatenate.3.refs_0_), channel_id=1, source_target_pairs={{0,2},{1,3},{2,0},{3,1},{4,6},{5,7},{6,4},{7,5},{8,10},{9,11},{10,... | collective-permute-start | bytes 356360 | tf_op jit(solution)/shard_map/ppermute | solution.py:127
  10.4 9.7 %collective-permute-start.7 = (bf16[16,3712]{1,0:T(8,128)(2,1)S(1)}, bf16[16,3712]{1,0:T(8,128)(2,1)S(1)}, u32[]{:S(2)}, u32[]{:S(2)}) collective-permute-start(bf16[16,3712]{1,0:T(8,128)(2,1)S(1)} %concatenate.3.refs_0_), channel_id=1, source_target_pairs={{0,1},{1,0},{2,3},{3,2},{4,5},{5,4},{6,7},{7,6},{8,9},{9,8},{10,11... | collective-permute-start | bytes 356360 | tf_op jit(solution)/shard_map/ppermute | solution.py:127
  10.6 11.7 %collective-permute-start.4 = (bf16[16,3712]{1,0:T(8,128)(2,1)S(1)}, bf16[16,3712]{1,0:T(8,128)(2,1)S(1)}, u32[]{:S(2)}, u32[]{:S(2)}) collective-permute-start(bf16[16,3712]{1,0:T(8,128)(2,1)S(1)} %collective-permute-done.refs_1_), channel_id=1, source_target_pairs={{0,2},{1,3},{2,0},{3,1},{4,6},{5,7},{6,4},{7,5},{8,10},{9,11},{10,... | collective-permute-start | bytes 356360 | tf_op jit(solution)/shard_map/ppermute | solution.py:127
  18.1 4.8 %collective-permute-start.5 = (bf16[16,3712]{1,0:T(8,128)(2,1)S(1)}, bf16[16,3712]{1,0:T(8,128)(2,1)S(1)}, u32[]{:S(2)}, u32[]{:S(2)}) collective-permute-start(bf16[16,3712]{1,0:T(8,128)(2,1)S(1)} %collective-permute-done.1.refs_2_), channel_id=1, source_target_pairs={{0,2},{1,3},{2,0},{3,1},{4,6},{5,7},{6,4},{7,5},{8,10},{9,11},{10,... | collective-permute-start | bytes 356360 | tf_op jit(solution)/shard_map/ppermute | solution.py:127
  19.6 4.8 %collective-permute-start.6 = (bf16[16,3712]{1,0:T(8,128)(2,1)S(1)}, bf16[16,3712]{1,0:T(8,128)(2,1)S(1)}, u32[]{:S(2)}, u32[]{:S(2)}) collective-permute-start(bf16[16,3712]{1,0:T(8,128)(2,1)S(1)} %collective-permute-done.2.refs_3_), channel_id=1, source_target_pairs={{0,2},{1,3},{2,0},{3,1},{4,6},{5,7},{6,4},{7,5},{8,10},{9,11},{10,... | collective-permute-start | bytes 356360 | tf_op jit(solution)/shard_map/ppermute | solution.py:127
  20.2 4.3 %collective-permute-start.10 = (bf16[16,3712]{1,0:T(8,128)(2,1)S(1)}, bf16[16,3712]{1,0:T(8,128)(2,1)S(1)}, u32[]{:S(2)}, u32[]{:S(2)}) collective-permute-start(bf16[16,3712]{1,0:T(8,128)(2,1)S(1)} %collective-permute-done.2.refs_3_), channel_id=1, source_target_pairs={{0,1},{1,0},{2,3},{3,2},{4,5},{5,4},{6,7},{7,6},{8,9},{9,8},{10,11... | collective-permute-start | bytes 356360 | tf_op jit(solution)/shard_map/ppermute | solution.py:127
  20.2 4.8 %collective-permute-start.8 = (bf16[16,3712]{1,0:T(8,128)(2,1)S(1)}, bf16[16,3712]{1,0:T(8,128)(2,1)S(1)}, u32[]{:S(2)}, u32[]{:S(2)}) collective-permute-start(bf16[16,3712]{1,0:T(8,128)(2,1)S(1)} %collective-permute-done.refs_1_), channel_id=1, source_target_pairs={{0,1},{1,0},{2,3},{3,2},{4,5},{5,4},{6,7},{7,6},{8,9},{9,8},{10,11... | collective-permute-start | bytes 356360 | tf_op jit(solution)/shard_map/ppermute | solution.py:127
  22.4 4.7 %collective-permute-start.9 = (bf16[16,3712]{1,0:T(8,128)(2,1)S(1)}, bf16[16,3712]{1,0:T(8,128)(2,1)S(1)}, u32[]{:S(2)}, u32[]{:S(2)}) collective-permute-start(bf16[16,3712]{1,0:T(8,128)(2,1)S(1)} %collective-permute-done.1.refs_2_), channel_id=1, source_target_pairs={{0,1},{1,0},{2,3},{3,2},{4,5},{5,4},{6,7},{7,6},{8,9},{9,8},{10,11... | collective-permute-start | bytes 356360 | tf_op jit(solution)/shard_map/ppermute | solution.py:127
  23.0 4.1 %collective-permute-start.11 = (bf16[16,3712]{1,0:T(8,128)(2,1)S(1)}, bf16[16,3712]{1,0:T(8,128)(2,1)S(1)}, u32[]{:S(2)}, u32[]{:S(2)}) collective-permute-start(bf16[16,3712]{1,0:T(8,128)(2,1)S(1)} %collective-permute-done.3.refs_4_), channel_id=1, source_target_pairs={{0,1},{1,0},{2,3},{3,2},{4,5},{5,4},{6,7},{7,6},{8,9},{9,8},{10,11... | collective-permute-start | bytes 356360 | tf_op jit(solution)/shard_map/ppermute | solution.py:127
  24.5 2.6 %collective-permute-start.12 = (bf16[16,3712]{1,0:T(8,128)(2,1)S(1)}, bf16[16,3712]{1,0:T(8,128)(2,1)S(1)}, u32[]{:S(2)}, u32[]{:S(2)}) collective-permute-start(bf16[16,3712]{1,0:T(8,128)(2,1)S(1)} %collective-permute-done.4.refs_5_), channel_id=1, source_target_pairs={{0,1},{1,0},{2,3},{3,2},{4,5},{5,4},{6,7},{7,6},{8,9},{9,8},{10,11... | collective-permute-start | bytes 356360 | tf_op jit(solution)/shard_map/ppermute | solution.py:127
  24.5 2.6 %collective-permute-start.13 = (bf16[16,3712]{1,0:T(8,128)(2,1)S(1)}, bf16[16,3712]{1,0:T(8,128)(2,1)S(1)}, u32[]{:S(2)}, u32[]{:S(2)}) collective-permute-start(bf16[16,3712]{1,0:T(8,128)(2,1)S(1)} %collective-permute-done.5.refs_6_), channel_id=1, source_target_pairs={{0,1},{1,0},{2,3},{3,2},{4,5},{5,4},{6,7},{7,6},{8,9},{9,8},{10,11... | collective-permute-start | bytes 356360 | tf_op jit(solution)/shard_map/ppermute | solution.py:127
  25.0 2.1 %collective-permute-start.14 = (bf16[16,3712]{1,0:T(8,128)(2,1)S(1)}, bf16[16,3712]{1,0:T(8,128)(2,1)S(1)}, u32[]{:S(2)}, u32[]{:S(2)}) collective-permute-start(bf16[16,3712]{1,0:T(8,128)(2,1)S(1)} %collective-permute-done.6.refs_7_), channel_id=1, source_target_pairs={{0,1},{1,0},{2,3},{3,2},{4,5},{5,4},{6,7},{7,6},{8,9},{9,8},{10,11... | collective-permute-start | bytes 356360 | tf_op jit(solution)/shard_map/ppermute | solution.py:127
  27.1 56.2 %copy-start = (bf16[1792]{0:T(1024)(128)(2,1)S(1)}, bf16[1792]{0:T(1024)(128)(2,1)}, u32[]{:S(2)}) copy-start(bf16[1792]{0:T(1024)(128)(2,1)} %param.14) | copy-start | bytes 10756
  68.3 2.0 %collective-permute-start.15 = (bf16[128,1920]{1,0:T(8,128)(2,1)S(1)}, bf16[128,1920]{1,0:T(8,128)(2,1)S(1)}, u32[]{:S(2)}, u32[]{:S(2)}) collective-permute-start(bf16[128,1920]{1,0:T(8,128)(2,1)S(1)} %get-tuple-element.6), channel_id=1, source_target_pairs={{0,1},{1,0},{2,3},{3,2},{4,5},{5,4},{6,7},{7,6},{8,9},{9,8},{10,11... | collective-permute-start | bytes 1474568 | tf_op jit(solution)/shard_map/ppermute | solution.py:127
  70.4 8.3 %collective-permute-start.16 = (bf16[64,1920]{1,0:T(8,128)(2,1)S(1)}, bf16[64,1920]{1,0:T(8,128)(2,1)S(1)}, u32[]{:S(2)}, u32[]{:S(2)}) collective-permute-start(bf16[64,1920]{1,0:T(8,128)(2,1)S(1)} %slice.37), channel_id=1, source_target_pairs={{0,2},{1,3},{2,0},{3,1},{4,6},{5,7},{6,4},{7,5},{8,10},{9,11},{10,... | collective-permute-start | bytes 737288 | tf_op jit(solution)/shard_map/ppermute | solution.py:127
  78.8 4.5 %collective-permute-start.17 = (bf16[16,1920]{1,0:T(8,128)(2,1)S(1)}, bf16[16,1920]{1,0:T(8,128)(2,1)S(1)}, u32[]{:S(2)}, u32[]{:S(2)}) collective-permute-start(bf16[16,1920]{1,0:T(8,128)(2,1)S(1)} %get-tuple-element.13), channel_id=1, source_target_pairs={{0,4},{4,0},{8,12},{12,8},{1,5},{5,1},{9,13},{13,9},{2,6},{6,2},{1... | collective-permute-start | bytes 184328 | tf_op jit(solution)/shard_map/ppermute | solution.py:127
  79.3 7.2 %collective-permute-start.18 = (bf16[16,1920]{1,0:T(8,128)(2,1)S(1)}, bf16[16,1920]{1,0:T(8,128)(2,1)S(1)}, u32[]{:S(2)}, u32[]{:S(2)}) collective-permute-start(bf16[16,1920]{1,0:T(8,128)(2,1)S(1)} %get-tuple-element.15), channel_id=1, source_target_pairs={{0,8},{4,12},{8,0},{12,4},{1,9},{5,13},{9,1},{13,5},{2,10},{6,14},... | collective-permute-start | bytes 184328 | tf_op jit(solution)/shard_map/ppermute | solution.py:127
  81.9 6.0 %collective-permute-start.19 = (bf16[16,1920]{1,0:T(8,128)(2,1)S(1)}, bf16[16,1920]{1,0:T(8,128)(2,1)S(1)}, u32[]{:S(2)}, u32[]{:S(2)}) collective-permute-start(bf16[16,1920]{1,0:T(8,128)(2,1)S(1)} %get-tuple-element.14), channel_id=1, source_target_pairs={{0,12},{4,8},{8,4},{12,0},{1,13},{5,9},{9,5},{13,1},{2,14},{6,10},... | collective-permute-start | bytes 184328 | tf_op jit(solution)/shard_map/ppermute | solution.py:127

commit v2 on v1

--- a/solution.py
+++ b/solution.py
@@ -127,74 +127,102 @@
     return lax.ppermute(value, axis, [(i, i ^ distance) for i in range(size)])
 
 
-def experts_kernel(features, rows, blocks, *refs):
+def experts_kernel(features, rows, blocks, group, *refs):
     token_refs, refs = refs[:blocks], refs[blocks:]
-    tail_ref, w_gate, w_up, w_down, keep_ref, send_ref, tokens, copied, spread, weighted, norms, grads, backs, hits, routes = refs
-    step, steps = pl.program_id(0), pl.num_programs(0)
+    tail_ref, w_gate, w_up, w_down, keep_ref, send_ref, tokens, copied, gates, ups, downs, loaded, spread, weighted, norms, grads, backs, hits, routes = refs
+    number = w_gate.shape[0]
     each = token_refs[0].shape[0]
     count = each * blocks
 
-    @pl.when(step == 0)
-    def _():
-        copies = [
-            pltpu.make_async_copy(ref, tokens.at[pl.ds(j * each, each)], copied.at[j])
-            for j, ref in enumerate(token_refs)
+    def loads(turn, k):
+        expert = turn * group + k
+        slot = lax.rem(turn, 2) * group + k
+        return [
+            pltpu.make_async_copy(source.at[expert], target.at[slot], loaded.at[slot, j])
+            for j, (source, target) in enumerate(((w_gate, gates), (w_up, ups), (w_down, downs)))
         ]
-        for copy in copies:
-            copy.start()
-        for copy in copies:
-            copy.wait()
-        codes = tokens[:, 2 * features :].astype(F32).T
-        named = codes[:TOPK]
-        weights = codes[TOPK : 2 * TOPK]
-        first = (lax.axis_index("expert") * steps).astype(F32)
-        hits[...] = named - first
-        local = named - first
-        earlier = (
-            lax.broadcasted_iota(jnp.int32, (count, count), 0)
-            < lax.broadcasted_iota(jnp.int32, (count, count), 1)
-        ).astype(BF16)
-        number = spread.shape[0] // rows
-        masks = [local == float(e) for e in range(number)]
-        member = jnp.concatenate(
-            [jnp.sum(m.astype(F32), axis=0, keepdims=True) for m in masks], axis=0
-        )
-        position = dot(member.astype(BF16), earlier)
-        slot = lax.broadcasted_iota(jnp.int32, (rows, count), 0).astype(F32)
-        for e in range(number):
-            weight = jnp.sum(jnp.where(masks[e], weights, 0.0), axis=0, keepdims=True)
-            chosen = (slot == position[e : e + 1]) & (member[e : e + 1] > 0.0)
-            spread[e * rows : (e + 1) * rows] = jnp.where(chosen, 1.0, 0.0).astype(BF16)
-            weighted[e * rows : (e + 1) * rows] = jnp.where(chosen, weight, 0.0).astype(BF16)
-        norms[...] = dot(spread[...], tokens[:, :features]).astype(BF16)
-        grads[...] = dot(spread[...], tokens[:, features : 2 * features]).astype(BF16)
-        routes[...] = jnp.zeros_like(routes)
-
-    here = pl.ds(pl.multiple_of(step * rows, rows), rows)
-    x, dy = norms[here], grads[here]
-    gate_pre = dot(x, w_gate[0])
-    up_pre = dot(x, w_up[0])
-    hidden_grad = dot(dy, w_down[0], NT)
-    logistic = jax.nn.sigmoid(gate_pre)
-    swish = gate_pre * logistic
-    gate_diff = (hidden_grad * up_pre * logistic * (1.0 + gate_pre * (1.0 - logistic))).astype(BF16)
-    up_diff = (hidden_grad * swish).astype(BF16)
-    backs[here] = (dot(gate_diff, w_gate[0], NT) + dot(up_diff, w_up[0], NT)).astype(BF16)
-    score = jnp.sum(swish * up_pre * hidden_grad, axis=1, keepdims=True)
-    by_token = jnp.sum(spread[here].astype(F32) * score, axis=0, keepdims=True)
-    routes[...] += jnp.where(hits[...] == step.astype(F32), by_token, 0.0)
-
-    @pl.when(step == steps - 1)
-    def _():
-        half = count // 2
-        result = dot(weighted[...], backs[...], TN).astype(BF16)
-        scores = jnp.concatenate([routes[...], jnp.zeros((LANES - TOPK, count), F32)], axis=0).T
-        tail = jnp.concatenate([tail_ref[...]] * blocks, axis=0)
-        last = (scores + tail).astype(BF16)
-        keep_ref[:, :features] = result[:half]
-        send_ref[:, :features] = result[half:]
-        keep_ref[:, features:] = last[:half]
-        send_ref[:, features:] = last[half:]
+
+    copies = [
+        pltpu.make_async_copy(ref, tokens.at[pl.ds(j * each, each)], copied.at[j])
+        for j, ref in enumerate(token_refs)
+    ]
+    for copy in copies:
+        copy.start()
+    for turn in range(2):
+        for k in range(group):
+            for copy in loads(turn, k):
+                copy.start()
+    for copy in copies:
+        copy.wait()
+    codes = tokens[:, 2 * features :].astype(F32).T
+    weights = codes[TOPK : 2 * TOPK]
+    local = codes[:TOPK] - (lax.axis_index("expert") * number).astype(F32)
+    hits[...] = local
+    earlier = (
+        lax.broadcasted_iota(jnp.int32, (count, count), 0)
+        < lax.broadcasted_iota(jnp.int32, (count, count), 1)
+    ).astype(BF16)
+    masks = [local == float(e) for e in range(number)]
+    member = jnp.concatenate(
+        [jnp.sum(m.astype(F32), axis=0, keepdims=True) for m in masks], axis=0
+    )
+    position = dot(member.astype(BF16), earlier)
+    slot = lax.broadcasted_iota(jnp.int32, (rows, count), 0).astype(F32)
+    for e in range(number):
+        weight = jnp.sum(jnp.where(masks[e], weights, 0.0), axis=0, keepdims=True)
+        chosen = (slot == position[e : e + 1]) & (member[e : e + 1] > 0.0)
+        spread[e * rows : (e + 1) * rows] = jnp.where(chosen, 1.0, 0.0).astype(BF16)
+        weighted[e * rows : (e + 1) * rows] = jnp.where(chosen, weight, 0.0).astype(BF16)
+    norms[...] = dot(spread[...], tokens[:, :features]).astype(BF16)
+    grads[...] = dot(spread[...], tokens[:, features : 2 * features]).astype(BF16)
+    routes[...] = jnp.zeros_like(routes)
+
+    def run(turn, _):
+        base = lax.rem(turn, 2) * group
+        heres = [
+            pl.ds(pl.multiple_of((turn * group + k) * rows, rows), rows) for k in range(group)
+        ]
+        for k in range(group):
+            for copy in loads(turn, k):
+                copy.wait()
+        pre = []
+        for k in range(group):
+            x, dy = norms[heres[k]], grads[heres[k]]
+            pre.append((dot(x, gates[base + k]), dot(x, ups[base + k]), dot(dy, downs[base + k], NT)))
+        for k in range(group):
+            gate_pre, up_pre, hidden_grad = pre[k]
+            logistic = jax.nn.sigmoid(gate_pre)
+            swish = gate_pre * logistic
+            gate_diff = (
+                hidden_grad * up_pre * logistic * (1.0 + gate_pre * (1.0 - logistic))
+            ).astype(BF16)
+            up_diff = (hidden_grad * swish).astype(BF16)
+            first_part = dot(gate_diff, gates[base + k], NT)
+            second_part = dot(ups[base + k], up_diff, NT).T
+            backs[heres[k]] = (first_part + second_part).astype(BF16)
+            score = jnp.sum(swish * up_pre * hidden_grad, axis=1, keepdims=True)
+            by_token = jnp.sum(spread[heres[k]].astype(F32) * score, axis=0, keepdims=True)
+            here = (turn * group + k).astype(F32)
+            routes[...] += jnp.where(hits[...] == here, by_token, 0.0)
+
+        @pl.when(turn + 2 < number // group)
+        def _():
+            for k in range(group):
+                for copy in loads(turn + 2, k):
+                    copy.start()
+
+        return 0
+
+    lax.fori_loop(0, number // group, run, 0)
+    half = count // 2
+    result = dot(weighted[...], backs[...], TN).astype(BF16)
+    scores = jnp.concatenate([routes[...], jnp.zeros((LANES - TOPK, count), F32)], axis=0).T
+    tail = jnp.concatenate([tail_ref[...]] * blocks, axis=0)
+    last = (scores + tail).astype(BF16)
+    keep_ref[:, :features] = result[:half]
+    send_ref[:, :features] = result[half:]
+    keep_ref[:, features:] = last[:half]
+    send_ref[:, features:] = last[half:]
 
 
 def run_experts(token_blocks, tail, w_gate, w_up, w_down, sources):
@@ -203,21 +231,21 @@
     count = blocks * token_blocks[0].shape[0]
     rows = sources * CAP
     width = features + LANES
+    group = 2
+    away = pl.BlockSpec(memory_space=pl.ANY)
+    near = pl.BlockSpec(memory_space=pltpu.VMEM)
     return pl.pallas_call(
-        functools.partial(experts_kernel, features, rows, blocks),
-        grid=(local,),
-        in_specs=[pl.BlockSpec(memory_space=pl.ANY)] * blocks
-        + [
-            pl.BlockSpec(tail.shape, lambda i: (0, 0)),
-            pl.BlockSpec((1, features, hidden), lambda i: (i, 0, 0)),
-            pl.BlockSpec((1, features, hidden), lambda i: (i, 0, 0)),
-            pl.BlockSpec((1, hidden, features), lambda i: (i, 0, 0)),
-        ],
-        out_specs=[pl.BlockSpec((count // 2, width), lambda i: (0, 0))] * 2,
+        functools.partial(experts_kernel, features, rows, blocks, group),
+        in_specs=[away] * blocks + [near, away, away, away],
+        out_specs=[near] * 2,
         out_shape=[jax.ShapeDtypeStruct((count // 2, width), BF16)] * 2,
         scratch_shapes=[
             pltpu.VMEM((count, 2 * features + LANES), BF16),
             pltpu.SemaphoreType.DMA((blocks,)),
+            pltpu.VMEM((2 * group, features, hidden), BF16),
+            pltpu.VMEM((2 * group, features, hidden), BF16),
+            pltpu.VMEM((2 * group, hidden, features), BF16),
+            pltpu.SemaphoreType.DMA((2 * group, 3)),
             pltpu.VMEM((local * rows, count), BF16),
             pltpu.VMEM((local * rows, count), BF16),
             pltpu.VMEM((local * rows, features), BF16),
@@ -226,7 +254,7 @@
             pltpu.VMEM((TOPK, count), F32),
             pltpu.VMEM((TOPK, count), F32),
         ],
-        compiler_params=pltpu.CompilerParams(vmem_limit_bytes=48 << 20),
+        compiler_params=pltpu.CompilerParams(vmem_limit_bytes=60 << 20),
         name="experts",
     )(*token_blocks, tail, w_gate, w_up, w_down)
 

time: 90.6 us -> 88.3 us (0.975)
  Pallas kernels: 41.1 us -> 35.6 us
  local copies, waits for them, and re-layouts: 4.08 us -> 5.97 us
  other arithmetic: 3.51 us -> 4.54 us
    pallas_call x1, Pallas kernels: 41.1 us -> 35.6 us  [run_experts(): pl.pallas_call(functools.partial(experts_kernel, features, rows, blocks,...]
    unnamed x5 -> x37, local copies, waits for them, and re-layouts: 2.12 us -> 3.41 us
    convert_element_type x1, other arithmetic: 0.12 us -> 1.14 us  [square_device(): total = (kept.astype(F32) + swap(sent, 'dp', 1).astype(F32)).astype(BF16)]
  transfers between devices with their start and end apart: 20 -> 20, of which waited for: 9 -> 9; matrix products, arithmetic and copies ran while one was open for 4% -> 5% of each run, Pallas kernels for 0% -> 0%
where the time goes in v2:
time: 88.3 us; the launch traced here: 87.8 us
  Pallas kernels  35.6 us (40%)
  waiting for transfers between devices  21.2 us (24%)
  starting transfers between devices  18.6 us (21%)
  local copies, waits for them, and re-layouts  5.97 us (7%)
  other arithmetic  4.54 us (5%)
  matrix products  0.94 us (1%)
    pallas_call x1, Pallas kernels, run_experts(): pl.pallas_call(functools.partial(experts_kernel, features, rows, blocks,...  35.6 us
    ppermute x20, waiting for transfers between devices, swap(): return lax.ppermute(value, axis, [(i, i ^ distance) for i in range(size)])  21.2 us
    ppermute x20, starting transfers between devices, swap(): return lax.ppermute(value, axis, [(i, i ^ distance) for i in range(size)])  18.6 us
    unnamed x37, local copies, waits for them, and re-layouts  3.41 us
  transfers between devices with their start and end apart: 20, of which 9 were waited for; matrix products, arithmetic and copies ran while one was open for 5% of the time, Pallas kernels for 0%

profile of v2, /device:TPU:0, one launch (start us, length us, event | category | flops | bytes accessed | tf_op | source)
XLA Modules:
  0.0 87.8 jit_solution(3444653323183011971)
XLA Ops:
  0.6 0.7 convert_element_type.50
  1.4 0.8 copy.16
  2.2 0.9 %concatenate.3.refs_0_ = bf16[16,3712]{1,0:T(8,128)(2,1)S(1)} concatenate(bf16[16,1792]{1,0:T(8,128)(2,1)} %param.9, bf16[16,1792]{1,0:T(8,128)(2,1)} %param.10, bf16[16,8]{1,0:T(8,128)(2,1)S(1)} %copy.15, bf16[16,8]{1,0:T(8,128)(2,1)S(1)} %copy.16, bf16[16,112]{1,0:T(8,128)(2,1)S(1)} %broadcast_in_dim.2), dimensions={1} | concatenate | bytes 237568 | tf_op jit(solution)/shard_map/concatenate | solution.py:275
  3.1 3.1 %collective-permute-start = (bf16[16,3712]{1,0:T(8,128)(2,1)S(1)}, bf16[16,3712]{1,0:T(8,128)(2,1)S(1)}, u32[]{:S(2)}, u32[]{:S(2)}) collective-permute-start(bf16[16,3712]{1,0:T(8,128)(2,1)S(1)} %concatenate.3.refs_0_), channel_id=1, source_target_pairs={{0,4},{4,0},{8,12},{12,8},{1,5},{5,1},{9,13},{13,9},{2,6},{6,2},{1... | collective-permute-start | bytes 356360 | tf_op jit(solution)/shard_map/ppermute | solution.py:127
  6.2 2.6 %collective-permute-start.1 = (bf16[16,3712]{1,0:T(8,128)(2,1)S(1)}, bf16[16,3712]{1,0:T(8,128)(2,1)S(1)}, u32[]{:S(2)}, u32[]{:S(2)}) collective-permute-start(bf16[16,3712]{1,0:T(8,128)(2,1)S(1)} %concatenate.3.refs_0_), channel_id=1, source_target_pairs={{0,8},{4,12},{8,0},{12,4},{1,9},{5,13},{9,1},{13,5},{2,10},{6,14},... | collective-permute-start | bytes 356360 | tf_op jit(solution)/shard_map/ppermute | solution.py:127
  8.8 1.7 %collective-permute-start.3 = (bf16[16,3712]{1,0:T(8,128)(2,1)S(1)}, bf16[16,3712]{1,0:T(8,128)(2,1)S(1)}, u32[]{:S(2)}, u32[]{:S(2)}) collective-permute-start(bf16[16,3712]{1,0:T(8,128)(2,1)S(1)} %concatenate.3.refs_0_), channel_id=1, source_target_pairs={{0,2},{1,3},{2,0},{3,1},{4,6},{5,7},{6,4},{7,5},{8,10},{9,11},{10,... | collective-permute-start | bytes 356360 | tf_op jit(solution)/shard_map/ppermute | solution.py:127
  10.7 1.7 %collective-permute-start.4 = (bf16[16,3712]{1,0:T(8,128)(2,1)S(1)}, bf16[16,3712]{1,0:T(8,128)(2,1)S(1)}, u32[]{:S(2)}, u32[]{:S(2)}) collective-permute-start(bf16[16,3712]{1,0:T(8,128)(2,1)S(1)} %collective-permute-done.refs_1_), channel_id=1, source_target_pairs={{0,2},{1,3},{2,0},{3,1},{4,6},{5,7},{6,4},{7,5},{8,10},{9,11},{10,... | collective-permute-start | bytes 356360 | tf_op jit(solution)/shard_map/ppermute | solution.py:127
  12.4 5.8 %collective-permute-done.1.refs_2_ = bf16[16,3712]{1,0:T(8,128)(2,1)S(1)} collective-permute-done((bf16[16,3712]{1,0:T(8,128)(2,1)S(1)}, bf16[16,3712]{1,0:T(8,128)(2,1)S(1)}, u32[]{:S(2)}, u32[]{:S(2)}) %collective-permute-start.1) | collective-permute-done | bytes 118816 | tf_op jit(solution)/shard_map/ppermute | solution.py:127
  18.2 1.5 %collective-permute-start.5 = (bf16[16,3712]{1,0:T(8,128)(2,1)S(1)}, bf16[16,3712]{1,0:T(8,128)(2,1)S(1)}, u32[]{:S(2)}, u32[]{:S(2)}) collective-permute-start(bf16[16,3712]{1,0:T(8,128)(2,1)S(1)} %collective-permute-done.1.refs_2_), channel_id=1, source_target_pairs={{0,2},{1,3},{2,0},{3,1},{4,6},{5,7},{6,4},{7,5},{8,10},{9,11},{10,... | collective-permute-start | bytes 356360 | tf_op jit(solution)/shard_map/ppermute | solution.py:127
  19.7 0.5 collective-permute-start.6
  20.3 0.5 collective-permute-start.8
  20.7 0.7 reshape.16
  21.4 1.0 %multiply_reduce_fusion.1 = f32[16]{0:T(128)S(1)} fusion(bf16[16,1792]{1,0:T(8,128)(2,1)} %param.11, bf16[16,1792]{1,0:T(8,128)(2,1)} %param.10), kind=kLoop, calls=%fused_computation.11 | loop fusion | flops 114672 | bytes 114752 | tf_op jit(solution)/shard_map/reduce_sum | solution.py:283
  23.0 1.5 %collective-permute-done.6.refs_7_ = bf16[16,3712]{1,0:T(8,128)(2,1)S(1)} collective-permute-done((bf16[16,3712]{1,0:T(8,128)(2,1)S(1)}, bf16[16,3712]{1,0:T(8,128)(2,1)S(1)}, u32[]{:S(2)}, u32[]{:S(2)}) %collective-permute-start.6) | collective-permute-done | bytes 118816 | tf_op jit(solution)/shard_map/ppermute | solution.py:127
  24.5 0.5 collective-permute-start.13
  25.1 0.9 %subtract_multiply_fusion = f32[16]{0:T(128)S(1)} fusion(f32[16]{0:T(128)S(1)} %multiply_reduce_fusion.1, bf16[16,1792]{1,0:T(8,128)(2,1)} %param.9, bf16[1792,1]{0,1:T(2,128)(2,1)S(1)} %reshape.16), kind=kOutput, calls=%fused_computation.12 | convolution fusion | flops 57440 | bytes 61056 | tf_op jit(solution)/shard_map/dot_general | solution.py:281
  26.1 0.9 %multiply_reduce_fusion = f32[1792]{0:T(1024)S(1)} fusion(bf16[16,1792]{1,0:T(8,128)(2,1)} %param.9, f32[16]{0:T(128)S(1)} %subtract_multiply_fusion), kind=kLoop, calls=%fused_computation.10 | loop fusion | flops 84224 | bytes 64576 | tf_op jit(solution)/shard_map/reduce_sum | solution.py:285
  27.1 0.7 pad.4.refs_16_
  28.6 0.6 copy-done.15
  29.2 35.6 %experts.1 = (bf16[128,1920]{1,0:T(8,128)(2,1)}, bf16[128,1920]{1,0:T(8,128)(2,1)}) custom-call(bf16[16,3712]{1,0:T(8,128)(2,1)} %copy-done, bf16[16,3712]{1,0:T(8,128)(2,1)} %copy-done.1, bf16[16,3712]{1,0:T(8,128)(2,1)} %copy-done.2, bf16[16,3712]{1,0:T(8,128)(2,1)} %copy-done.3, bf16[16,3712]{1,0:T(8,128)(2,1)} %copy-done.4, bf16[16,3712]{1,0:T(8,128)(2,1)} %copy-done.6, ...), custom_call_target="tpu_custom_call" | custom-call | tf_op jit(solution)/shard_map/experts/pallas_call | solution.py:237
  64.8 0.5 collective-permute-start.15
  65.3 1.7 %collective-permute-done.15 = bf16[128,1920]{1,0:T(8,128)(2,1)S(1)} collective-permute-done((bf16[128,1920]{1,0:T(8,128)(2,1)}, bf16[128,1920]{1,0:T(8,128)(2,1)S(1)}, u32[]{:S(2)}, u32[]{:S(2)}) %collective-permute-start.15) | collective-permute-done | bytes 491552 | tf_op jit(solution)/shard_map/ppermute | solution.py:127
  67.0 1.1 %add_convert_fusion = bf16[128,1920]{1,0:T(8,128)(2,1)S(1)} fusion(bf16[128,1920]{1,0:T(8,128)(2,1)S(1)} %collective-permute-done.15, bf16[128,1920]{1,0:T(8,128)(2,1)} %get-tuple-element.5), kind=kLoop, calls=%fused_computation.5 | loop fusion | flops 983040 | bytes 1474560 | tf_op jit(solution)/shard_map/convert_element_type | solution.py:290
  68.2 1.3 %collective-permute-start.16 = (bf16[64,1920]{1,0:T(8,128)(2,1)S(1)}, bf16[64,1920]{1,0:T(8,128)(2,1)S(1)}, u32[]{:S(2)}, u32[]{:S(2)}) collective-permute-start(bf16[64,1920]{1,0:T(8,128)(2,1)S(1)} %slice.37), channel_id=1, source_target_pairs={{0,2},{1,3},{2,0},{3,1},{4,6},{5,7},{6,4},{7,5},{8,10},{9,11},{10,... | collective-permute-start | bytes 737288 | tf_op jit(solution)/shard_map/ppermute | solution.py:127
  69.5 6.9 %collective-permute-done.16 = bf16[64,1920]{1,0:T(8,128)(2,1)S(1)} collective-permute-done((bf16[64,1920]{1,0:T(8,128)(2,1)S(1)}, bf16[64,1920]{1,0:T(8,128)(2,1)S(1)}, u32[]{:S(2)}, u32[]{:S(2)}) %collective-permute-start.16) | collective-permute-done | bytes 245792 | tf_op jit(solution)/shard_map/ppermute | solution.py:127
  77.1 2.6 %collective-permute-start.18 = (bf16[16,1920]{1,0:T(8,128)(2,1)S(1)}, bf16[16,1920]{1,0:T(8,128)(2,1)S(1)}, u32[]{:S(2)}, u32[]{:S(2)}) collective-permute-start(bf16[16,1920]{1,0:T(8,128)(2,1)S(1)} %get-tuple-element.15), channel_id=1, source_target_pairs={{0,8},{4,12},{8,0},{12,4},{1,9},{5,13},{9,1},{13,5},{2,10},{6,14},... | collective-permute-start | bytes 184328 | tf_op jit(solution)/shard_map/ppermute | solution.py:127
  79.6 1.4 %collective-permute-start.19 = (bf16[16,1920]{1,0:T(8,128)(2,1)S(1)}, bf16[16,1920]{1,0:T(8,128)(2,1)S(1)}, u32[]{:S(2)}, u32[]{:S(2)}) collective-permute-start(bf16[16,1920]{1,0:T(8,128)(2,1)S(1)} %get-tuple-element.14), channel_id=1, source_target_pairs={{0,12},{4,8},{8,4},{12,0},{1,13},{5,9},{9,5},{13,1},{2,14},{6,10},... | collective-permute-start | bytes 184328 | tf_op jit(solution)/shard_map/ppermute | solution.py:127
  81.1 3.1 %collective-permute-done.18 = bf16[16,1920]{1,0:T(8,128)(2,1)S(1)} collective-permute-done((bf16[16,1920]{1,0:T(8,128)(2,1)S(1)}, bf16[16,1920]{1,0:T(8,128)(2,1)S(1)}, u32[]{:S(2)}, u32[]{:S(2)}) %collective-permute-start.18) | collective-permute-done | bytes 61472 | tf_op jit(solution)/shard_map/ppermute | solution.py:127
  84.2 1.5 %collective-permute-done.19 = bf16[16,1920]{1,0:T(8,128)(2,1)S(1)} collective-permute-done((bf16[16,1920]{1,0:T(8,128)(2,1)S(1)}, bf16[16,1920]{1,0:T(8,128)(2,1)S(1)}, u32[]{:S(2)}, u32[]{:S(2)}) %collective-permute-start.19) | collective-permute-done | bytes 61472 | tf_op jit(solution)/shard_map/ppermute | solution.py:127
  85.8 0.7 fusion.4
  86.5 0.7 reshape.15
  87.2 0.7 copy.17
  (65 shorter events, 2.5 us)
Async XLA Ops:
  3.1 24.7 %copy-start = (bf16[16,3712]{1,0:T(8,128)(2,1)}, bf16[16,3712]{1,0:T(8,128)(2,1)S(1)}, u32[]{:S(2)}) copy-start(bf16[16,3712]{1,0:T(8,128)(2,1)S(1)} %concatenate.3.refs_0_) | copy-start | bytes 356356
  3.1 7.6 %collective-permute-start = (bf16[16,3712]{1,0:T(8,128)(2,1)S(1)}, bf16[16,3712]{1,0:T(8,128)(2,1)S(1)}, u32[]{:S(2)}, u32[]{:S(2)}) collective-permute-start(bf16[16,3712]{1,0:T(8,128)(2,1)S(1)} %concatenate.3.refs_0_), channel_id=1, source_target_pairs={{0,4},{4,0},{8,12},{12,8},{1,5},{5,1},{9,13},{13,9},{2,6},{6,2},{1... | collective-permute-start | bytes 356360 | tf_op jit(solution)/shard_map/ppermute | solution.py:127
  6.2 12.0 %collective-permute-start.1 = (bf16[16,3712]{1,0:T(8,128)(2,1)S(1)}, bf16[16,3712]{1,0:T(8,128)(2,1)S(1)}, u32[]{:S(2)}, u32[]{:S(2)}) collective-permute-start(bf16[16,3712]{1,0:T(8,128)(2,1)S(1)} %concatenate.3.refs_0_), channel_id=1, source_target_pairs={{0,8},{4,12},{8,0},{12,4},{1,9},{5,13},{9,1},{13,5},{2,10},{6,14},... | collective-permute-start | bytes 356360 | tf_op jit(solution)/shard_map/ppermute | solution.py:127
  8.8 10.9 %collective-permute-start.2 = (bf16[16,3712]{1,0:T(8,128)(2,1)S(1)}, bf16[16,3712]{1,0:T(8,128)(2,1)S(1)}, u32[]{:S(2)}, u32[]{:S(2)}) collective-permute-start(bf16[16,3712]{1,0:T(8,128)(2,1)S(1)} %concatenate.3.refs_0_), channel_id=1, source_target_pairs={{0,12},{4,8},{8,4},{12,0},{1,13},{5,9},{9,5},{13,1},{2,14},{6,10},... | collective-permute-start | bytes 356360 | tf_op jit(solution)/shard_map/ppermute | solution.py:127
  8.8 11.4 %collective-permute-start.3 = (bf16[16,3712]{1,0:T(8,128)(2,1)S(1)}, bf16[16,3712]{1,0:T(8,128)(2,1)S(1)}, u32[]{:S(2)}, u32[]{:S(2)}) collective-permute-start(bf16[16,3712]{1,0:T(8,128)(2,1)S(1)} %concatenate.3.refs_0_), channel_id=1, source_target_pairs={{0,2},{1,3},{2,0},{3,1},{4,6},{5,7},{6,4},{7,5},{8,10},{9,11},{10,... | collective-permute-start | bytes 356360 | tf_op jit(solution)/shard_map/ppermute | solution.py:127
  10.5 9.8 %collective-permute-start.7 = (bf16[16,3712]{1,0:T(8,128)(2,1)S(1)}, bf16[16,3712]{1,0:T(8,128)(2,1)S(1)}, u32[]{:S(2)}, u32[]{:S(2)}) collective-permute-start(bf16[16,3712]{1,0:T(8,128)(2,1)S(1)} %concatenate.3.refs_0_), channel_id=1, source_target_pairs={{0,1},{1,0},{2,3},{3,2},{4,5},{5,4},{6,7},{7,6},{8,9},{9,8},{10,11... | collective-permute-start | bytes 356360 | tf_op jit(solution)/shard_map/ppermute | solution.py:127
  10.7 17.2 %copy-start.1 = (bf16[16,3712]{1,0:T(8,128)(2,1)}, bf16[16,3712]{1,0:T(8,128)(2,1)S(1)}, u32[]{:S(2)}) copy-start(bf16[16,3712]{1,0:T(8,128)(2,1)S(1)} %collective-permute-done.refs_1_) | copy-start | bytes 356356
  10.7 11.7 %collective-permute-start.4 = (bf16[16,3712]{1,0:T(8,128)(2,1)S(1)}, bf16[16,3712]{1,0:T(8,128)(2,1)S(1)}, u32[]{:S(2)}, u32[]{:S(2)}) collective-permute-start(bf16[16,3712]{1,0:T(8,128)(2,1)S(1)} %collective-permute-done.refs_1_), channel_id=1, source_target_pairs={{0,2},{1,3},{2,0},{3,1},{4,6},{5,7},{6,4},{7,5},{8,10},{9,11},{10,... | collective-permute-start | bytes 356360 | tf_op jit(solution)/shard_map/ppermute | solution.py:127
  18.2 9.7 %copy-start.2 = (bf16[16,3712]{1,0:T(8,128)(2,1)}, bf16[16,3712]{1,0:T(8,128)(2,1)S(1)}, u32[]{:S(2)}) copy-start(bf16[16,3712]{1,0:T(8,128)(2,1)S(1)} %collective-permute-done.1.refs_2_) | copy-start | bytes 356356
  18.2 4.8 %collective-permute-start.5 = (bf16[16,3712]{1,0:T(8,128)(2,1)S(1)}, bf16[16,3712]{1,0:T(8,128)(2,1)S(1)}, u32[]{:S(2)}, u32[]{:S(2)}) collective-permute-start(bf16[16,3712]{1,0:T(8,128)(2,1)S(1)} %collective-permute-done.1.refs_2_), channel_id=1, source_target_pairs={{0,2},{1,3},{2,0},{3,1},{4,6},{5,7},{6,4},{7,5},{8,10},{9,11},{10,... | collective-permute-start | bytes 356360 | tf_op jit(solution)/shard_map/ppermute | solution.py:127
  19.7 8.2 %copy-start.3 = (bf16[16,3712]{1,0:T(8,128)(2,1)}, bf16[16,3712]{1,0:T(8,128)(2,1)S(1)}, u32[]{:S(2)}) copy-start(bf16[16,3712]{1,0:T(8,128)(2,1)S(1)} %collective-permute-done.2.refs_3_) | copy-start | bytes 356356
  19.7 4.8 %collective-permute-start.6 = (bf16[16,3712]{1,0:T(8,128)(2,1)S(1)}, bf16[16,3712]{1,0:T(8,128)(2,1)S(1)}, u32[]{:S(2)}, u32[]{:S(2)}) collective-permute-start(bf16[16,3712]{1,0:T(8,128)(2,1)S(1)} %collective-permute-done.2.refs_3_), channel_id=1, source_target_pairs={{0,2},{1,3},{2,0},{3,1},{4,6},{5,7},{6,4},{7,5},{8,10},{9,11},{10,... | collective-permute-start | bytes 356360 | tf_op jit(solution)/shard_map/ppermute | solution.py:127
  20.2 7.7 %copy-start.4 = (bf16[16,3712]{1,0:T(8,128)(2,1)}, bf16[16,3712]{1,0:T(8,128)(2,1)S(1)}, u32[]{:S(2)}) copy-start(bf16[16,3712]{1,0:T(8,128)(2,1)S(1)} %collective-permute-done.3.refs_4_) | copy-start | bytes 356356
  20.2 4.3 %collective-permute-start.10 = (bf16[16,3712]{1,0:T(8,128)(2,1)S(1)}, bf16[16,3712]{1,0:T(8,128)(2,1)S(1)}, u32[]{:S(2)}, u32[]{:S(2)}) collective-permute-start(bf16[16,3712]{1,0:T(8,128)(2,1)S(1)} %collective-permute-done.2.refs_3_), channel_id=1, source_target_pairs={{0,1},{1,0},{2,3},{3,2},{4,5},{5,4},{6,7},{7,6},{8,9},{9,8},{10,11... | collective-permute-start | bytes 356360 | tf_op jit(solution)/shard_map/ppermute | solution.py:127
  20.2 7.6 %copy-start.5 = (bf16[16,3712]{1,0:T(8,128)(2,1)}, bf16[16,3712]{1,0:T(8,128)(2,1)S(1)}, u32[]{:S(2)}) copy-start(bf16[16,3712]{1,0:T(8,128)(2,1)S(1)} %collective-permute-done.7.refs_8_) | copy-start | bytes 356356
  20.3 4.8 %collective-permute-start.8 = (bf16[16,3712]{1,0:T(8,128)(2,1)S(1)}, bf16[16,3712]{1,0:T(8,128)(2,1)S(1)}, u32[]{:S(2)}, u32[]{:S(2)}) collective-permute-start(bf16[16,3712]{1,0:T(8,128)(2,1)S(1)} %collective-permute-done.refs_1_), channel_id=1, source_target_pairs={{0,1},{1,0},{2,3},{3,2},{4,5},{5,4},{6,7},{7,6},{8,9},{9,8},{10,11... | collective-permute-start | bytes 356360 | tf_op jit(solution)/shard_map/ppermute | solution.py:127
  22.4 5.5 %copy-start.6 = (bf16[16,3712]{1,0:T(8,128)(2,1)}, bf16[16,3712]{1,0:T(8,128)(2,1)S(1)}, u32[]{:S(2)}) copy-start(bf16[16,3712]{1,0:T(8,128)(2,1)S(1)} %collective-permute-done.4.refs_5_) | copy-start | bytes 356356
  22.4 5.3 %collective-permute-start.9 = (bf16[16,3712]{1,0:T(8,128)(2,1)S(1)}, bf16[16,3712]{1,0:T(8,128)(2,1)S(1)}, u32[]{:S(2)}, u32[]{:S(2)}) collective-permute-start(bf16[16,3712]{1,0:T(8,128)(2,1)S(1)} %collective-permute-done.1.refs_2_), channel_id=1, source_target_pairs={{0,1},{1,0},{2,3},{3,2},{4,5},{5,4},{6,7},{7,6},{8,9},{9,8},{10,11... | collective-permute-start | bytes 356360 | tf_op jit(solution)/shard_map/ppermute | solution.py:127
  23.0 4.9 %copy-start.7 = (bf16[16,3712]{1,0:T(8,128)(2,1)}, bf16[16,3712]{1,0:T(8,128)(2,1)S(1)}, u32[]{:S(2)}) copy-start(bf16[16,3712]{1,0:T(8,128)(2,1)S(1)} %collective-permute-done.5.refs_6_) | copy-start | bytes 356356
  23.0 4.7 %collective-permute-start.11 = (bf16[16,3712]{1,0:T(8,128)(2,1)S(1)}, bf16[16,3712]{1,0:T(8,128)(2,1)S(1)}, u32[]{:S(2)}, u32[]{:S(2)}) collective-permute-start(bf16[16,3712]{1,0:T(8,128)(2,1)S(1)} %collective-permute-done.3.refs_4_), channel_id=1, source_target_pairs={{0,1},{1,0},{2,3},{3,2},{4,5},{5,4},{6,7},{7,6},{8,9},{9,8},{10,11... | collective-permute-start | bytes 356360 | tf_op jit(solution)/shard_map/ppermute | solution.py:127
  24.5 3.4 %copy-start.8 = (bf16[16,3712]{1,0:T(8,128)(2,1)}, bf16[16,3712]{1,0:T(8,128)(2,1)S(1)}, u32[]{:S(2)}) copy-start(bf16[16,3712]{1,0:T(8,128)(2,1)S(1)} %collective-permute-done.6.refs_7_) | copy-start | bytes 356356
  24.5 3.3 %collective-permute-start.12 = (bf16[16,3712]{1,0:T(8,128)(2,1)S(1)}, bf16[16,3712]{1,0:T(8,128)(2,1)S(1)}, u32[]{:S(2)}, u32[]{:S(2)}) collective-permute-start(bf16[16,3712]{1,0:T(8,128)(2,1)S(1)} %collective-permute-done.4.refs_5_), channel_id=1, source_target_pairs={{0,1},{1,0},{2,3},{3,2},{4,5},{5,4},{6,7},{7,6},{8,9},{9,8},{10,11... | collective-permute-start | bytes 356360 | tf_op jit(solution)/shard_map/ppermute | solution.py:127
  24.5 3.4 %copy-start.9 = (bf16[16,3712]{1,0:T(8,128)(2,1)}, bf16[16,3712]{1,0:T(8,128)(2,1)S(1)}, u32[]{:S(2)}) copy-start(bf16[16,3712]{1,0:T(8,128)(2,1)S(1)} %collective-permute-done.10.refs_11_) | copy-start | bytes 356356
  24.5 3.3 %collective-permute-start.13 = (bf16[16,3712]{1,0:T(8,128)(2,1)S(1)}, bf16[16,3712]{1,0:T(8,128)(2,1)S(1)}, u32[]{:S(2)}, u32[]{:S(2)}) collective-permute-start(bf16[16,3712]{1,0:T(8,128)(2,1)S(1)} %collective-permute-done.5.refs_6_), channel_id=1, source_target_pairs={{0,1},{1,0},{2,3},{3,2},{4,5},{5,4},{6,7},{7,6},{8,9},{9,8},{10,11... | collective-permute-start | bytes 356360 | tf_op jit(solution)/shard_map/ppermute | solution.py:127
  25.0 2.9 %copy-start.10 = (bf16[16,3712]{1,0:T(8,128)(2,1)}, bf16[16,3712]{1,0:T(8,128)(2,1)S(1)}, u32[]{:S(2)}) copy-start(bf16[16,3712]{1,0:T(8,128)(2,1)S(1)} %collective-permute-done.8.refs_9_) | copy-start | bytes 356356
  25.1 2.8 %collective-permute-start.14 = (bf16[16,3712]{1,0:T(8,128)(2,1)S(1)}, bf16[16,3712]{1,0:T(8,128)(2,1)S(1)}, u32[]{:S(2)}, u32[]{:S(2)}) collective-permute-start(bf16[16,3712]{1,0:T(8,128)(2,1)S(1)} %collective-permute-done.6.refs_7_), channel_id=1, source_target_pairs={{0,1},{1,0},{2,3},{3,2},{4,5},{5,4},{6,7},{7,6},{8,9},{9,8},{10,11... | collective-permute-start | bytes 356360 | tf_op jit(solution)/shard_map/ppermute | solution.py:127
  27.8 53.3 %copy-start.16 = (bf16[1792]{0:T(1024)(128)(2,1)S(1)}, bf16[1792]{0:T(1024)(128)(2,1)}, u32[]{:S(2)}) copy-start(bf16[1792]{0:T(1024)(128)(2,1)} %param.14) | copy-start | bytes 10756
  64.8 2.2 %collective-permute-start.15 = (bf16[128,1920]{1,0:T(8,128)(2,1)}, bf16[128,1920]{1,0:T(8,128)(2,1)S(1)}, u32[]{:S(2)}, u32[]{:S(2)}) collective-permute-start(bf16[128,1920]{1,0:T(8,128)(2,1)} %get-tuple-element.6), channel_id=1, source_target_pairs={{0,1},{1,0},{2,3},{3,2},{4,5},{5,4},{6,7},{7,6},{8,9},{9,8},{10,11... | collective-permute-start | bytes 1474568 | tf_op jit(solution)/shard_map/ppermute | solution.py:127
  68.2 8.3 %collective-permute-start.16 = (bf16[64,1920]{1,0:T(8,128)(2,1)S(1)}, bf16[64,1920]{1,0:T(8,128)(2,1)S(1)}, u32[]{:S(2)}, u32[]{:S(2)}) collective-permute-start(bf16[64,1920]{1,0:T(8,128)(2,1)S(1)} %slice.37), channel_id=1, source_target_pairs={{0,2},{1,3},{2,0},{3,1},{4,6},{5,7},{6,4},{7,5},{8,10},{9,11},{10,... | collective-permute-start | bytes 737288 | tf_op jit(solution)/shard_map/ppermute | solution.py:127
  76.6 4.6 %collective-permute-start.17 = (bf16[16,1920]{1,0:T(8,128)(2,1)S(1)}, bf16[16,1920]{1,0:T(8,128)(2,1)S(1)}, u32[]{:S(2)}, u32[]{:S(2)}) collective-permute-start(bf16[16,1920]{1,0:T(8,128)(2,1)S(1)} %get-tuple-element.13), channel_id=1, source_target_pairs={{0,4},{4,0},{8,12},{12,8},{1,5},{5,1},{9,13},{13,9},{2,6},{6,2},{1... | collective-permute-start | bytes 184328 | tf_op jit(solution)/shard_map/ppermute | solution.py:127
  77.1 7.1 %collective-permute-start.18 = (bf16[16,1920]{1,0:T(8,128)(2,1)S(1)}, bf16[16,1920]{1,0:T(8,128)(2,1)S(1)}, u32[]{:S(2)}, u32[]{:S(2)}) collective-permute-start(bf16[16,1920]{1,0:T(8,128)(2,1)S(1)} %get-tuple-element.15), channel_id=1, source_target_pairs={{0,8},{4,12},{8,0},{12,4},{1,9},{5,13},{9,1},{13,5},{2,10},{6,14},... | collective-permute-start | bytes 184328 | tf_op jit(solution)/shard_map/ppermute | solution.py:127
  79.6 6.0 %collective-permute-start.19 = (bf16[16,1920]{1,0:T(8,128)(2,1)S(1)}, bf16[16,1920]{1,0:T(8,128)(2,1)S(1)}, u32[]{:S(2)}, u32[]{:S(2)}) collective-permute-start(bf16[16,1920]{1,0:T(8,128)(2,1)S(1)} %get-tuple-element.14), channel_id=1, source_target_pairs={{0,12},{4,8},{8,4},{12,0},{1,13},{5,9},{9,5},{13,1},{2,14},{6,10},... | collective-permute-start | bytes 184328 | tf_op jit(solution)/shard_map/ppermute | solution.py:127
  (5 other events, 3.4 us)

commit v3 on v2

--- a/solution.py
+++ b/solution.py
@@ -2,6 +2,7 @@
 
 import jax
 import jax.numpy as jnp
+import numpy as np
 from jax import lax
 from jax.experimental import pallas as pl
 from jax.experimental.pallas import tpu as pltpu
@@ -131,29 +132,31 @@
     token_refs, refs = refs[:blocks], refs[blocks:]
     tail_ref, w_gate, w_up, w_down, keep_ref, send_ref, tokens, copied, gates, ups, downs, loaded, spread, weighted, norms, grads, backs, hits, routes = refs
     number = w_gate.shape[0]
-    each = token_refs[0].shape[0]
-    count = each * blocks
+    starts = np.cumsum([0] + [ref.shape[0] for ref in token_refs])
+    count = int(starts[-1])
 
     def loads(turn, k):
         expert = turn * group + k
-        slot = lax.rem(turn, 2) * group + k
+        slot = lax.rem(turn, 3) * group + k
         return [
             pltpu.make_async_copy(source.at[expert], target.at[slot], loaded.at[slot, j])
             for j, (source, target) in enumerate(((w_gate, gates), (w_up, ups), (w_down, downs)))
         ]
 
     copies = [
-        pltpu.make_async_copy(ref, tokens.at[pl.ds(j * each, each)], copied.at[j])
+        pltpu.make_async_copy(ref, tokens.at[pl.ds(int(starts[j]), ref.shape[0])], copied.at[j])
         for j, ref in enumerate(token_refs)
     ]
     for copy in copies:
         copy.start()
-    for turn in range(2):
-        for k in range(group):
-            for copy in loads(turn, k):
-                copy.start()
     for copy in copies:
         copy.wait()
+    for k in range(group):
+        for copy in loads(0, k):
+            copy.start()
+    for k in range(group):
+        for copy in loads(1, k):
+            copy.start()
     codes = tokens[:, 2 * features :].astype(F32).T
     weights = codes[TOPK : 2 * TOPK]
     local = codes[:TOPK] - (lax.axis_index("expert") * number).astype(F32)
@@ -178,13 +181,19 @@
     routes[...] = jnp.zeros_like(routes)
 
     def run(turn, _):
-        base = lax.rem(turn, 2) * group
+        base = lax.rem(turn, 3) * group
         heres = [
             pl.ds(pl.multiple_of((turn * group + k) * rows, rows), rows) for k in range(group)
         ]
         for k in range(group):
             for copy in loads(turn, k):
                 copy.wait()
+        @pl.when(turn + 2 < number // group)
+        def _():
+            for k in range(group):
+                for copy in loads(turn + 2, k):
+                    copy.start()
+
         pre = []
         for k in range(group):
             x, dy = norms[heres[k]], grads[heres[k]]
@@ -205,20 +214,26 @@
             here = (turn * group + k).astype(F32)
             routes[...] += jnp.where(hits[...] == here, by_token, 0.0)
 
-        @pl.when(turn + 2 < number // group)
-        def _():
-            for k in range(group):
-                for copy in loads(turn + 2, k):
-                    copy.start()
-
         return 0
 
     lax.fori_loop(0, number // group, run, 0)
     half = count // 2
     result = dot(weighted[...], backs[...], TN).astype(BF16)
-    scores = jnp.concatenate([routes[...], jnp.zeros((LANES - TOPK, count), F32)], axis=0).T
-    tail = jnp.concatenate([tail_ref[...]] * blocks, axis=0)
-    last = (scores + tail).astype(BF16)
+    each = tail_ref.shape[0]
+    line = features // LANES
+    token = lax.broadcasted_iota(jnp.int32, (count, LANES), 0)
+    lane = lax.broadcasted_iota(jnp.int32, (count, LANES), 1)
+    repeat = (
+        lax.broadcasted_iota(jnp.int32, (TOPK, LANES), 1) % TOPK
+        == lax.broadcasted_iota(jnp.int32, (TOPK, LANES), 0)
+    ).astype(BF16)
+    scores = dot(routes[...].astype(BF16), repeat, TN)
+    scores = jnp.where(lane // TOPK == token % each, scores, 0.0).astype(BF16)
+    row = lax.broadcasted_iota(jnp.int32, (count, count), 0)
+    column = lax.broadcasted_iota(jnp.int32, (count, count), 1)
+    gather = ((row % each == line) & (row // each == column // each)).astype(BF16)
+    tail = jnp.concatenate([tail_ref[...]] * (count // each), axis=0)
+    last = (dot(gather, scores) + tail).astype(BF16)
     keep_ref[:, :features] = result[:half]
     send_ref[:, :features] = result[half:]
     keep_ref[:, features:] = last[:half]
@@ -228,7 +243,7 @@
 def run_experts(token_blocks, tail, w_gate, w_up, w_down, sources):
     local, features, hidden = w_gate.shape
     blocks = len(token_blocks)
-    count = blocks * token_blocks[0].shape[0]
+    count = sum(block.shape[0] for block in token_blocks)
     rows = sources * CAP
     width = features + LANES
     group = 2
@@ -242,10 +257,10 @@
         scratch_shapes=[
             pltpu.VMEM((count, 2 * features + LANES), BF16),
             pltpu.SemaphoreType.DMA((blocks,)),
-            pltpu.VMEM((2 * group, features, hidden), BF16),
-            pltpu.VMEM((2 * group, features, hidden), BF16),
-            pltpu.VMEM((2 * group, hidden, features), BF16),
-            pltpu.SemaphoreType.DMA((2 * group, 3)),
+            pltpu.VMEM((3 * group, features, hidden), BF16),
+            pltpu.VMEM((3 * group, features, hidden), BF16),
+            pltpu.VMEM((3 * group, hidden, features), BF16),
+            pltpu.SemaphoreType.DMA((3 * group, 3)),
             pltpu.VMEM((local * rows, count), BF16),
             pltpu.VMEM((local * rows, count), BF16),
             pltpu.VMEM((local * rows, features), BF16),
@@ -254,9 +269,82 @@
             pltpu.VMEM((TOPK, count), F32),
             pltpu.VMEM((TOPK, count), F32),
         ],
-        compiler_params=pltpu.CompilerParams(vmem_limit_bytes=60 << 20),
+        compiler_params=pltpu.CompilerParams(vmem_limit_bytes=44 << 20),
         name="experts",
     )(*token_blocks, tail, w_gate, w_up, w_down)
+
+
+def pack_kernel(norm_ref, grad_ref, shared_ref, ids_ref, weight_ref, gate_ref, packed_ref, tail_ref, term_ref):
+    tokens, features = norm_ref.shape
+    norm = norm_ref[...].astype(F32)
+    grad = grad_ref[...].astype(F32)
+    gate = gate_ref[...].astype(F32)
+    packed_ref[:, :features] = norm_ref[...]
+    packed_ref[:, features : 2 * features] = grad_ref[...]
+    lane = lax.broadcasted_iota(jnp.int32, (TOPK, LANES), 1)
+    source = lax.broadcasted_iota(jnp.int32, (TOPK, LANES), 0)
+    ids = ids_ref[...].astype(F32).astype(BF16)
+    codes = dot(ids, (lane == source).astype(BF16)) + dot(
+        weight_ref[...], (lane == source + TOPK).astype(BF16)
+    )
+    packed_ref[:, 2 * features :] = codes.astype(BF16)
+    gate_value = jax.nn.sigmoid(jnp.sum(norm * gate, axis=1, keepdims=True))
+    inner = jnp.sum(grad * shared_ref[...].astype(F32), axis=1, keepdims=True)
+    delta = inner * gate_value * (1.0 - gate_value)
+    term_ref[...] = delta * gate
+    local = jnp.sum(delta * norm, axis=0, keepdims=True)
+    tail_ref[...] = jnp.zeros_like(tail_ref)
+    for r in range(features // LANES):
+        tail_ref[r : r + 1, :] = local[:, r * LANES : (r + 1) * LANES]
+
+
+def pack(norm_input, out_grad, shared_out, expert_ids, route_weight, shared_gate):
+    tokens, features = norm_input.shape
+    return pl.pallas_call(
+        pack_kernel,
+        out_shape=[
+            jax.ShapeDtypeStruct((tokens, 2 * features + LANES), BF16),
+            jax.ShapeDtypeStruct((tokens, LANES), F32),
+            jax.ShapeDtypeStruct((tokens, features), F32),
+        ],
+        compiler_params=pltpu.CompilerParams(vmem_limit_bytes=4 << 20),
+        name="pack",
+    )(norm_input, out_grad, shared_out, expert_ids, route_weight, shared_gate[None, :])
+
+
+def finish_kernel(total_ref, *refs):
+    parts, (term_ref, input_ref, route_ref, gate_ref) = refs[:-4], refs[-4:]
+    tokens, features = term_ref.shape
+    final = total_ref[:tokens].astype(F32)
+    for part in parts:
+        final = final + part[...].astype(F32)
+    input_ref[...] = (final[:, :features] + term_ref[...]).astype(BF16)
+    line = features // LANES
+    gate_ref[...] = final[:line, features:]
+    lane = lax.broadcasted_iota(jnp.int32, (tokens, LANES), 1)
+    token = lax.broadcasted_iota(jnp.int32, (tokens, LANES), 0)
+    spread = jnp.where(lane // TOPK == token, final[line : line + 1, features:], 0.0)
+    choose = (
+        lax.broadcasted_iota(jnp.int32, (LANES, TOPK), 0) % TOPK
+        == lax.broadcasted_iota(jnp.int32, (LANES, TOPK), 1)
+    ).astype(F32)
+    route_ref[...] = jnp.dot(
+        spread, choose, precision=lax.Precision.HIGHEST, preferred_element_type=F32
+    )
+
+
+def finish(total, parts, term):
+    tokens, features = term.shape
+    return pl.pallas_call(
+        finish_kernel,
+        out_shape=[
+            jax.ShapeDtypeStruct((tokens, features), BF16),
+            jax.ShapeDtypeStruct((tokens, TOPK), F32),
+            jax.ShapeDtypeStruct((features // LANES, LANES), F32),
+        ],
+        compiler_params=pltpu.CompilerParams(vmem_limit_bytes=4 << 20),
+        name="finish",
+    )(total, *parts, term)
 
 
 def square_device(
@@ -264,41 +352,24 @@
 ):
     tokens, features = norm_input.shape
     sources = lax.axis_size("expert")
-    codes = jnp.concatenate(
-        [
-            expert_ids.astype(BF16),
-            route_weight,
-            jnp.zeros((tokens, LANES - 2 * TOPK), BF16),
-        ],
-        axis=1,
-    )
-    mine = jnp.concatenate([norm_input, out_grad, codes], axis=1)
-    held = [mine] + [swap(mine, "expert", d) for d in range(1, sources)]
-    held = held + [swap(block, "dp", 2) for block in held]
-    held = held + [swap(block, "dp", 1) for block in held]
-
-    gate_value = jax.nn.sigmoid(
-        jnp.dot(norm_input, shared_gate, preferred_element_type=F32)
-    )
-    inner = jnp.sum(out_grad.astype(F32) * shared_out.astype(F32), axis=1)
-    gate_delta = inner * gate_value * (1.0 - gate_value)
-    gate_local = jnp.sum(gate_delta[:, None] * norm_input.astype(F32), axis=0)
-    share = features // tokens
-    tail = jnp.pad(gate_local.reshape(tokens, share), ((0, 0), (TOPK, LANES - TOPK - share)))
-
+    mine, tail, term = pack(
+        norm_input, out_grad, shared_out, expert_ids, route_weight, shared_gate
+    )
+    along = [mine] + [swap(mine, "expert", d) for d in range(1, sources)]
+    near, far = jnp.concatenate(along[:2], axis=0), jnp.concatenate(along[2:], axis=0)
+    near_x, far_x = swap(near, "dp", 2), swap(far, "dp", 2)
+    both = jnp.concatenate([near, far], axis=0)
+    held = [near, far, near_x, far_x]
+    held += [swap(block, "dp", 1) for block in (both, near_x, far_x)]
     kept, sent = run_experts(held, tail, w_gate, w_up, w_down, sources)
     total = (kept.astype(F32) + swap(sent, "dp", 1).astype(F32)).astype(BF16)
     half = total.shape[0] // 2
     total = (total[:half].astype(F32) + swap(total[half:], "dp", 2).astype(F32)).astype(BF16)
-    final = total[:tokens].astype(F32)
-    for d in range(1, sources):
-        final = final + swap(total[d * tokens : (d + 1) * tokens], "expert", d).astype(F32)
-    input_grad = (
-        final[:, :features] + gate_delta[:, None] * shared_gate.astype(F32)[None, :]
-    ).astype(BF16)
-    route_grad = final[:, features : features + TOPK]
-    gate_grad = final[:, features + TOPK : features + TOPK + share].reshape(features)
-    return (input_grad, route_grad, gate_grad)
+    parts = [
+        swap(total[d * tokens : (d + 1) * tokens], "expert", d) for d in range(sources - 1, 0, -1)
+    ]
+    input_grad, route_grad, gate_grad = finish(total, parts, term)
+    return (input_grad, route_grad, gate_grad.reshape(features))
 
 
 def solution(mesh):

time: 88.3 us -> 84.7 us (0.959)
  waiting for transfers between devices: 21.2 us -> 30.1 us
  other arithmetic: 4.54 us -> 0.23 us
  Pallas kernels: 35.6 us -> 32.2 us
  starting transfers between devices: 18.6 us -> 15.7 us
  matrix products: 0.94 us -> 0 us
    ppermute x20 -> x13, waiting for transfers between devices: 21.2 us -> 30.1 us  [swap(): return lax.ppermute(value, axis, [(i, i ^ distance) for i in range(size)])]
    pallas_call x1, Pallas kernels: 35.6 us -> 31.3 us  [run_experts(): pl.pallas_call(functools.partial(experts_kernel, features, rows, blocks,...]
    ppermute x20 -> x13, starting transfers between devices: 18.6 us -> 15.7 us  [swap(): return lax.ppermute(value, axis, [(i, i ^ distance) for i in range(size)])]
    reduce_sum x2 -> x0, other arithmetic: 1.9 us -> none  [the longest x1 0.97 us: square_device(): inner = jnp.sum(out_grad.astype(F32) * shared_out.astype(F32), axis=1)]
    convert_element_type x3 -> x0, other arithmetic: 1.4 us -> none  [the longest x1 0.7 us: square_device(): input_grad = (final[:, :features] + gate_delta[:, None] * shared_gate.ast...]
    unnamed x37 -> x11, local copies, waits for them, and re-layouts: 3.41 us -> 4.65 us
    convert_element_type x1, other arithmetic: 1.14 us -> 0.12 us  [square_device(): total = (kept.astype(F32) + swap(sent, 'dp', 1).astype(F32)).astype(BF16)]
    dot_general x1 -> x0, matrix products: 0.94 us -> none  [square_device(): jnp.dot(norm_input, shared_gate, preferred_element_type=F32)]
  transfers between devices with their start and end apart: 20 -> 13, of which waited for: 9 -> 9; matrix products, arithmetic and copies ran while one was open for 5% -> 0% of each run, Pallas kernels for 0% -> 0%
where the time goes in v3:
time: 84.7 us; the launch traced here: 84.4 us
  Pallas kernels  32.2 us (38%)
  waiting for transfers between devices  30.1 us (36%)
  starting transfers between devices  15.7 us (19%)
  local copies, waits for them, and re-layouts  5.41 us (6%)
    pallas_call x1, Pallas kernels, run_experts(): pl.pallas_call(functools.partial(experts_kernel, features, rows, blocks,...  31.3 us
    ppermute x13, waiting for transfers between devices, swap(): return lax.ppermute(value, axis, [(i, i ^ distance) for i in range(size)])  30.1 us
    ppermute x13, starting transfers between devices, swap(): return lax.ppermute(value, axis, [(i, i ^ distance) for i in range(size)])  15.7 us
    unnamed x11, local copies, waits for them, and re-layouts  4.65 us
  transfers between devices with their start and end apart: 13, of which 9 were waited for; matrix products, arithmetic and copies ran while one was open for 0% of the time, Pallas kernels for 0%

profile of v3, /device:TPU:0, one launch (start us, length us, event | category | flops | bytes accessed | tf_op | source)
XLA Modules:
  0.0 84.4 jit_solution(10041134822907976578)
XLA Ops:
  0.6 0.8 copy.13.weight_ref
  1.4 0.7 broadcast_in_dim.3.gate_ref
  2.1 0.8 copy.12.ids_ref
  2.8 0.8 copy-done
  3.7 0.8 copy-done.1
  4.5 0.8 copy-done.2
  5.3 0.1 pack.1
  5.4 5.1 %collective-permute-start.2 = (bf16[16,3712]{1,0:T(8,128)(2,1)S(1)}, bf16[16,3712]{1,0:T(8,128)(2,1)S(1)}, u32[]{:S(2)}, u32[]{:S(2)}) collective-permute-start(bf16[16,3712]{1,0:T(8,128)(2,1)S(1)} %get-tuple-element.11), channel_id=1, source_target_pairs={{0,12},{4,8},{8,4},{12,0},{1,13},{5,9},{9,5},{13,1},{2,14},{6,10},... | collective-permute-start | bytes 356360 | tf_op jit(solution)/shard_map/ppermute | solution.py:128
  10.6 0.6 collective-permute-start
  11.2 7.0 %collective-permute-done = bf16[16,3712]{1,0:T(8,128)(2,1)S(1)} collective-permute-done((bf16[16,3712]{1,0:T(8,128)(2,1)S(1)}, bf16[16,3712]{1,0:T(8,128)(2,1)S(1)}, u32[]{:S(2)}, u32[]{:S(2)}) %collective-permute-start) | collective-permute-done | bytes 118816 | tf_op jit(solution)/shard_map/ppermute | solution.py:128
  18.2 1.6 %collective-permute-start.3 = (bf16[32,3712]{1,0:T(8,128)(2,1)S(1)}, bf16[32,3712]{1,0:T(8,128)(2,1)S(1)}, u32[]{:S(2)}, u32[]{:S(2)}) collective-permute-start(bf16[32,3712]{1,0:T(8,128)(2,1)S(1)} %constant_dynamic-update-slice_fusion.refs_0_), channel_id=1, source_target_pairs={{0,2},{1,3},{2,0},{3,1},{4,6},{5,7},{6,4},{7,5},{8,10},{9,11},{10,... | collective-permute-start | bytes 712712 | tf_op jit(solution)/shard_map/ppermute | solution.py:128
  19.8 0.8 collective-permute-done.1
  20.6 1.6 %collective-permute-start.4 = (bf16[32,3712]{1,0:T(8,128)(2,1)S(1)}, bf16[32,3712]{1,0:T(8,128)(2,1)S(1)}, u32[]{:S(2)}, u32[]{:S(2)}) collective-permute-start(bf16[32,3712]{1,0:T(8,128)(2,1)S(1)} %constant_dynamic-update-slice_fusion.2.refs_1_), channel_id=1, source_target_pairs={{0,2},{1,3},{2,0},{3,1},{4,6},{5,7},{6,4},{7,5},{8,10},{9,11},{10,... | collective-permute-start | bytes 712712 | tf_op jit(solution)/shard_map/ppermute | solution.py:128
  22.2 0.1 pad_maximum_fusion
  22.2 0.1 collective-permute-start.5
  22.3 4.7 %collective-permute-done.3.refs_2_ = bf16[32,3712]{1,0:T(8,128)(2,1)S(1)} collective-permute-done((bf16[32,3712]{1,0:T(8,128)(2,1)S(1)}, bf16[32,3712]{1,0:T(8,128)(2,1)S(1)}, u32[]{:S(2)}, u32[]{:S(2)}) %collective-permute-start.3) | collective-permute-done | bytes 237600 | tf_op jit(solution)/shard_map/ppermute | solution.py:128
  27.0 3.1 %collective-permute-done.4.refs_3_ = bf16[32,3712]{1,0:T(8,128)(2,1)S(1)} collective-permute-done((bf16[32,3712]{1,0:T(8,128)(2,1)S(1)}, bf16[32,3712]{1,0:T(8,128)(2,1)S(1)}, u32[]{:S(2)}, u32[]{:S(2)}) %collective-permute-start.4) | collective-permute-done | bytes 237600 | tf_op jit(solution)/shard_map/ppermute | solution.py:128
  30.1 1.5 %collective-permute-done.7.refs_6_ = bf16[32,3712]{1,0:T(8,128)(2,1)S(1)} collective-permute-done((bf16[32,3712]{1,0:T(8,128)(2,1)S(1)}, bf16[32,3712]{1,0:T(8,128)(2,1)S(1)}, u32[]{:S(2)}, u32[]{:S(2)}) %collective-permute-start.7) | collective-permute-done | bytes 237600 | tf_op jit(solution)/shard_map/ppermute | solution.py:128
  31.6 31.3 %experts.1 = (bf16[128,1920]{1,0:T(8,128)(2,1)S(1)}, bf16[128,1920]{1,0:T(8,128)(2,1)S(1)}) custom-call(bf16[32,3712]{1,0:T(8,128)(2,1)S(1)} %constant_dynamic-update-slice_fusion.refs_0_, bf16[32,3712]{1,0:T(8,128)(2,1)S(1)} %constant_dynamic-update-slice_fusion.2.refs_1_, bf16[32,3712]{1,0:T(8,128)(2,1)S(1)} %collective-permute-done.3.refs_2_, ...), custom_call_target="tpu_custom_call" | custom-call | tf_op jit(solution)/shard_map/experts/pallas_call | solution.py:252
  62.9 0.2 collective-permute-start.8
  63.1 1.7 %collective-permute-done.8 = bf16[128,1920]{1,0:T(8,128)(2,1)S(1)} collective-permute-done((bf16[128,1920]{1,0:T(8,128)(2,1)S(1)}, bf16[128,1920]{1,0:T(8,128)(2,1)S(1)}, u32[]{:S(2)}, u32[]{:S(2)}) %collective-permute-start.8) | collective-permute-done | bytes 491552 | tf_op jit(solution)/shard_map/ppermute | solution.py:128
  64.8 0.1 add_convert_fusion
  65.0 1.6 %collective-permute-start.9 = (bf16[64,1920]{1,0:T(8,128)(2,1)S(1)}, bf16[64,1920]{1,0:T(8,128)(2,1)S(1)}, u32[]{:S(2)}, u32[]{:S(2)}) collective-permute-start(bf16[64,1920]{1,0:T(8,128)(2,1)S(1)} %slice.21), channel_id=1, source_target_pairs={{0,2},{1,3},{2,0},{3,1},{4,6},{5,7},{6,4},{7,5},{8,10},{9,11},{10,... | collective-permute-start | bytes 737288 | tf_op jit(solution)/shard_map/ppermute | solution.py:128
  66.5 6.5 %collective-permute-done.9 = bf16[64,1920]{1,0:T(8,128)(2,1)S(1)} collective-permute-done((bf16[64,1920]{1,0:T(8,128)(2,1)S(1)}, bf16[64,1920]{1,0:T(8,128)(2,1)S(1)}, u32[]{:S(2)}, u32[]{:S(2)}) %collective-permute-start.9) | collective-permute-done | bytes 245792 | tf_op jit(solution)/shard_map/ppermute | solution.py:128
  73.0 0.1 add_convert_fusion.1.total_ref
  73.1 2.5 %collective-permute-start.12 = (bf16[16,1920]{1,0:T(8,128)(2,1)S(1)}, bf16[16,1920]{1,0:T(8,128)(2,1)S(1)}, u32[]{:S(2)}, u32[]{:S(2)}) collective-permute-start(bf16[16,1920]{1,0:T(8,128)(2,1)S(1)} %get-tuple-element.22), channel_id=1, source_target_pairs={{0,4},{4,0},{8,12},{12,8},{1,5},{5,1},{9,13},{13,9},{2,6},{6,2},{1... | collective-permute-start | bytes 184328 | tf_op jit(solution)/shard_map/ppermute | solution.py:128
  75.7 1.2 %collective-permute-start.11 = (bf16[16,1920]{1,0:T(8,128)(2,1)S(1)}, bf16[16,1920]{1,0:T(8,128)(2,1)S(1)}, u32[]{:S(2)}, u32[]{:S(2)}) collective-permute-start(bf16[16,1920]{1,0:T(8,128)(2,1)S(1)} %get-tuple-element.23), channel_id=1, source_target_pairs={{0,8},{4,12},{8,0},{12,4},{1,9},{5,13},{9,1},{13,5},{2,10},{6,14},... | collective-permute-start | bytes 184328 | tf_op jit(solution)/shard_map/ppermute | solution.py:128
  76.9 1.2 %collective-permute-start.10 = (bf16[16,1920]{1,0:T(8,128)(2,1)S(1)}, bf16[16,1920]{1,0:T(8,128)(2,1)S(1)}, u32[]{:S(2)}, u32[]{:S(2)}) collective-permute-start(bf16[16,1920]{1,0:T(8,128)(2,1)S(1)} %get-tuple-element.24), channel_id=1, source_target_pairs={{0,12},{4,8},{8,4},{12,0},{1,13},{5,9},{9,5},{13,1},{2,14},{6,10},... | collective-permute-start | bytes 184328 | tf_op jit(solution)/shard_map/ppermute | solution.py:128
  78.1 3.9 %collective-permute-done.11.refs_1_ = bf16[16,1920]{1,0:T(8,128)(2,1)S(1)} collective-permute-done((bf16[16,1920]{1,0:T(8,128)(2,1)S(1)}, bf16[16,1920]{1,0:T(8,128)(2,1)S(1)}, u32[]{:S(2)}, u32[]{:S(2)}) %collective-permute-start.11) | collective-permute-done | bytes 61472 | tf_op jit(solution)/shard_map/ppermute | solution.py:128
  82.1 1.0 %collective-permute-done.10.refs_0_ = bf16[16,1920]{1,0:T(8,128)(2,1)S(1)} collective-permute-done((bf16[16,1920]{1,0:T(8,128)(2,1)S(1)}, bf16[16,1920]{1,0:T(8,128)(2,1)S(1)}, u32[]{:S(2)}, u32[]{:S(2)}) %collective-permute-start.10) | collective-permute-done | bytes 61472 | tf_op jit(solution)/shard_map/ppermute | solution.py:128
  83.0 0.7 finish.1
  83.7 0.7 copy.14
  (16 shorter events, 0.1 us)
Async XLA Ops:
  2.8 0.8 copy-start
  3.7 0.8 copy-start.1
  4.5 0.8 copy-start.2
  5.4 15.2 %collective-permute-start.2 = (bf16[16,3712]{1,0:T(8,128)(2,1)S(1)}, bf16[16,3712]{1,0:T(8,128)(2,1)S(1)}, u32[]{:S(2)}, u32[]{:S(2)}) collective-permute-start(bf16[16,3712]{1,0:T(8,128)(2,1)S(1)} %get-tuple-element.11), channel_id=1, source_target_pairs={{0,12},{4,8},{8,4},{12,0},{1,13},{5,9},{9,5},{13,1},{2,14},{6,10},... | collective-permute-start | bytes 356360 | tf_op jit(solution)/shard_map/ppermute | solution.py:128
  10.6 10.0 %collective-permute-start.1 = (bf16[16,3712]{1,0:T(8,128)(2,1)S(1)}, bf16[16,3712]{1,0:T(8,128)(2,1)S(1)}, u32[]{:S(2)}, u32[]{:S(2)}) collective-permute-start(bf16[16,3712]{1,0:T(8,128)(2,1)S(1)} %get-tuple-element.11), channel_id=1, source_target_pairs={{0,8},{4,12},{8,0},{12,4},{1,9},{5,13},{9,1},{13,5},{2,10},{6,14},... | collective-permute-start | bytes 356360 | tf_op jit(solution)/shard_map/ppermute | solution.py:128
  10.6 7.6 %collective-permute-start = (bf16[16,3712]{1,0:T(8,128)(2,1)S(1)}, bf16[16,3712]{1,0:T(8,128)(2,1)S(1)}, u32[]{:S(2)}, u32[]{:S(2)}) collective-permute-start(bf16[16,3712]{1,0:T(8,128)(2,1)S(1)} %get-tuple-element.11), channel_id=1, source_target_pairs={{0,4},{4,0},{8,12},{12,8},{1,5},{5,1},{9,13},{13,9},{2,6},{6,2},{1... | collective-permute-start | bytes 356360 | tf_op jit(solution)/shard_map/ppermute | solution.py:128
  18.2 8.8 %collective-permute-start.3 = (bf16[32,3712]{1,0:T(8,128)(2,1)S(1)}, bf16[32,3712]{1,0:T(8,128)(2,1)S(1)}, u32[]{:S(2)}, u32[]{:S(2)}) collective-permute-start(bf16[32,3712]{1,0:T(8,128)(2,1)S(1)} %constant_dynamic-update-slice_fusion.refs_0_), channel_id=1, source_target_pairs={{0,2},{1,3},{2,0},{3,1},{4,6},{5,7},{6,4},{7,5},{8,10},{9,11},{10,... | collective-permute-start | bytes 712712 | tf_op jit(solution)/shard_map/ppermute | solution.py:128
  20.6 9.4 %collective-permute-start.4 = (bf16[32,3712]{1,0:T(8,128)(2,1)S(1)}, bf16[32,3712]{1,0:T(8,128)(2,1)S(1)}, u32[]{:S(2)}, u32[]{:S(2)}) collective-permute-start(bf16[32,3712]{1,0:T(8,128)(2,1)S(1)} %constant_dynamic-update-slice_fusion.2.refs_1_), channel_id=1, source_target_pairs={{0,2},{1,3},{2,0},{3,1},{4,6},{5,7},{6,4},{7,5},{8,10},{9,11},{10,... | collective-permute-start | bytes 712712 | tf_op jit(solution)/shard_map/ppermute | solution.py:128
  22.2 9.3 %collective-permute-start.5 = (bf16[64,3712]{1,0:T(8,128)(2,1)S(1)}, bf16[64,3712]{1,0:T(8,128)(2,1)S(1)}, u32[]{:S(2)}, u32[]{:S(2)}) collective-permute-start(bf16[64,3712]{1,0:T(8,128)(2,1)S(1)} %pad_maximum_fusion), channel_id=1, source_target_pairs={{0,1},{1,0},{2,3},{3,2},{4,5},{5,4},{6,7},{7,6},{8,9},{9,8},{10,11... | collective-permute-start | bytes 1425416 | tf_op jit(solution)/shard_map/ppermute | solution.py:128
  27.0 3.1 %collective-permute-start.6 = (bf16[32,3712]{1,0:T(8,128)(2,1)S(1)}, bf16[32,3712]{1,0:T(8,128)(2,1)S(1)}, u32[]{:S(2)}, u32[]{:S(2)}) collective-permute-start(bf16[32,3712]{1,0:T(8,128)(2,1)S(1)} %collective-permute-done.3.refs_2_), channel_id=1, source_target_pairs={{0,1},{1,0},{2,3},{3,2},{4,5},{5,4},{6,7},{7,6},{8,9},{9,8},{10,11... | collective-permute-start | bytes 712712 | tf_op jit(solution)/shard_map/ppermute | solution.py:128
  30.1 1.5 %collective-permute-start.7 = (bf16[32,3712]{1,0:T(8,128)(2,1)S(1)}, bf16[32,3712]{1,0:T(8,128)(2,1)S(1)}, u32[]{:S(2)}, u32[]{:S(2)}) collective-permute-start(bf16[32,3712]{1,0:T(8,128)(2,1)S(1)} %collective-permute-done.4.refs_3_), channel_id=1, source_target_pairs={{0,1},{1,0},{2,3},{3,2},{4,5},{5,4},{6,7},{7,6},{8,9},{9,8},{10,11... | collective-permute-start | bytes 712712 | tf_op jit(solution)/shard_map/ppermute | solution.py:128
  62.9 1.9 %collective-permute-start.8 = (bf16[128,1920]{1,0:T(8,128)(2,1)S(1)}, bf16[128,1920]{1,0:T(8,128)(2,1)S(1)}, u32[]{:S(2)}, u32[]{:S(2)}) collective-permute-start(bf16[128,1920]{1,0:T(8,128)(2,1)S(1)} %get-tuple-element.14), channel_id=1, source_target_pairs={{0,1},{1,0},{2,3},{3,2},{4,5},{5,4},{6,7},{7,6},{8,9},{9,8},{10,11... | collective-permute-start | bytes 1474568 | tf_op jit(solution)/shard_map/ppermute | solution.py:128
  65.0 8.1 %collective-permute-start.9 = (bf16[64,1920]{1,0:T(8,128)(2,1)S(1)}, bf16[64,1920]{1,0:T(8,128)(2,1)S(1)}, u32[]{:S(2)}, u32[]{:S(2)}) collective-permute-start(bf16[64,1920]{1,0:T(8,128)(2,1)S(1)} %slice.21), channel_id=1, source_target_pairs={{0,2},{1,3},{2,0},{3,1},{4,6},{5,7},{6,4},{7,5},{8,10},{9,11},{10,... | collective-permute-start | bytes 737288 | tf_op jit(solution)/shard_map/ppermute | solution.py:128
  73.1 5.0 %collective-permute-start.12 = (bf16[16,1920]{1,0:T(8,128)(2,1)S(1)}, bf16[16,1920]{1,0:T(8,128)(2,1)S(1)}, u32[]{:S(2)}, u32[]{:S(2)}) collective-permute-start(bf16[16,1920]{1,0:T(8,128)(2,1)S(1)} %get-tuple-element.22), channel_id=1, source_target_pairs={{0,4},{4,0},{8,12},{12,8},{1,5},{5,1},{9,13},{13,9},{2,6},{6,2},{1... | collective-permute-start | bytes 184328 | tf_op jit(solution)/shard_map/ppermute | solution.py:128
  75.7 6.4 %collective-permute-start.11 = (bf16[16,1920]{1,0:T(8,128)(2,1)S(1)}, bf16[16,1920]{1,0:T(8,128)(2,1)S(1)}, u32[]{:S(2)}, u32[]{:S(2)}) collective-permute-start(bf16[16,1920]{1,0:T(8,128)(2,1)S(1)} %get-tuple-element.23), channel_id=1, source_target_pairs={{0,8},{4,12},{8,0},{12,4},{1,9},{5,13},{9,1},{13,5},{2,10},{6,14},... | collective-permute-start | bytes 184328 | tf_op jit(solution)/shard_map/ppermute | solution.py:128
  76.9 6.1 %collective-permute-start.10 = (bf16[16,1920]{1,0:T(8,128)(2,1)S(1)}, bf16[16,1920]{1,0:T(8,128)(2,1)S(1)}, u32[]{:S(2)}, u32[]{:S(2)}) collective-permute-start(bf16[16,1920]{1,0:T(8,128)(2,1)S(1)} %get-tuple-element.24), channel_id=1, source_target_pairs={{0,12},{4,8},{8,4},{12,0},{1,13},{5,9},{9,5},{13,1},{2,14},{6,10},... | collective-permute-start | bytes 184328 | tf_op jit(solution)/shard_map/ppermute | solution.py:128

commit v4 on v3

--- a/solution.py
+++ b/solution.py
@@ -274,22 +274,58 @@
     )(*token_blocks, tail, w_gate, w_up, w_down)
 
 
-def pack_kernel(norm_ref, grad_ref, shared_ref, ids_ref, weight_ref, gate_ref, packed_ref, tail_ref, term_ref):
-    tokens, features = norm_ref.shape
-    norm = norm_ref[...].astype(F32)
-    grad = grad_ref[...].astype(F32)
-    gate = gate_ref[...].astype(F32)
-    packed_ref[:, :features] = norm_ref[...]
-    packed_ref[:, features : 2 * features] = grad_ref[...]
+def in_hbm(value):
+    return pltpu.with_memory_space_constraint(value, pltpu.HBM)
+
+
+def pack_kernel(norm_ref, grad_ref, ids_ref, weight_ref, packed_ref, copied):
+    features = norm_ref.shape[1]
+    copies = [
+        pltpu.make_async_copy(ref, packed_ref.at[:, pl.ds(j * features, features)], copied.at[j])
+        for j, ref in enumerate((norm_ref, grad_ref))
+    ]
+    for copy in copies:
+        copy.start()
     lane = lax.broadcasted_iota(jnp.int32, (TOPK, LANES), 1)
     source = lax.broadcasted_iota(jnp.int32, (TOPK, LANES), 0)
     ids = ids_ref[...].astype(F32).astype(BF16)
-    codes = dot(ids, (lane == source).astype(BF16)) + dot(
-        weight_ref[...], (lane == source + TOPK).astype(BF16)
+    codes = dot(ids, (lane == source).astype(BF16), TN) + dot(
+        weight_ref[...], (lane == source + TOPK).astype(BF16), TN
     )
     packed_ref[:, 2 * features :] = codes.astype(BF16)
+    for copy in copies:
+        copy.wait()
+
+
+def pack(norm_input, out_grad, expert_ids, route_weight):
+    tokens, features = norm_input.shape
+    away = pl.BlockSpec(memory_space=pltpu.HBM)
+    near = pl.BlockSpec(memory_space=pltpu.VMEM)
+    return pl.pallas_call(
+        pack_kernel,
+        in_specs=[away, away, near, near],
+        out_specs=near,
+        out_shape=jax.ShapeDtypeStruct((tokens, 2 * features + LANES), BF16),
+        scratch_shapes=[pltpu.SemaphoreType.DMA((2,))],
+        compiler_params=pltpu.CompilerParams(vmem_limit_bytes=4 << 20),
+        name="pack",
+    )(*map(in_hbm, (norm_input, out_grad, expert_ids.T, route_weight.T)))
+
+
+def shared_kernel(norm_ref, grad_ref, shared_ref, gate_ref, tail_ref, term_ref, copied, norms, grads, outs):
+    features = norm_ref.shape[1]
+    copies = [
+        pltpu.make_async_copy(ref, target, copied.at[j])
+        for j, (ref, target) in enumerate(((norm_ref, norms), (grad_ref, grads), (shared_ref, outs)))
+    ]
+    for copy in copies:
+        copy.start()
+    for copy in copies:
+        copy.wait()
+    norm = norms[...].astype(F32)
+    gate = gate_ref[...].astype(F32)
     gate_value = jax.nn.sigmoid(jnp.sum(norm * gate, axis=1, keepdims=True))
-    inner = jnp.sum(grad * shared_ref[...].astype(F32), axis=1, keepdims=True)
+    inner = jnp.sum(grads[...].astype(F32) * outs[...].astype(F32), axis=1, keepdims=True)
     delta = inner * gate_value * (1.0 - gate_value)
     term_ref[...] = delta * gate
     local = jnp.sum(delta * norm, axis=0, keepdims=True)
@@ -298,18 +334,23 @@
         tail_ref[r : r + 1, :] = local[:, r * LANES : (r + 1) * LANES]
 
 
-def pack(norm_input, out_grad, shared_out, expert_ids, route_weight, shared_gate):
+def shared(norm_input, out_grad, shared_out, shared_gate):
     tokens, features = norm_input.shape
+    away = pl.BlockSpec(memory_space=pltpu.HBM)
+    near = pl.BlockSpec(memory_space=pltpu.VMEM)
     return pl.pallas_call(
-        pack_kernel,
+        shared_kernel,
+        in_specs=[away, away, away, near],
+        out_specs=[near, near],
         out_shape=[
-            jax.ShapeDtypeStruct((tokens, 2 * features + LANES), BF16),
             jax.ShapeDtypeStruct((tokens, LANES), F32),
             jax.ShapeDtypeStruct((tokens, features), F32),
         ],
+        scratch_shapes=[pltpu.SemaphoreType.DMA((3,))]
+        + [pltpu.VMEM((tokens, features), BF16)] * 3,
         compiler_params=pltpu.CompilerParams(vmem_limit_bytes=4 << 20),
-        name="pack",
-    )(norm_input, out_grad, shared_out, expert_ids, route_weight, shared_gate[None, :])
+        name="shared",
+    )(*map(in_hbm, (norm_input, out_grad, shared_out)), shared_gate[None, :])
 
 
 def finish_kernel(total_ref, *refs):
@@ -325,11 +366,11 @@
     token = lax.broadcasted_iota(jnp.int32, (tokens, LANES), 0)
     spread = jnp.where(lane // TOPK == token, final[line : line + 1, features:], 0.0)
     choose = (
-        lax.broadcasted_iota(jnp.int32, (LANES, TOPK), 0) % TOPK
-        == lax.broadcasted_iota(jnp.int32, (LANES, TOPK), 1)
+        lax.broadcasted_iota(jnp.int32, (TOPK, LANES), 1) % TOPK
+        == lax.broadcasted_iota(jnp.int32, (TOPK, LANES), 0)
     ).astype(F32)
-    route_ref[...] = jnp.dot(
-        spread, choose, precision=lax.Precision.HIGHEST, preferred_element_type=F32
+    route_ref[...] = lax.dot_general(
+        choose, spread, NT, precision=lax.Precision.HIGHEST, preferred_element_type=F32
     )
 
 
@@ -339,7 +380,7 @@
         finish_kernel,
         out_shape=[
             jax.ShapeDtypeStruct((tokens, features), BF16),
-            jax.ShapeDtypeStruct((tokens, TOPK), F32),
+            jax.ShapeDtypeStruct((TOPK, tokens), F32),
             jax.ShapeDtypeStruct((features // LANES, LANES), F32),
         ],
         compiler_params=pltpu.CompilerParams(vmem_limit_bytes=4 << 20),
@@ -352,15 +393,12 @@
 ):
     tokens, features = norm_input.shape
     sources = lax.axis_size("expert")
-    mine, tail, term = pack(
-        norm_input, out_grad, shared_out, expert_ids, route_weight, shared_gate
-    )
-    along = [mine] + [swap(mine, "expert", d) for d in range(1, sources)]
-    near, far = jnp.concatenate(along[:2], axis=0), jnp.concatenate(along[2:], axis=0)
-    near_x, far_x = swap(near, "dp", 2), swap(far, "dp", 2)
-    both = jnp.concatenate([near, far], axis=0)
-    held = [near, far, near_x, far_x]
-    held += [swap(block, "dp", 1) for block in (both, near_x, far_x)]
+    mine = pack(norm_input, out_grad, expert_ids, route_weight)
+    tail, term = shared(norm_input, out_grad, shared_out, shared_gate)
+    held = [mine] + [swap(mine, "expert", d) for d in range(1, sources)]
+    held[2], tail, term = lax.optimization_barrier((held[2], tail, term))
+    held = held + [swap(block, "dp", 2) for block in held]
+    held = held + [swap(block, "dp", 1) for block in held]
     kept, sent = run_experts(held, tail, w_gate, w_up, w_down, sources)
     total = (kept.astype(F32) + swap(sent, "dp", 1).astype(F32)).astype(BF16)
     half = total.shape[0] // 2
@@ -369,7 +407,7 @@
         swap(total[d * tokens : (d + 1) * tokens], "expert", d) for d in range(sources - 1, 0, -1)
     ]
     input_grad, route_grad, gate_grad = finish(total, parts, term)
-    return (input_grad, route_grad, gate_grad.reshape(features))
+    return (input_grad, route_grad.T, gate_grad.reshape(features))
 
 
 def solution(mesh):

time: 84.7 us -> 81.4 us (0.961)
  waiting for transfers between devices: 30.1 us -> 24.4 us
  local copies, waits for them, and re-layouts: 5.41 us -> 0.73 us
  starting transfers between devices: 15.7 us -> 19.8 us
  Pallas kernels: 32.2 us -> 35.3 us
    ppermute x13 -> x20, waiting for transfers between devices: 30.1 us -> 24.4 us  [swap(): return lax.ppermute(value, axis, [(i, i ^ distance) for i in range(size)])]
    unnamed x11 -> x0, local copies, waits for them, and re-layouts: 4.65 us -> none
    ppermute x13 -> x20, starting transfers between devices: 15.7 us -> 19.8 us  [swap(): return lax.ppermute(value, axis, [(i, i ^ distance) for i in range(size)])]
    pallas_call x1 -> x2, Pallas kernels: 0.14 us -> 2.6 us  [the longest x1 1.56 us: pack(): pl.pallas_call(pack_kernel, in_specs=[away, away, near, near], out_specs=...]
  transfers between devices with their start and end apart: 13 -> 20, of which waited for: 9 -> 10; matrix products, arithmetic and copies ran while one was open for 0% -> 1% of each run, Pallas kernels for 0% -> 1%
where the time goes in v4:
time: 81.4 us; the launch traced here: 81.1 us
  Pallas kernels  35.3 us (43%)
  waiting for transfers between devices  24.4 us (30%)
  starting transfers between devices  19.8 us (24%)
    pallas_call x1, Pallas kernels, run_experts(): pl.pallas_call(functools.partial(experts_kernel, features, rows, blocks,...  32 us
    ppermute x20, waiting for transfers between devices, swap(): return lax.ppermute(value, axis, [(i, i ^ distance) for i in range(size)])  24.4 us
    ppermute x20, starting transfers between devices, swap(): return lax.ppermute(value, axis, [(i, i ^ distance) for i in range(size)])  19.8 us
  transfers between devices with their start and end apart: 20, of which 10 were waited for; matrix products, arithmetic and copies ran while one was open for 1% of the time, Pallas kernels for 1%

profile of v4, /device:TPU:0, one launch (start us, length us, event | category | flops | bytes accessed | tf_op | source)
XLA Modules:
  0.0 81.1 jit_solution(15021295570071599759)
XLA Ops:
  0.6 1.6 %pack.1.refs_0_ = bf16[16,3712]{1,0:T(8,128)(2,1)S(1)} custom-call(bf16[16,1792]{1,0:T(8,128)(2,1)} %norm_ref.3, bf16[16,1792]{1,0:T(8,128)(2,1)} %grad_ref.3, s32[8,16]{1,0:T(8,128)} %bitcast.4, bf16[8,16]{1,0:T(8,128)(2,1)} %bitcast.5), custom_call_target="tpu_custom_call" | custom-call | tf_op jit(solution)/shard_map/pack/pallas_call | solution.py:304
  2.2 4.1 %collective-permute-start.1 = (bf16[16,3712]{1,0:T(8,128)(2,1)S(1)}, bf16[16,3712]{1,0:T(8,128)(2,1)S(1)}, u32[]{:S(2)}, u32[]{:S(2)}) collective-permute-start(bf16[16,3712]{1,0:T(8,128)(2,1)S(1)} %pack.1.refs_0_), channel_id=1, source_target_pairs={{0,8},{4,12},{8,0},{12,4},{1,9},{5,13},{9,1},{13,5},{2,10},{6,14},... | collective-permute-start | bytes 356360 | tf_op jit(solution)/shard_map/ppermute | solution.py:128
  6.3 1.5 %collective-permute-start.3 = (bf16[16,3712]{1,0:T(8,128)(2,1)S(1)}, bf16[16,3712]{1,0:T(8,128)(2,1)S(1)}, u32[]{:S(2)}, u32[]{:S(2)}) collective-permute-start(bf16[16,3712]{1,0:T(8,128)(2,1)S(1)} %pack.1.refs_0_), channel_id=1, source_target_pairs={{0,2},{1,3},{2,0},{3,1},{4,6},{5,7},{6,4},{7,5},{8,10},{9,11},{10,... | collective-permute-start | bytes 356360 | tf_op jit(solution)/shard_map/ppermute | solution.py:128
  7.8 1.3 %collective-permute-start.2 = (bf16[16,3712]{1,0:T(8,128)(2,1)S(1)}, bf16[16,3712]{1,0:T(8,128)(2,1)S(1)}, u32[]{:S(2)}, u32[]{:S(2)}) collective-permute-start(bf16[16,3712]{1,0:T(8,128)(2,1)S(1)} %pack.1.refs_0_), channel_id=1, source_target_pairs={{0,12},{4,8},{8,4},{12,0},{1,13},{5,9},{9,5},{13,1},{2,14},{6,10},... | collective-permute-start | bytes 356360 | tf_op jit(solution)/shard_map/ppermute | solution.py:128
  9.1 0.0 collective-permute-start.7
  9.1 0.2 collective-permute-start
  9.4 0.7 broadcast_in_dim.3.gate_ref
  10.1 1.0 %shared.1 = (f32[16,128]{1,0:T(8,128)S(1)}, f32[16,1792]{1,0:T(8,128)S(1)}) custom-call(bf16[16,1792]{1,0:T(8,128)(2,1)} %norm_ref.3, bf16[16,1792]{1,0:T(8,128)(2,1)} %grad_ref.3, bf16[16,1792]{1,0:T(8,128)(2,1)} %shared_ref.1, bf16[1,1792]{1,0:T(2,128)(2,1)S(1)} %broadcast_in_dim.3.gate_ref), custom_call_target="tpu_custom_call" | custom-call | tf_op jit(solution)/shard_map/shared/pallas_call | solution.py:341
  11.1 4.3 %collective-permute-done.1.refs_2_ = bf16[16,3712]{1,0:T(8,128)(2,1)S(1)} collective-permute-done((bf16[16,3712]{1,0:T(8,128)(2,1)S(1)}, bf16[16,3712]{1,0:T(8,128)(2,1)S(1)}, u32[]{:S(2)}, u32[]{:S(2)}) %collective-permute-start.1) | collective-permute-done | bytes 118816 | tf_op jit(solution)/shard_map/ppermute | solution.py:128
  15.4 0.1 collective-permute-done.2.refs_3_
  15.5 0.5 collective-permute-start.10
  15.9 1.9 %collective-permute-start.6 = (bf16[16,3712]{1,0:T(8,128)(2,1)S(1)}, bf16[16,3712]{1,0:T(8,128)(2,1)S(1)}, u32[]{:S(2)}, u32[]{:S(2)}) collective-permute-start(bf16[16,3712]{1,0:T(8,128)(2,1)S(1)} %collective-permute-done.2.refs_3_), channel_id=1, source_target_pairs={{0,2},{1,3},{2,0},{3,1},{4,6},{5,7},{6,4},{7,5},{8,10},{9,11},{10,... | collective-permute-start | bytes 356360 | tf_op jit(solution)/shard_map/ppermute | solution.py:128
  17.8 0.2 collective-permute-start.5
  18.0 1.9 %collective-permute-start.4 = (bf16[16,3712]{1,0:T(8,128)(2,1)S(1)}, bf16[16,3712]{1,0:T(8,128)(2,1)S(1)}, u32[]{:S(2)}, u32[]{:S(2)}) collective-permute-start(bf16[16,3712]{1,0:T(8,128)(2,1)S(1)} %collective-permute-done.refs_1_), channel_id=1, source_target_pairs={{0,2},{1,3},{2,0},{3,1},{4,6},{5,7},{6,4},{7,5},{8,10},{9,11},{10,... | collective-permute-start | bytes 356360 | tf_op jit(solution)/shard_map/ppermute | solution.py:128
  19.9 0.5 collective-permute-start.8
  20.4 1.6 %collective-permute-done.6.refs_7_ = bf16[16,3712]{1,0:T(8,128)(2,1)S(1)} collective-permute-done((bf16[16,3712]{1,0:T(8,128)(2,1)S(1)}, bf16[16,3712]{1,0:T(8,128)(2,1)S(1)}, u32[]{:S(2)}, u32[]{:S(2)}) %collective-permute-start.6) | collective-permute-done | bytes 118816 | tf_op jit(solution)/shard_map/ppermute | solution.py:128
  22.0 2.5 %collective-permute-done.5.refs_6_ = bf16[16,3712]{1,0:T(8,128)(2,1)S(1)} collective-permute-done((bf16[16,3712]{1,0:T(8,128)(2,1)S(1)}, bf16[16,3712]{1,0:T(8,128)(2,1)S(1)}, u32[]{:S(2)}, u32[]{:S(2)}) %collective-permute-start.5) | collective-permute-done | bytes 118816 | tf_op jit(solution)/shard_map/ppermute | solution.py:128
  24.6 1.8 %collective-permute-done.4.refs_5_ = bf16[16,3712]{1,0:T(8,128)(2,1)S(1)} collective-permute-done((bf16[16,3712]{1,0:T(8,128)(2,1)S(1)}, bf16[16,3712]{1,0:T(8,128)(2,1)S(1)}, u32[]{:S(2)}, u32[]{:S(2)}) %collective-permute-start.4) | collective-permute-done | bytes 118816 | tf_op jit(solution)/shard_map/ppermute | solution.py:128
  26.4 1.3 %collective-permute-done.12.refs_13_ = bf16[16,3712]{1,0:T(8,128)(2,1)S(1)} collective-permute-done((bf16[16,3712]{1,0:T(8,128)(2,1)S(1)}, bf16[16,3712]{1,0:T(8,128)(2,1)S(1)}, u32[]{:S(2)}, u32[]{:S(2)}) %collective-permute-start.12) | collective-permute-done | bytes 118816 | tf_op jit(solution)/shard_map/ppermute | solution.py:128
  27.7 32.0 %experts.1 = (bf16[128,1920]{1,0:T(8,128)(2,1)S(1)}, bf16[128,1920]{1,0:T(8,128)(2,1)S(1)}) custom-call(bf16[16,3712]{1,0:T(8,128)(2,1)S(1)} %pack.1.refs_0_, bf16[16,3712]{1,0:T(8,128)(2,1)S(1)} %collective-permute-done.refs_1_, bf16[16,3712]{1,0:T(8,128)(2,1)S(1)} %collective-permute-done.1.refs_2_, bf16[16,3712]{1,0:T(8,128)(2,1)S(1)} %collective-permute-done.2.refs_3_, ...), custom_call_target="tpu_custom_call" | custom-call | tf_op jit(solution)/shard_map/experts/pallas_call | solution.py:252
  59.7 0.2 collective-permute-start.15
  59.9 1.7 %collective-permute-done.15 = bf16[128,1920]{1,0:T(8,128)(2,1)S(1)} collective-permute-done((bf16[128,1920]{1,0:T(8,128)(2,1)S(1)}, bf16[128,1920]{1,0:T(8,128)(2,1)S(1)}, u32[]{:S(2)}, u32[]{:S(2)}) %collective-permute-start.15) | collective-permute-done | bytes 491552 | tf_op jit(solution)/shard_map/ppermute | solution.py:128
  61.6 0.1 add_convert_fusion
  61.7 1.8 %collective-permute-start.16 = (bf16[64,1920]{1,0:T(8,128)(2,1)S(1)}, bf16[64,1920]{1,0:T(8,128)(2,1)S(1)}, u32[]{:S(2)}, u32[]{:S(2)}) collective-permute-start(bf16[64,1920]{1,0:T(8,128)(2,1)S(1)} %slice.21), channel_id=1, source_target_pairs={{0,2},{1,3},{2,0},{3,1},{4,6},{5,7},{6,4},{7,5},{8,10},{9,11},{10,... | collective-permute-start | bytes 737288 | tf_op jit(solution)/shard_map/ppermute | solution.py:128
  63.6 6.3 %collective-permute-done.16 = bf16[64,1920]{1,0:T(8,128)(2,1)S(1)} collective-permute-done((bf16[64,1920]{1,0:T(8,128)(2,1)S(1)}, bf16[64,1920]{1,0:T(8,128)(2,1)S(1)}, u32[]{:S(2)}, u32[]{:S(2)}) %collective-permute-start.16) | collective-permute-done | bytes 245792 | tf_op jit(solution)/shard_map/ppermute | solution.py:128
  69.8 0.1 add_convert_fusion.1.total_ref
  69.9 2.4 %collective-permute-start.19 = (bf16[16,1920]{1,0:T(8,128)(2,1)S(1)}, bf16[16,1920]{1,0:T(8,128)(2,1)S(1)}, u32[]{:S(2)}, u32[]{:S(2)}) collective-permute-start(bf16[16,1920]{1,0:T(8,128)(2,1)S(1)} %get-tuple-element.23), channel_id=1, source_target_pairs={{0,4},{4,0},{8,12},{12,8},{1,5},{5,1},{9,13},{13,9},{2,6},{6,2},{1... | collective-permute-start | bytes 184328 | tf_op jit(solution)/shard_map/ppermute | solution.py:128
  72.3 2.0 %collective-permute-start.18 = (bf16[16,1920]{1,0:T(8,128)(2,1)S(1)}, bf16[16,1920]{1,0:T(8,128)(2,1)S(1)}, u32[]{:S(2)}, u32[]{:S(2)}) collective-permute-start(bf16[16,1920]{1,0:T(8,128)(2,1)S(1)} %get-tuple-element.24), channel_id=1, source_target_pairs={{0,8},{4,12},{8,0},{12,4},{1,9},{5,13},{9,1},{13,5},{2,10},{6,14},... | collective-permute-start | bytes 184328 | tf_op jit(solution)/shard_map/ppermute | solution.py:128
  74.3 1.4 %collective-permute-start.17 = (bf16[16,1920]{1,0:T(8,128)(2,1)S(1)}, bf16[16,1920]{1,0:T(8,128)(2,1)S(1)}, u32[]{:S(2)}, u32[]{:S(2)}) collective-permute-start(bf16[16,1920]{1,0:T(8,128)(2,1)S(1)} %get-tuple-element.25), channel_id=1, source_target_pairs={{0,12},{4,8},{8,4},{12,0},{1,13},{5,9},{9,5},{13,1},{2,14},{6,10},... | collective-permute-start | bytes 184328 | tf_op jit(solution)/shard_map/ppermute | solution.py:128
  75.7 3.7 %collective-permute-done.18.refs_1_ = bf16[16,1920]{1,0:T(8,128)(2,1)S(1)} collective-permute-done((bf16[16,1920]{1,0:T(8,128)(2,1)S(1)}, bf16[16,1920]{1,0:T(8,128)(2,1)S(1)}, u32[]{:S(2)}, u32[]{:S(2)}) %collective-permute-start.18) | collective-permute-done | bytes 61472 | tf_op jit(solution)/shard_map/ppermute | solution.py:128
  79.3 1.1 %collective-permute-done.17.refs_0_ = bf16[16,1920]{1,0:T(8,128)(2,1)S(1)} collective-permute-done((bf16[16,1920]{1,0:T(8,128)(2,1)S(1)}, bf16[16,1920]{1,0:T(8,128)(2,1)S(1)}, u32[]{:S(2)}, u32[]{:S(2)}) %collective-permute-start.17) | collective-permute-done | bytes 61472 | tf_op jit(solution)/shard_map/ppermute | solution.py:128
  80.4 0.7 finish.1
  (17 shorter events, 0.1 us)
Async XLA Ops:
  2.2 13.2 %collective-permute-start.1 = (bf16[16,3712]{1,0:T(8,128)(2,1)S(1)}, bf16[16,3712]{1,0:T(8,128)(2,1)S(1)}, u32[]{:S(2)}, u32[]{:S(2)}) collective-permute-start(bf16[16,3712]{1,0:T(8,128)(2,1)S(1)} %pack.1.refs_0_), channel_id=1, source_target_pairs={{0,8},{4,12},{8,0},{12,4},{1,9},{5,13},{9,1},{13,5},{2,10},{6,14},... | collective-permute-start | bytes 356360 | tf_op jit(solution)/shard_map/ppermute | solution.py:128
  6.3 9.1 %collective-permute-start.3 = (bf16[16,3712]{1,0:T(8,128)(2,1)S(1)}, bf16[16,3712]{1,0:T(8,128)(2,1)S(1)}, u32[]{:S(2)}, u32[]{:S(2)}) collective-permute-start(bf16[16,3712]{1,0:T(8,128)(2,1)S(1)} %pack.1.refs_0_), channel_id=1, source_target_pairs={{0,2},{1,3},{2,0},{3,1},{4,6},{5,7},{6,4},{7,5},{8,10},{9,11},{10,... | collective-permute-start | bytes 356360 | tf_op jit(solution)/shard_map/ppermute | solution.py:128
  7.8 7.7 %collective-permute-start.2 = (bf16[16,3712]{1,0:T(8,128)(2,1)S(1)}, bf16[16,3712]{1,0:T(8,128)(2,1)S(1)}, u32[]{:S(2)}, u32[]{:S(2)}) collective-permute-start(bf16[16,3712]{1,0:T(8,128)(2,1)S(1)} %pack.1.refs_0_), channel_id=1, source_target_pairs={{0,12},{4,8},{8,4},{12,0},{1,13},{5,9},{9,5},{13,1},{2,14},{6,10},... | collective-permute-start | bytes 356360 | tf_op jit(solution)/shard_map/ppermute | solution.py:128
  9.1 8.7 %collective-permute-start.7 = (bf16[16,3712]{1,0:T(8,128)(2,1)S(1)}, bf16[16,3712]{1,0:T(8,128)(2,1)S(1)}, u32[]{:S(2)}, u32[]{:S(2)}) collective-permute-start(bf16[16,3712]{1,0:T(8,128)(2,1)S(1)} %pack.1.refs_0_), channel_id=1, source_target_pairs={{0,1},{1,0},{2,3},{3,2},{4,5},{5,4},{6,7},{7,6},{8,9},{9,8},{10,11... | collective-permute-start | bytes 356360 | tf_op jit(solution)/shard_map/ppermute | solution.py:128
  9.1 8.8 %collective-permute-start = (bf16[16,3712]{1,0:T(8,128)(2,1)S(1)}, bf16[16,3712]{1,0:T(8,128)(2,1)S(1)}, u32[]{:S(2)}, u32[]{:S(2)}) collective-permute-start(bf16[16,3712]{1,0:T(8,128)(2,1)S(1)} %pack.1.refs_0_), channel_id=1, source_target_pairs={{0,4},{4,0},{8,12},{12,8},{1,5},{5,1},{9,13},{13,9},{2,6},{6,2},{1... | collective-permute-start | bytes 356360 | tf_op jit(solution)/shard_map/ppermute | solution.py:128
  15.4 4.4 %collective-permute-start.11 = (bf16[16,3712]{1,0:T(8,128)(2,1)S(1)}, bf16[16,3712]{1,0:T(8,128)(2,1)S(1)}, u32[]{:S(2)}, u32[]{:S(2)}) collective-permute-start(bf16[16,3712]{1,0:T(8,128)(2,1)S(1)} %collective-permute-done.3.refs_4_), channel_id=1, source_target_pairs={{0,1},{1,0},{2,3},{3,2},{4,5},{5,4},{6,7},{7,6},{8,9},{9,8},{10,11... | collective-permute-start | bytes 356360 | tf_op jit(solution)/shard_map/ppermute | solution.py:128
  15.5 4.4 %collective-permute-start.10 = (bf16[16,3712]{1,0:T(8,128)(2,1)S(1)}, bf16[16,3712]{1,0:T(8,128)(2,1)S(1)}, u32[]{:S(2)}, u32[]{:S(2)}) collective-permute-start(bf16[16,3712]{1,0:T(8,128)(2,1)S(1)} %collective-permute-done.2.refs_3_), channel_id=1, source_target_pairs={{0,1},{1,0},{2,3},{3,2},{4,5},{5,4},{6,7},{7,6},{8,9},{9,8},{10,11... | collective-permute-start | bytes 356360 | tf_op jit(solution)/shard_map/ppermute | solution.py:128
  15.9 6.1 %collective-permute-start.6 = (bf16[16,3712]{1,0:T(8,128)(2,1)S(1)}, bf16[16,3712]{1,0:T(8,128)(2,1)S(1)}, u32[]{:S(2)}, u32[]{:S(2)}) collective-permute-start(bf16[16,3712]{1,0:T(8,128)(2,1)S(1)} %collective-permute-done.2.refs_3_), channel_id=1, source_target_pairs={{0,2},{1,3},{2,0},{3,1},{4,6},{5,7},{6,4},{7,5},{8,10},{9,11},{10,... | collective-permute-start | bytes 356360 | tf_op jit(solution)/shard_map/ppermute | solution.py:128
  17.8 6.7 %collective-permute-start.5 = (bf16[16,3712]{1,0:T(8,128)(2,1)S(1)}, bf16[16,3712]{1,0:T(8,128)(2,1)S(1)}, u32[]{:S(2)}, u32[]{:S(2)}) collective-permute-start(bf16[16,3712]{1,0:T(8,128)(2,1)S(1)} %collective-permute-done.1.refs_2_), channel_id=1, source_target_pairs={{0,2},{1,3},{2,0},{3,1},{4,6},{5,7},{6,4},{7,5},{8,10},{9,11},{10,... | collective-permute-start | bytes 356360 | tf_op jit(solution)/shard_map/ppermute | solution.py:128
  18.0 8.4 %collective-permute-start.4 = (bf16[16,3712]{1,0:T(8,128)(2,1)S(1)}, bf16[16,3712]{1,0:T(8,128)(2,1)S(1)}, u32[]{:S(2)}, u32[]{:S(2)}) collective-permute-start(bf16[16,3712]{1,0:T(8,128)(2,1)S(1)} %collective-permute-done.refs_1_), channel_id=1, source_target_pairs={{0,2},{1,3},{2,0},{3,1},{4,6},{5,7},{6,4},{7,5},{8,10},{9,11},{10,... | collective-permute-start | bytes 356360 | tf_op jit(solution)/shard_map/ppermute | solution.py:128
  19.9 6.5 %collective-permute-start.9 = (bf16[16,3712]{1,0:T(8,128)(2,1)S(1)}, bf16[16,3712]{1,0:T(8,128)(2,1)S(1)}, u32[]{:S(2)}, u32[]{:S(2)}) collective-permute-start(bf16[16,3712]{1,0:T(8,128)(2,1)S(1)} %collective-permute-done.1.refs_2_), channel_id=1, source_target_pairs={{0,1},{1,0},{2,3},{3,2},{4,5},{5,4},{6,7},{7,6},{8,9},{9,8},{10,11... | collective-permute-start | bytes 356360 | tf_op jit(solution)/shard_map/ppermute | solution.py:128
  19.9 6.5 %collective-permute-start.8 = (bf16[16,3712]{1,0:T(8,128)(2,1)S(1)}, bf16[16,3712]{1,0:T(8,128)(2,1)S(1)}, u32[]{:S(2)}, u32[]{:S(2)}) collective-permute-start(bf16[16,3712]{1,0:T(8,128)(2,1)S(1)} %collective-permute-done.refs_1_), channel_id=1, source_target_pairs={{0,1},{1,0},{2,3},{3,2},{4,5},{5,4},{6,7},{7,6},{8,9},{9,8},{10,11... | collective-permute-start | bytes 356360 | tf_op jit(solution)/shard_map/ppermute | solution.py:128
  22.0 4.4 %collective-permute-start.14 = (bf16[16,3712]{1,0:T(8,128)(2,1)S(1)}, bf16[16,3712]{1,0:T(8,128)(2,1)S(1)}, u32[]{:S(2)}, u32[]{:S(2)}) collective-permute-start(bf16[16,3712]{1,0:T(8,128)(2,1)S(1)} %collective-permute-done.6.refs_7_), channel_id=1, source_target_pairs={{0,1},{1,0},{2,3},{3,2},{4,5},{5,4},{6,7},{7,6},{8,9},{9,8},{10,11... | collective-permute-start | bytes 356360 | tf_op jit(solution)/shard_map/ppermute | solution.py:128
  24.6 1.8 %collective-permute-start.13 = (bf16[16,3712]{1,0:T(8,128)(2,1)S(1)}, bf16[16,3712]{1,0:T(8,128)(2,1)S(1)}, u32[]{:S(2)}, u32[]{:S(2)}) collective-permute-start(bf16[16,3712]{1,0:T(8,128)(2,1)S(1)} %collective-permute-done.5.refs_6_), channel_id=1, source_target_pairs={{0,1},{1,0},{2,3},{3,2},{4,5},{5,4},{6,7},{7,6},{8,9},{9,8},{10,11... | collective-permute-start | bytes 356360 | tf_op jit(solution)/shard_map/ppermute | solution.py:128
  26.4 1.3 %collective-permute-start.12 = (bf16[16,3712]{1,0:T(8,128)(2,1)S(1)}, bf16[16,3712]{1,0:T(8,128)(2,1)S(1)}, u32[]{:S(2)}, u32[]{:S(2)}) collective-permute-start(bf16[16,3712]{1,0:T(8,128)(2,1)S(1)} %collective-permute-done.4.refs_5_), channel_id=1, source_target_pairs={{0,1},{1,0},{2,3},{3,2},{4,5},{5,4},{6,7},{7,6},{8,9},{9,8},{10,11... | collective-permute-start | bytes 356360 | tf_op jit(solution)/shard_map/ppermute | solution.py:128
  59.7 1.9 %collective-permute-start.15 = (bf16[128,1920]{1,0:T(8,128)(2,1)S(1)}, bf16[128,1920]{1,0:T(8,128)(2,1)S(1)}, u32[]{:S(2)}, u32[]{:S(2)}) collective-permute-start(bf16[128,1920]{1,0:T(8,128)(2,1)S(1)} %get-tuple-element.18), channel_id=1, source_target_pairs={{0,1},{1,0},{2,3},{3,2},{4,5},{5,4},{6,7},{7,6},{8,9},{9,8},{10,11... | collective-permute-start | bytes 1474568 | tf_op jit(solution)/shard_map/ppermute | solution.py:128
  61.7 8.1 %collective-permute-start.16 = (bf16[64,1920]{1,0:T(8,128)(2,1)S(1)}, bf16[64,1920]{1,0:T(8,128)(2,1)S(1)}, u32[]{:S(2)}, u32[]{:S(2)}) collective-permute-start(bf16[64,1920]{1,0:T(8,128)(2,1)S(1)} %slice.21), channel_id=1, source_target_pairs={{0,2},{1,3},{2,0},{3,1},{4,6},{5,7},{6,4},{7,5},{8,10},{9,11},{10,... | collective-permute-start | bytes 737288 | tf_op jit(solution)/shard_map/ppermute | solution.py:128
  69.9 5.8 %collective-permute-start.19 = (bf16[16,1920]{1,0:T(8,128)(2,1)S(1)}, bf16[16,1920]{1,0:T(8,128)(2,1)S(1)}, u32[]{:S(2)}, u32[]{:S(2)}) collective-permute-start(bf16[16,1920]{1,0:T(8,128)(2,1)S(1)} %get-tuple-element.23), channel_id=1, source_target_pairs={{0,4},{4,0},{8,12},{12,8},{1,5},{5,1},{9,13},{13,9},{2,6},{6,2},{1... | collective-permute-start | bytes 184328 | tf_op jit(solution)/shard_map/ppermute | solution.py:128
  72.3 7.1 %collective-permute-start.18 = (bf16[16,1920]{1,0:T(8,128)(2,1)S(1)}, bf16[16,1920]{1,0:T(8,128)(2,1)S(1)}, u32[]{:S(2)}, u32[]{:S(2)}) collective-permute-start(bf16[16,1920]{1,0:T(8,128)(2,1)S(1)} %get-tuple-element.24), channel_id=1, source_target_pairs={{0,8},{4,12},{8,0},{12,4},{1,9},{5,13},{9,1},{13,5},{2,10},{6,14},... | collective-permute-start | bytes 184328 | tf_op jit(solution)/shard_map/ppermute | solution.py:128
  74.3 6.1 %collective-permute-start.17 = (bf16[16,1920]{1,0:T(8,128)(2,1)S(1)}, bf16[16,1920]{1,0:T(8,128)(2,1)S(1)}, u32[]{:S(2)}, u32[]{:S(2)}) collective-permute-start(bf16[16,1920]{1,0:T(8,128)(2,1)S(1)} %get-tuple-element.25), channel_id=1, source_target_pairs={{0,12},{4,8},{8,4},{12,0},{1,13},{5,9},{9,5},{13,1},{2,14},{6,10},... | collective-permute-start | bytes 184328 | tf_op jit(solution)/shard_map/ppermute | solution.py:128

commit v5 on v4

--- a/solution.py
+++ b/solution.py
@@ -149,11 +149,11 @@
     ]
     for copy in copies:
         copy.start()
-    for copy in copies:
-        copy.wait()
     for k in range(group):
         for copy in loads(0, k):
             copy.start()
+    for copy in copies:
+        copy.wait()
     for k in range(group):
         for copy in loads(1, k):
             copy.start()
@@ -358,7 +358,7 @@
     tokens, features = term_ref.shape
     final = total_ref[:tokens].astype(F32)
     for part in parts:
-        final = final + part[...].astype(F32)
+        final = final + part[:tokens].astype(F32)
     input_ref[...] = (final[:, :features] + term_ref[...]).astype(BF16)
     line = features // LANES
     gate_ref[...] = final[:line, features:]
@@ -388,6 +388,10 @@
     )(total, *parts, term)
 
 
+def add(a, b):
+    return (a.astype(F32) + b.astype(F32)).astype(BF16)
+
+
 def square_device(
     norm_input, out_grad, shared_out, expert_ids, route_weight, shared_gate, w_gate, w_up, w_down
 ):
@@ -395,17 +399,25 @@
     sources = lax.axis_size("expert")
     mine = pack(norm_input, out_grad, expert_ids, route_weight)
     tail, term = shared(norm_input, out_grad, shared_out, shared_gate)
-    held = [mine] + [swap(mine, "expert", d) for d in range(1, sources)]
-    held[2], tail, term = lax.optimization_barrier((held[2], tail, term))
-    held = held + [swap(block, "dp", 2) for block in held]
+    x0 = swap(mine, "dp", 2)
+    z1 = swap(mine, "expert", 1)
+    z2 = swap(mine, "expert", 2)
+    z3 = swap(z2, "expert", 1)
+    z3, tail, term = lax.optimization_barrier((z3, tail, term))
+    xz1 = swap(z1, "dp", 2)
+    xz2 = swap(z2, "dp", 2)
+    xz3 = swap(xz2, "expert", 1)
+    held = [mine, z1, z2, z3, x0, xz1, xz2, xz3]
     held = held + [swap(block, "dp", 1) for block in held]
     kept, sent = run_experts(held, tail, w_gate, w_up, w_down, sources)
     total = (kept.astype(F32) + swap(sent, "dp", 1).astype(F32)).astype(BF16)
-    half = total.shape[0] // 2
-    total = (total[:half].astype(F32) + swap(total[half:], "dp", 2).astype(F32)).astype(BF16)
-    parts = [
-        swap(total[d * tokens : (d + 1) * tokens], "expert", d) for d in range(sources - 1, 0, -1)
-    ]
+    own = [total[j * tokens : (j + 1) * tokens] for j in range(2 * sources)]
+    far = swap(jnp.concatenate([own[3], own[7]], axis=0), "expert", 1)
+    near = swap(total[4 * tokens : 6 * tokens], "dp", 2)
+    third = swap(add(own[6], far[tokens:]), "dp", 2)
+    second = swap(add(own[1], near[tokens:]), "expert", 1)
+    fourth = swap(add(add(own[2], far[:tokens]), third), "expert", 2)
+    parts = [near, second, fourth]
     input_grad, route_grad, gate_grad = finish(total, parts, term)
     return (input_grad, route_grad.T, gate_grad.reshape(features))
 

time: 81.4 us -> 76.4 us (0.939)
  waiting for transfers between devices: 24.4 us -> 19.2 us
    ppermute x20 -> x21, waiting for transfers between devices: 24.4 us -> 19.2 us  [swap(): return lax.ppermute(value, axis, [(i, i ^ distance) for i in range(size)])]
    ppermute x20 -> x21, starting transfers between devices: 19.8 us -> 20 us  [swap(): return lax.ppermute(value, axis, [(i, i ^ distance) for i in range(size)])]
  transfers between devices with their start and end apart: 20 -> 21, of which waited for: 10 -> 10; matrix products, arithmetic and copies ran while one was open for 1% -> 1% of each run, Pallas kernels for 1% -> 1%
where the time goes in v5:
time: 76.4 us; the launch traced here: 76.1 us
  Pallas kernels  35.3 us (46%)
  starting transfers between devices  20 us (26%)
  waiting for transfers between devices  19.2 us (25%)
    pallas_call x1, Pallas kernels, run_experts(): pl.pallas_call(functools.partial(experts_kernel, features, rows, blocks,...  31.9 us
    ppermute x21, starting transfers between devices, swap(): return lax.ppermute(value, axis, [(i, i ^ distance) for i in range(size)])  20 us
    ppermute x21, waiting for transfers between devices, swap(): return lax.ppermute(value, axis, [(i, i ^ distance) for i in range(size)])  19.2 us
    pallas_call x1, Pallas kernels, pack(): pl.pallas_call(pack_kernel, in_specs=[away, away, near, near], out_specs=...  1.56 us
  transfers between devices with their start and end apart: 21, of which 10 were waited for; matrix products, arithmetic and copies ran while one was open for 1% of the time, Pallas kernels for 1%

profile of v5, /device:TPU:0, one launch (start us, length us, event | category | flops | bytes accessed | tf_op | source)
XLA Modules:
  0.0 76.1 jit_solution(16417039274852447595)
XLA Ops:
  0.6 1.6 %pack.1.refs_0_ = bf16[16,3712]{1,0:T(8,128)(2,1)S(1)} custom-call(bf16[16,1792]{1,0:T(8,128)(2,1)} %norm_ref.3, bf16[16,1792]{1,0:T(8,128)(2,1)} %grad_ref.3, s32[8,16]{1,0:T(8,128)} %bitcast.4, bf16[8,16]{1,0:T(8,128)(2,1)} %bitcast.5), custom_call_target="tpu_custom_call" | custom-call | tf_op jit(solution)/shard_map/pack/pallas_call | solution.py:304
  2.2 4.1 %collective-permute-start.1 = (bf16[16,3712]{1,0:T(8,128)(2,1)S(1)}, bf16[16,3712]{1,0:T(8,128)(2,1)S(1)}, u32[]{:S(2)}, u32[]{:S(2)}) collective-permute-start(bf16[16,3712]{1,0:T(8,128)(2,1)S(1)} %pack.1.refs_0_), channel_id=1, source_target_pairs={{0,8},{4,12},{8,0},{12,4},{1,9},{5,13},{9,1},{13,5},{2,10},{6,14},... | collective-permute-start | bytes 356360 | tf_op jit(solution)/shard_map/ppermute | solution.py:128
  6.3 1.5 %collective-permute-start.3 = (bf16[16,3712]{1,0:T(8,128)(2,1)S(1)}, bf16[16,3712]{1,0:T(8,128)(2,1)S(1)}, u32[]{:S(2)}, u32[]{:S(2)}) collective-permute-start(bf16[16,3712]{1,0:T(8,128)(2,1)S(1)} %pack.1.refs_0_), channel_id=1, source_target_pairs={{0,2},{1,3},{2,0},{3,1},{4,6},{5,7},{6,4},{7,5},{8,10},{9,11},{10,... | collective-permute-start | bytes 356360 | tf_op jit(solution)/shard_map/ppermute | solution.py:128
  7.8 1.6 %collective-permute-start = (bf16[16,3712]{1,0:T(8,128)(2,1)S(1)}, bf16[16,3712]{1,0:T(8,128)(2,1)S(1)}, u32[]{:S(2)}, u32[]{:S(2)}) collective-permute-start(bf16[16,3712]{1,0:T(8,128)(2,1)S(1)} %pack.1.refs_0_), channel_id=1, source_target_pairs={{0,4},{4,0},{8,12},{12,8},{1,5},{5,1},{9,13},{13,9},{2,6},{6,2},{1... | collective-permute-start | bytes 356360 | tf_op jit(solution)/shard_map/ppermute | solution.py:128
  9.4 2.8 %collective-permute-done.1.refs_2_ = bf16[16,3712]{1,0:T(8,128)(2,1)S(1)} collective-permute-done((bf16[16,3712]{1,0:T(8,128)(2,1)S(1)}, bf16[16,3712]{1,0:T(8,128)(2,1)S(1)}, u32[]{:S(2)}, u32[]{:S(2)}) %collective-permute-start.1) | collective-permute-done | bytes 118816 | tf_op jit(solution)/shard_map/ppermute | solution.py:128
  12.2 1.5 %collective-permute-start.5 = (bf16[16,3712]{1,0:T(8,128)(2,1)S(1)}, bf16[16,3712]{1,0:T(8,128)(2,1)S(1)}, u32[]{:S(2)}, u32[]{:S(2)}) collective-permute-start(bf16[16,3712]{1,0:T(8,128)(2,1)S(1)} %collective-permute-done.1.refs_2_), channel_id=1, source_target_pairs={{0,2},{1,3},{2,0},{3,1},{4,6},{5,7},{6,4},{7,5},{8,10},{9,11},{10,... | collective-permute-start | bytes 356360 | tf_op jit(solution)/shard_map/ppermute | solution.py:128
  13.7 0.6 collective-permute-start.2
  14.3 0.5 collective-permute-start.11
  14.9 2.1 %collective-permute-done.5.refs_6_ = bf16[16,3712]{1,0:T(8,128)(2,1)S(1)} collective-permute-done((bf16[16,3712]{1,0:T(8,128)(2,1)S(1)}, bf16[16,3712]{1,0:T(8,128)(2,1)S(1)}, u32[]{:S(2)}, u32[]{:S(2)}) %collective-permute-start.5) | collective-permute-done | bytes 118816 | tf_op jit(solution)/shard_map/ppermute | solution.py:128
  17.0 1.6 %collective-permute-start.4 = (bf16[16,3712]{1,0:T(8,128)(2,1)S(1)}, bf16[16,3712]{1,0:T(8,128)(2,1)S(1)}, u32[]{:S(2)}, u32[]{:S(2)}) collective-permute-start(bf16[16,3712]{1,0:T(8,128)(2,1)S(1)} %collective-permute-done.refs_1_), channel_id=1, source_target_pairs={{0,2},{1,3},{2,0},{3,1},{4,6},{5,7},{6,4},{7,5},{8,10},{9,11},{10,... | collective-permute-start | bytes 356360 | tf_op jit(solution)/shard_map/ppermute | solution.py:128
  18.6 0.9 %collective-permute-start.6 = (bf16[16,3712]{1,0:T(8,128)(2,1)S(1)}, bf16[16,3712]{1,0:T(8,128)(2,1)S(1)}, u32[]{:S(2)}, u32[]{:S(2)}) collective-permute-start(bf16[16,3712]{1,0:T(8,128)(2,1)S(1)} %collective-permute-done.5.refs_6_), channel_id=1, source_target_pairs={{0,4},{4,0},{8,12},{12,8},{1,5},{5,1},{9,13},{13,9},{2,6},{6,2},{1... | collective-permute-start | bytes 356360 | tf_op jit(solution)/shard_map/ppermute | solution.py:128
  19.5 0.7 broadcast_in_dim.3.gate_ref
  20.2 1.0 %shared.1 = (f32[16,128]{1,0:T(8,128)S(1)}, f32[16,1792]{1,0:T(8,128)S(1)}) custom-call(bf16[16,1792]{1,0:T(8,128)(2,1)} %norm_ref.3, bf16[16,1792]{1,0:T(8,128)(2,1)} %grad_ref.3, bf16[16,1792]{1,0:T(8,128)(2,1)} %shared_ref.1, bf16[1,1792]{1,0:T(2,128)(2,1)S(1)} %broadcast_in_dim.3.gate_ref), custom_call_target="tpu_custom_call" | custom-call | tf_op jit(solution)/shard_map/shared/pallas_call | solution.py:341
  21.3 0.5 collective-permute-start.10
  21.9 0.4 collective-permute-start.12
  22.3 1.1 %collective-permute-done.6.refs_7_ = bf16[16,3712]{1,0:T(8,128)(2,1)S(1)} collective-permute-done((bf16[16,3712]{1,0:T(8,128)(2,1)S(1)}, bf16[16,3712]{1,0:T(8,128)(2,1)S(1)}, u32[]{:S(2)}, u32[]{:S(2)}) %collective-permute-start.6) | collective-permute-done | bytes 118816 | tf_op jit(solution)/shard_map/ppermute | solution.py:128
  23.5 1.3 %collective-permute-done.14.refs_15_ = bf16[16,3712]{1,0:T(8,128)(2,1)S(1)} collective-permute-done((bf16[16,3712]{1,0:T(8,128)(2,1)S(1)}, bf16[16,3712]{1,0:T(8,128)(2,1)S(1)}, u32[]{:S(2)}, u32[]{:S(2)}) %collective-permute-start.14) | collective-permute-done | bytes 118816 | tf_op jit(solution)/shard_map/ppermute | solution.py:128
  24.8 31.9 %experts.1 = (bf16[128,1920]{1,0:T(8,128)(2,1)S(1)}, bf16[128,1920]{1,0:T(8,128)(2,1)S(1)}) custom-call(bf16[16,3712]{1,0:T(8,128)(2,1)S(1)} %pack.1.refs_0_, bf16[16,3712]{1,0:T(8,128)(2,1)S(1)} %collective-permute-done.refs_1_, bf16[16,3712]{1,0:T(8,128)(2,1)S(1)} %collective-permute-done.1.refs_2_, bf16[16,3712]{1,0:T(8,128)(2,1)S(1)} %collective-permute-done.2.refs_3_, ...), custom_call_target="tpu_custom_call" | custom-call | tf_op jit(solution)/shard_map/experts/pallas_call | solution.py:252
  56.7 0.2 collective-permute-start.15
  56.9 1.7 %collective-permute-done.15 = bf16[128,1920]{1,0:T(8,128)(2,1)S(1)} collective-permute-done((bf16[128,1920]{1,0:T(8,128)(2,1)S(1)}, bf16[128,1920]{1,0:T(8,128)(2,1)S(1)}, u32[]{:S(2)}, u32[]{:S(2)}) %collective-permute-start.15) | collective-permute-done | bytes 491552 | tf_op jit(solution)/shard_map/ppermute | solution.py:128
  58.6 0.1 add_convert_fusion.total_ref
  58.8 0.9 %collective-permute-start.18 = (bf16[32,1920]{1,0:T(8,128)(2,1)S(1)}, bf16[32,1920]{1,0:T(8,128)(2,1)S(1)}, u32[]{:S(2)}, u32[]{:S(2)}) collective-permute-start(bf16[32,1920]{1,0:T(8,128)(2,1)S(1)} %pad_maximum_fusion), channel_id=1, source_target_pairs={{0,4},{4,0},{8,12},{12,8},{1,5},{5,1},{9,13},{13,9},{2,6},{6,2},{1... | collective-permute-start | bytes 368648 | tf_op jit(solution)/shard_map/ppermute | solution.py:128
  59.7 0.7 collective-permute-start.16
  60.4 3.8 %collective-permute-done.18 = bf16[32,1920]{1,0:T(8,128)(2,1)S(1)} collective-permute-done((bf16[32,1920]{1,0:T(8,128)(2,1)S(1)}, bf16[32,1920]{1,0:T(8,128)(2,1)S(1)}, u32[]{:S(2)}, u32[]{:S(2)}) %collective-permute-start.18) | collective-permute-done | bytes 122912 | tf_op jit(solution)/shard_map/ppermute | solution.py:128
  64.3 0.5 collective-permute-start.19
  64.8 0.1 collective-permute-done.16.refs_0_
  64.9 3.7 %collective-permute-done.19 = bf16[16,1920]{1,0:T(8,128)(2,1)S(1)} collective-permute-done((bf16[16,1920]{1,0:T(8,128)(2,1)S(1)}, bf16[16,1920]{1,0:T(8,128)(2,1)S(1)}, u32[]{:S(2)}, u32[]{:S(2)}) %collective-permute-start.19) | collective-permute-done | bytes 61472 | tf_op jit(solution)/shard_map/ppermute | solution.py:128
  68.6 2.6 %collective-permute-start.20 = (bf16[16,1920]{1,0:T(8,128)(2,1)S(1)}, bf16[16,1920]{1,0:T(8,128)(2,1)S(1)}, u32[]{:S(2)}, u32[]{:S(2)}) collective-permute-start(bf16[16,1920]{1,0:T(8,128)(2,1)S(1)} %get-tuple-element.23), channel_id=1, source_target_pairs={{0,8},{4,12},{8,0},{12,4},{1,9},{5,13},{9,1},{13,5},{2,10},{6,14},... | collective-permute-start | bytes 184328 | tf_op jit(solution)/shard_map/ppermute | solution.py:128
  71.2 1.7 %collective-permute-start.17 = (bf16[16,1920]{1,0:T(8,128)(2,1)S(1)}, bf16[16,1920]{1,0:T(8,128)(2,1)S(1)}, u32[]{:S(2)}, u32[]{:S(2)}) collective-permute-start(bf16[16,1920]{1,0:T(8,128)(2,1)S(1)} %get-tuple-element.24), channel_id=1, source_target_pairs={{0,4},{4,0},{8,12},{12,8},{1,5},{5,1},{9,13},{13,9},{2,6},{6,2},{1... | collective-permute-start | bytes 184328 | tf_op jit(solution)/shard_map/ppermute | solution.py:128
  72.9 0.9 %collective-permute-done.20.refs_2_ = bf16[16,1920]{1,0:T(8,128)(2,1)S(1)} collective-permute-done((bf16[16,1920]{1,0:T(8,128)(2,1)S(1)}, bf16[16,1920]{1,0:T(8,128)(2,1)S(1)}, u32[]{:S(2)}, u32[]{:S(2)}) %collective-permute-start.20) | collective-permute-done | bytes 61472 | tf_op jit(solution)/shard_map/ppermute | solution.py:128
  73.8 1.6 %collective-permute-done.17.refs_1_ = bf16[16,1920]{1,0:T(8,128)(2,1)S(1)} collective-permute-done((bf16[16,1920]{1,0:T(8,128)(2,1)S(1)}, bf16[16,1920]{1,0:T(8,128)(2,1)S(1)}, u32[]{:S(2)}, u32[]{:S(2)}) %collective-permute-start.17) | collective-permute-done | bytes 61472 | tf_op jit(solution)/shard_map/ppermute | solution.py:128
  75.4 0.7 finish.1
  (21 shorter events, 0.4 us)
Async XLA Ops:
  2.2 10.0 %collective-permute-start.1 = (bf16[16,3712]{1,0:T(8,128)(2,1)S(1)}, bf16[16,3712]{1,0:T(8,128)(2,1)S(1)}, u32[]{:S(2)}, u32[]{:S(2)}) collective-permute-start(bf16[16,3712]{1,0:T(8,128)(2,1)S(1)} %pack.1.refs_0_), channel_id=1, source_target_pairs={{0,8},{4,12},{8,0},{12,4},{1,9},{5,13},{9,1},{13,5},{2,10},{6,14},... | collective-permute-start | bytes 356360 | tf_op jit(solution)/shard_map/ppermute | solution.py:128
  6.3 8.0 %collective-permute-start.3 = (bf16[16,3712]{1,0:T(8,128)(2,1)S(1)}, bf16[16,3712]{1,0:T(8,128)(2,1)S(1)}, u32[]{:S(2)}, u32[]{:S(2)}) collective-permute-start(bf16[16,3712]{1,0:T(8,128)(2,1)S(1)} %pack.1.refs_0_), channel_id=1, source_target_pairs={{0,2},{1,3},{2,0},{3,1},{4,6},{5,7},{6,4},{7,5},{8,10},{9,11},{10,... | collective-permute-start | bytes 356360 | tf_op jit(solution)/shard_map/ppermute | solution.py:128
  7.8 7.0 %collective-permute-start = (bf16[16,3712]{1,0:T(8,128)(2,1)S(1)}, bf16[16,3712]{1,0:T(8,128)(2,1)S(1)}, u32[]{:S(2)}, u32[]{:S(2)}) collective-permute-start(bf16[16,3712]{1,0:T(8,128)(2,1)S(1)} %pack.1.refs_0_), channel_id=1, source_target_pairs={{0,4},{4,0},{8,12},{12,8},{1,5},{5,1},{9,13},{13,9},{2,6},{6,2},{1... | collective-permute-start | bytes 356360 | tf_op jit(solution)/shard_map/ppermute | solution.py:128
  12.2 4.8 %collective-permute-start.5 = (bf16[16,3712]{1,0:T(8,128)(2,1)S(1)}, bf16[16,3712]{1,0:T(8,128)(2,1)S(1)}, u32[]{:S(2)}, u32[]{:S(2)}) collective-permute-start(bf16[16,3712]{1,0:T(8,128)(2,1)S(1)} %collective-permute-done.1.refs_2_), channel_id=1, source_target_pairs={{0,2},{1,3},{2,0},{3,1},{4,6},{5,7},{6,4},{7,5},{8,10},{9,11},{10,... | collective-permute-start | bytes 356360 | tf_op jit(solution)/shard_map/ppermute | solution.py:128
  13.7 4.9 %collective-permute-start.2 = (bf16[16,3712]{1,0:T(8,128)(2,1)S(1)}, bf16[16,3712]{1,0:T(8,128)(2,1)S(1)}, u32[]{:S(2)}, u32[]{:S(2)}) collective-permute-start(bf16[16,3712]{1,0:T(8,128)(2,1)S(1)} %collective-permute-done.1.refs_2_), channel_id=1, source_target_pairs={{0,4},{4,0},{8,12},{12,8},{1,5},{5,1},{9,13},{13,9},{2,6},{6,2},{1... | collective-permute-start | bytes 356360 | tf_op jit(solution)/shard_map/ppermute | solution.py:128
  14.3 6.9 %collective-permute-start.7 = (bf16[16,3712]{1,0:T(8,128)(2,1)S(1)}, bf16[16,3712]{1,0:T(8,128)(2,1)S(1)}, u32[]{:S(2)}, u32[]{:S(2)}) collective-permute-start(bf16[16,3712]{1,0:T(8,128)(2,1)S(1)} %pack.1.refs_0_), channel_id=1, source_target_pairs={{0,1},{1,0},{2,3},{3,2},{4,5},{5,4},{6,7},{7,6},{8,9},{9,8},{10,11... | collective-permute-start | bytes 356360 | tf_op jit(solution)/shard_map/ppermute | solution.py:128
  14.3 7.0 %collective-permute-start.11 = (bf16[16,3712]{1,0:T(8,128)(2,1)S(1)}, bf16[16,3712]{1,0:T(8,128)(2,1)S(1)}, u32[]{:S(2)}, u32[]{:S(2)}) collective-permute-start(bf16[16,3712]{1,0:T(8,128)(2,1)S(1)} %collective-permute-done.3.refs_4_), channel_id=1, source_target_pairs={{0,1},{1,0},{2,3},{3,2},{4,5},{5,4},{6,7},{7,6},{8,9},{9,8},{10,11... | collective-permute-start | bytes 356360 | tf_op jit(solution)/shard_map/ppermute | solution.py:128
  14.8 7.0 %collective-permute-start.9 = (bf16[16,3712]{1,0:T(8,128)(2,1)S(1)}, bf16[16,3712]{1,0:T(8,128)(2,1)S(1)}, u32[]{:S(2)}, u32[]{:S(2)}) collective-permute-start(bf16[16,3712]{1,0:T(8,128)(2,1)S(1)} %collective-permute-done.1.refs_2_), channel_id=1, source_target_pairs={{0,1},{1,0},{2,3},{3,2},{4,5},{5,4},{6,7},{7,6},{8,9},{9,8},{10,11... | collective-permute-start | bytes 356360 | tf_op jit(solution)/shard_map/ppermute | solution.py:128
  17.0 4.8 %collective-permute-start.4 = (bf16[16,3712]{1,0:T(8,128)(2,1)S(1)}, bf16[16,3712]{1,0:T(8,128)(2,1)S(1)}, u32[]{:S(2)}, u32[]{:S(2)}) collective-permute-start(bf16[16,3712]{1,0:T(8,128)(2,1)S(1)} %collective-permute-done.refs_1_), channel_id=1, source_target_pairs={{0,2},{1,3},{2,0},{3,1},{4,6},{5,7},{6,4},{7,5},{8,10},{9,11},{10,... | collective-permute-start | bytes 356360 | tf_op jit(solution)/shard_map/ppermute | solution.py:128
  18.6 4.8 %collective-permute-start.6 = (bf16[16,3712]{1,0:T(8,128)(2,1)S(1)}, bf16[16,3712]{1,0:T(8,128)(2,1)S(1)}, u32[]{:S(2)}, u32[]{:S(2)}) collective-permute-start(bf16[16,3712]{1,0:T(8,128)(2,1)S(1)} %collective-permute-done.5.refs_6_), channel_id=1, source_target_pairs={{0,4},{4,0},{8,12},{12,8},{1,5},{5,1},{9,13},{13,9},{2,6},{6,2},{1... | collective-permute-start | bytes 356360 | tf_op jit(solution)/shard_map/ppermute | solution.py:128
  21.2 2.2 %collective-permute-start.8 = (bf16[16,3712]{1,0:T(8,128)(2,1)S(1)}, bf16[16,3712]{1,0:T(8,128)(2,1)S(1)}, u32[]{:S(2)}, u32[]{:S(2)}) collective-permute-start(bf16[16,3712]{1,0:T(8,128)(2,1)S(1)} %collective-permute-done.refs_1_), channel_id=1, source_target_pairs={{0,1},{1,0},{2,3},{3,2},{4,5},{5,4},{6,7},{7,6},{8,9},{9,8},{10,11... | collective-permute-start | bytes 356360 | tf_op jit(solution)/shard_map/ppermute | solution.py:128
  21.3 2.2 %collective-permute-start.10 = (bf16[16,3712]{1,0:T(8,128)(2,1)S(1)}, bf16[16,3712]{1,0:T(8,128)(2,1)S(1)}, u32[]{:S(2)}, u32[]{:S(2)}) collective-permute-start(bf16[16,3712]{1,0:T(8,128)(2,1)S(1)} %collective-permute-done.2.refs_3_), channel_id=1, source_target_pairs={{0,1},{1,0},{2,3},{3,2},{4,5},{5,4},{6,7},{7,6},{8,9},{9,8},{10,11... | collective-permute-start | bytes 356360 | tf_op jit(solution)/shard_map/ppermute | solution.py:128
  21.8 1.7 %collective-permute-start.13 = (bf16[16,3712]{1,0:T(8,128)(2,1)S(1)}, bf16[16,3712]{1,0:T(8,128)(2,1)S(1)}, u32[]{:S(2)}, u32[]{:S(2)}) collective-permute-start(bf16[16,3712]{1,0:T(8,128)(2,1)S(1)} %collective-permute-done.5.refs_6_), channel_id=1, source_target_pairs={{0,1},{1,0},{2,3},{3,2},{4,5},{5,4},{6,7},{7,6},{8,9},{9,8},{10,11... | collective-permute-start | bytes 356360 | tf_op jit(solution)/shard_map/ppermute | solution.py:128
  21.9 1.6 %collective-permute-start.12 = (bf16[16,3712]{1,0:T(8,128)(2,1)S(1)}, bf16[16,3712]{1,0:T(8,128)(2,1)S(1)}, u32[]{:S(2)}, u32[]{:S(2)}) collective-permute-start(bf16[16,3712]{1,0:T(8,128)(2,1)S(1)} %collective-permute-done.4.refs_5_), channel_id=1, source_target_pairs={{0,1},{1,0},{2,3},{3,2},{4,5},{5,4},{6,7},{7,6},{8,9},{9,8},{10,11... | collective-permute-start | bytes 356360 | tf_op jit(solution)/shard_map/ppermute | solution.py:128
  23.4 1.3 %collective-permute-start.14 = (bf16[16,3712]{1,0:T(8,128)(2,1)S(1)}, bf16[16,3712]{1,0:T(8,128)(2,1)S(1)}, u32[]{:S(2)}, u32[]{:S(2)}) collective-permute-start(bf16[16,3712]{1,0:T(8,128)(2,1)S(1)} %collective-permute-done.6.refs_7_), channel_id=1, source_target_pairs={{0,1},{1,0},{2,3},{3,2},{4,5},{5,4},{6,7},{7,6},{8,9},{9,8},{10,11... | collective-permute-start | bytes 356360 | tf_op jit(solution)/shard_map/ppermute | solution.py:128
  56.7 1.9 %collective-permute-start.15 = (bf16[128,1920]{1,0:T(8,128)(2,1)S(1)}, bf16[128,1920]{1,0:T(8,128)(2,1)S(1)}, u32[]{:S(2)}, u32[]{:S(2)}) collective-permute-start(bf16[128,1920]{1,0:T(8,128)(2,1)S(1)} %get-tuple-element.18), channel_id=1, source_target_pairs={{0,1},{1,0},{2,3},{3,2},{4,5},{5,4},{6,7},{7,6},{8,9},{9,8},{10,11... | collective-permute-start | bytes 1474568 | tf_op jit(solution)/shard_map/ppermute | solution.py:128
  58.8 5.4 %collective-permute-start.18 = (bf16[32,1920]{1,0:T(8,128)(2,1)S(1)}, bf16[32,1920]{1,0:T(8,128)(2,1)S(1)}, u32[]{:S(2)}, u32[]{:S(2)}) collective-permute-start(bf16[32,1920]{1,0:T(8,128)(2,1)S(1)} %pad_maximum_fusion), channel_id=1, source_target_pairs={{0,4},{4,0},{8,12},{12,8},{1,5},{5,1},{9,13},{13,9},{2,6},{6,2},{1... | collective-permute-start | bytes 368648 | tf_op jit(solution)/shard_map/ppermute | solution.py:128
  59.7 5.2 %collective-permute-start.16 = (bf16[32,1920]{1,0:T(8,128)(2,1)S(1)}, bf16[32,1920]{1,0:T(8,128)(2,1)S(1)}, u32[]{:S(2)}, u32[]{:S(2)}) collective-permute-start(bf16[32,1920]{1,0:T(8,128)(2,1)S(1)} %slice.36), channel_id=1, source_target_pairs={{0,2},{1,3},{2,0},{3,1},{4,6},{5,7},{6,4},{7,5},{8,10},{9,11},{10,... | collective-permute-start | bytes 368648 | tf_op jit(solution)/shard_map/ppermute | solution.py:128
  64.3 4.3 %collective-permute-start.19 = (bf16[16,1920]{1,0:T(8,128)(2,1)S(1)}, bf16[16,1920]{1,0:T(8,128)(2,1)S(1)}, u32[]{:S(2)}, u32[]{:S(2)}) collective-permute-start(bf16[16,1920]{1,0:T(8,128)(2,1)S(1)} %add_convert_fusion.2), channel_id=1, source_target_pairs={{0,2},{1,3},{2,0},{3,1},{4,6},{5,7},{6,4},{7,5},{8,10},{9,11},{10,... | collective-permute-start | bytes 184328 | tf_op jit(solution)/shard_map/ppermute | solution.py:128
  68.6 5.2 %collective-permute-start.20 = (bf16[16,1920]{1,0:T(8,128)(2,1)S(1)}, bf16[16,1920]{1,0:T(8,128)(2,1)S(1)}, u32[]{:S(2)}, u32[]{:S(2)}) collective-permute-start(bf16[16,1920]{1,0:T(8,128)(2,1)S(1)} %get-tuple-element.23), channel_id=1, source_target_pairs={{0,8},{4,12},{8,0},{12,4},{1,9},{5,13},{9,1},{13,5},{2,10},{6,14},... | collective-permute-start | bytes 184328 | tf_op jit(solution)/shard_map/ppermute | solution.py:128
  71.2 4.2 %collective-permute-start.17 = (bf16[16,1920]{1,0:T(8,128)(2,1)S(1)}, bf16[16,1920]{1,0:T(8,128)(2,1)S(1)}, u32[]{:S(2)}, u32[]{:S(2)}) collective-permute-start(bf16[16,1920]{1,0:T(8,128)(2,1)S(1)} %get-tuple-element.24), channel_id=1, source_target_pairs={{0,4},{4,0},{8,12},{12,8},{1,5},{5,1},{9,13},{13,9},{2,6},{6,2},{1... | collective-permute-start | bytes 184328 | tf_op jit(solution)/shard_map/ppermute | solution.py:128

commit v6 on v5

--- a/solution.py
+++ b/solution.py
@@ -130,7 +130,7 @@
 
 def experts_kernel(features, rows, blocks, group, *refs):
     token_refs, refs = refs[:blocks], refs[blocks:]
-    tail_ref, w_gate, w_up, w_down, keep_ref, send_ref, tokens, copied, gates, ups, downs, loaded, spread, weighted, norms, grads, backs, hits, routes = refs
+    tail_ref, w_gate, w_up, w_down, keep_ref, send_ref, gates, ups, downs, loaded, spread, weighted, norms, grads, backs, hits, routes = refs
     number = w_gate.shape[0]
     starts = np.cumsum([0] + [ref.shape[0] for ref in token_refs])
     count = int(starts[-1])
@@ -143,21 +143,13 @@
             for j, (source, target) in enumerate(((w_gate, gates), (w_up, ups), (w_down, downs)))
         ]
 
-    copies = [
-        pltpu.make_async_copy(ref, tokens.at[pl.ds(int(starts[j]), ref.shape[0])], copied.at[j])
-        for j, ref in enumerate(token_refs)
-    ]
-    for copy in copies:
-        copy.start()
     for k in range(group):
         for copy in loads(0, k):
             copy.start()
-    for copy in copies:
-        copy.wait()
-    for k in range(group):
-        for copy in loads(1, k):
-            copy.start()
-    codes = tokens[:, 2 * features :].astype(F32).T
+    def together(columns):
+        return jnp.concatenate([ref[:, columns] for ref in token_refs], axis=0)
+
+    codes = together(slice(2 * features, None)).astype(F32).T
     weights = codes[TOPK : 2 * TOPK]
     local = codes[:TOPK] - (lax.axis_index("expert") * number).astype(F32)
     hits[...] = local
@@ -176,8 +168,11 @@
         chosen = (slot == position[e : e + 1]) & (member[e : e + 1] > 0.0)
         spread[e * rows : (e + 1) * rows] = jnp.where(chosen, 1.0, 0.0).astype(BF16)
         weighted[e * rows : (e + 1) * rows] = jnp.where(chosen, weight, 0.0).astype(BF16)
-    norms[...] = dot(spread[...], tokens[:, :features]).astype(BF16)
-    grads[...] = dot(spread[...], tokens[:, features : 2 * features]).astype(BF16)
+    for k in range(group):
+        for copy in loads(1, k):
+            copy.start()
+    norms[...] = dot(spread[...], together(slice(0, features))).astype(BF16)
+    grads[...] = dot(spread[...], together(slice(features, 2 * features))).astype(BF16)
     routes[...] = jnp.zeros_like(routes)
 
     def run(turn, _):
@@ -251,12 +246,10 @@
     near = pl.BlockSpec(memory_space=pltpu.VMEM)
     return pl.pallas_call(
         functools.partial(experts_kernel, features, rows, blocks, group),
-        in_specs=[away] * blocks + [near, away, away, away],
+        in_specs=[near] * (blocks + 1) + [away] * 3,
         out_specs=[near] * 2,
         out_shape=[jax.ShapeDtypeStruct((count // 2, width), BF16)] * 2,
         scratch_shapes=[
-            pltpu.VMEM((count, 2 * features + LANES), BF16),
-            pltpu.SemaphoreType.DMA((blocks,)),
             pltpu.VMEM((3 * group, features, hidden), BF16),
             pltpu.VMEM((3 * group, features, hidden), BF16),
             pltpu.VMEM((3 * group, hidden, features), BF16),

time: 76.4 us -> 75.3 us (0.986)
  Pallas kernels: 35.3 us -> 34.1 us
    pallas_call x1, Pallas kernels: 31.9 us -> 30.8 us  [run_experts(): pl.pallas_call(functools.partial(experts_kernel, features, rows, blocks,...]
where the time goes in v6:
time: 75.3 us; the launch traced here: 75 us
  Pallas kernels  34.1 us (45%)
  starting transfers between devices  20 us (27%)
  waiting for transfers between devices  19.2 us (25%)
    pallas_call x1, Pallas kernels, run_experts(): pl.pallas_call(functools.partial(experts_kernel, features, rows, blocks,...  30.8 us
    ppermute x21, starting transfers between devices, swap(): return lax.ppermute(value, axis, [(i, i ^ distance) for i in range(size)])  20 us
    ppermute x21, waiting for transfers between devices, swap(): return lax.ppermute(value, axis, [(i, i ^ distance) for i in range(size)])  19.2 us
    pallas_call x1, Pallas kernels, pack(): pl.pallas_call(pack_kernel, in_specs=[away, away, near, near], out_specs=...  1.56 us
  transfers between devices with their start and end apart: 21, of which 10 were waited for; matrix products, arithmetic and copies ran while one was open for 1% of the time, Pallas kernels for 1%

profile of v6, /device:TPU:0, one launch (start us, length us, event | category | flops | bytes accessed | tf_op | source)
XLA Modules:
  0.0 75.0 jit_solution(16087000476458833002)
XLA Ops:
  0.6 1.6 %pack.1.refs_0_ = bf16[16,3712]{1,0:T(8,128)(2,1)S(1)} custom-call(bf16[16,1792]{1,0:T(8,128)(2,1)} %norm_ref.3, bf16[16,1792]{1,0:T(8,128)(2,1)} %grad_ref.3, s32[8,16]{1,0:T(8,128)} %bitcast.4, bf16[8,16]{1,0:T(8,128)(2,1)} %bitcast.5), custom_call_target="tpu_custom_call" | custom-call | tf_op jit(solution)/shard_map/pack/pallas_call | solution.py:297
  2.2 4.1 %collective-permute-start.1 = (bf16[16,3712]{1,0:T(8,128)(2,1)S(1)}, bf16[16,3712]{1,0:T(8,128)(2,1)S(1)}, u32[]{:S(2)}, u32[]{:S(2)}) collective-permute-start(bf16[16,3712]{1,0:T(8,128)(2,1)S(1)} %pack.1.refs_0_), channel_id=1, source_target_pairs={{0,8},{4,12},{8,0},{12,4},{1,9},{5,13},{9,1},{13,5},{2,10},{6,14},... | collective-permute-start | bytes 356360 | tf_op jit(solution)/shard_map/ppermute | solution.py:128
  6.3 1.5 %collective-permute-start.3 = (bf16[16,3712]{1,0:T(8,128)(2,1)S(1)}, bf16[16,3712]{1,0:T(8,128)(2,1)S(1)}, u32[]{:S(2)}, u32[]{:S(2)}) collective-permute-start(bf16[16,3712]{1,0:T(8,128)(2,1)S(1)} %pack.1.refs_0_), channel_id=1, source_target_pairs={{0,2},{1,3},{2,0},{3,1},{4,6},{5,7},{6,4},{7,5},{8,10},{9,11},{10,... | collective-permute-start | bytes 356360 | tf_op jit(solution)/shard_map/ppermute | solution.py:128
  7.8 1.6 %collective-permute-start = (bf16[16,3712]{1,0:T(8,128)(2,1)S(1)}, bf16[16,3712]{1,0:T(8,128)(2,1)S(1)}, u32[]{:S(2)}, u32[]{:S(2)}) collective-permute-start(bf16[16,3712]{1,0:T(8,128)(2,1)S(1)} %pack.1.refs_0_), channel_id=1, source_target_pairs={{0,4},{4,0},{8,12},{12,8},{1,5},{5,1},{9,13},{13,9},{2,6},{6,2},{1... | collective-permute-start | bytes 356360 | tf_op jit(solution)/shard_map/ppermute | solution.py:128
  9.4 2.8 %collective-permute-done.1.refs_2_ = bf16[16,3712]{1,0:T(8,128)(2,1)S(1)} collective-permute-done((bf16[16,3712]{1,0:T(8,128)(2,1)S(1)}, bf16[16,3712]{1,0:T(8,128)(2,1)S(1)}, u32[]{:S(2)}, u32[]{:S(2)}) %collective-permute-start.1) | collective-permute-done | bytes 118816 | tf_op jit(solution)/shard_map/ppermute | solution.py:128
  12.2 1.5 %collective-permute-start.5 = (bf16[16,3712]{1,0:T(8,128)(2,1)S(1)}, bf16[16,3712]{1,0:T(8,128)(2,1)S(1)}, u32[]{:S(2)}, u32[]{:S(2)}) collective-permute-start(bf16[16,3712]{1,0:T(8,128)(2,1)S(1)} %collective-permute-done.1.refs_2_), channel_id=1, source_target_pairs={{0,2},{1,3},{2,0},{3,1},{4,6},{5,7},{6,4},{7,5},{8,10},{9,11},{10,... | collective-permute-start | bytes 356360 | tf_op jit(solution)/shard_map/ppermute | solution.py:128
  13.7 0.6 collective-permute-start.2
  14.3 0.5 collective-permute-start.11
  14.9 2.1 %collective-permute-done.5.refs_6_ = bf16[16,3712]{1,0:T(8,128)(2,1)S(1)} collective-permute-done((bf16[16,3712]{1,0:T(8,128)(2,1)S(1)}, bf16[16,3712]{1,0:T(8,128)(2,1)S(1)}, u32[]{:S(2)}, u32[]{:S(2)}) %collective-permute-start.5) | collective-permute-done | bytes 118816 | tf_op jit(solution)/shard_map/ppermute | solution.py:128
  17.0 1.6 %collective-permute-start.4 = (bf16[16,3712]{1,0:T(8,128)(2,1)S(1)}, bf16[16,3712]{1,0:T(8,128)(2,1)S(1)}, u32[]{:S(2)}, u32[]{:S(2)}) collective-permute-start(bf16[16,3712]{1,0:T(8,128)(2,1)S(1)} %collective-permute-done.refs_1_), channel_id=1, source_target_pairs={{0,2},{1,3},{2,0},{3,1},{4,6},{5,7},{6,4},{7,5},{8,10},{9,11},{10,... | collective-permute-start | bytes 356360 | tf_op jit(solution)/shard_map/ppermute | solution.py:128
  18.6 0.9 %collective-permute-start.6 = (bf16[16,3712]{1,0:T(8,128)(2,1)S(1)}, bf16[16,3712]{1,0:T(8,128)(2,1)S(1)}, u32[]{:S(2)}, u32[]{:S(2)}) collective-permute-start(bf16[16,3712]{1,0:T(8,128)(2,1)S(1)} %collective-permute-done.5.refs_6_), channel_id=1, source_target_pairs={{0,4},{4,0},{8,12},{12,8},{1,5},{5,1},{9,13},{13,9},{2,6},{6,2},{1... | collective-permute-start | bytes 356360 | tf_op jit(solution)/shard_map/ppermute | solution.py:128
  19.5 0.7 broadcast_in_dim.3.gate_ref
  20.2 1.0 %shared.1 = (f32[16,128]{1,0:T(8,128)S(1)}, f32[16,1792]{1,0:T(8,128)S(1)}) custom-call(bf16[16,1792]{1,0:T(8,128)(2,1)} %norm_ref.3, bf16[16,1792]{1,0:T(8,128)(2,1)} %grad_ref.3, bf16[16,1792]{1,0:T(8,128)(2,1)} %shared_ref.1, bf16[1,1792]{1,0:T(2,128)(2,1)S(1)} %broadcast_in_dim.3.gate_ref), custom_call_target="tpu_custom_call" | custom-call | tf_op jit(solution)/shard_map/shared/pallas_call | solution.py:334
  21.3 0.5 collective-permute-start.10
  21.9 0.4 collective-permute-start.12
  22.3 1.1 %collective-permute-done.6.refs_7_ = bf16[16,3712]{1,0:T(8,128)(2,1)S(1)} collective-permute-done((bf16[16,3712]{1,0:T(8,128)(2,1)S(1)}, bf16[16,3712]{1,0:T(8,128)(2,1)S(1)}, u32[]{:S(2)}, u32[]{:S(2)}) %collective-permute-start.6) | collective-permute-done | bytes 118816 | tf_op jit(solution)/shard_map/ppermute | solution.py:128
  23.5 1.3 %collective-permute-done.14.refs_15_ = bf16[16,3712]{1,0:T(8,128)(2,1)S(1)} collective-permute-done((bf16[16,3712]{1,0:T(8,128)(2,1)S(1)}, bf16[16,3712]{1,0:T(8,128)(2,1)S(1)}, u32[]{:S(2)}, u32[]{:S(2)}) %collective-permute-start.14) | collective-permute-done | bytes 118816 | tf_op jit(solution)/shard_map/ppermute | solution.py:128
  24.8 30.8 %experts.1 = (bf16[128,1920]{1,0:T(8,128)(2,1)S(1)}, bf16[128,1920]{1,0:T(8,128)(2,1)S(1)}) custom-call(bf16[16,3712]{1,0:T(8,128)(2,1)S(1)} %pack.1.refs_0_, bf16[16,3712]{1,0:T(8,128)(2,1)S(1)} %collective-permute-done.refs_1_, bf16[16,3712]{1,0:T(8,128)(2,1)S(1)} %collective-permute-done.1.refs_2_, bf16[16,3712]{1,0:T(8,128)(2,1)S(1)} %collective-permute-done.2.refs_3_, ...), custom_call_target="tpu_custom_call" | custom-call | tf_op jit(solution)/shard_map/experts/pallas_call | solution.py:247
  55.5 0.2 collective-permute-start.15
  55.8 1.7 %collective-permute-done.15 = bf16[128,1920]{1,0:T(8,128)(2,1)S(1)} collective-permute-done((bf16[128,1920]{1,0:T(8,128)(2,1)S(1)}, bf16[128,1920]{1,0:T(8,128)(2,1)S(1)}, u32[]{:S(2)}, u32[]{:S(2)}) %collective-permute-start.15) | collective-permute-done | bytes 491552 | tf_op jit(solution)/shard_map/ppermute | solution.py:128
  57.5 0.1 add_convert_fusion.total_ref
  57.6 0.9 %collective-permute-start.18 = (bf16[32,1920]{1,0:T(8,128)(2,1)S(1)}, bf16[32,1920]{1,0:T(8,128)(2,1)S(1)}, u32[]{:S(2)}, u32[]{:S(2)}) collective-permute-start(bf16[32,1920]{1,0:T(8,128)(2,1)S(1)} %pad_maximum_fusion), channel_id=1, source_target_pairs={{0,4},{4,0},{8,12},{12,8},{1,5},{5,1},{9,13},{13,9},{2,6},{6,2},{1... | collective-permute-start | bytes 368648 | tf_op jit(solution)/shard_map/ppermute | solution.py:128
  58.6 0.6 collective-permute-start.16
  59.2 3.9 %collective-permute-done.18 = bf16[32,1920]{1,0:T(8,128)(2,1)S(1)} collective-permute-done((bf16[32,1920]{1,0:T(8,128)(2,1)S(1)}, bf16[32,1920]{1,0:T(8,128)(2,1)S(1)}, u32[]{:S(2)}, u32[]{:S(2)}) %collective-permute-start.18) | collective-permute-done | bytes 122912 | tf_op jit(solution)/shard_map/ppermute | solution.py:128
  63.1 0.5 collective-permute-start.19
  63.6 0.1 collective-permute-done.16.refs_0_
  63.7 3.7 %collective-permute-done.19 = bf16[16,1920]{1,0:T(8,128)(2,1)S(1)} collective-permute-done((bf16[16,1920]{1,0:T(8,128)(2,1)S(1)}, bf16[16,1920]{1,0:T(8,128)(2,1)S(1)}, u32[]{:S(2)}, u32[]{:S(2)}) %collective-permute-start.19) | collective-permute-done | bytes 61472 | tf_op jit(solution)/shard_map/ppermute | solution.py:128
  67.4 2.6 %collective-permute-start.20 = (bf16[16,1920]{1,0:T(8,128)(2,1)S(1)}, bf16[16,1920]{1,0:T(8,128)(2,1)S(1)}, u32[]{:S(2)}, u32[]{:S(2)}) collective-permute-start(bf16[16,1920]{1,0:T(8,128)(2,1)S(1)} %get-tuple-element.23), channel_id=1, source_target_pairs={{0,8},{4,12},{8,0},{12,4},{1,9},{5,13},{9,1},{13,5},{2,10},{6,14},... | collective-permute-start | bytes 184328 | tf_op jit(solution)/shard_map/ppermute | solution.py:128
  70.0 1.7 %collective-permute-start.17 = (bf16[16,1920]{1,0:T(8,128)(2,1)S(1)}, bf16[16,1920]{1,0:T(8,128)(2,1)S(1)}, u32[]{:S(2)}, u32[]{:S(2)}) collective-permute-start(bf16[16,1920]{1,0:T(8,128)(2,1)S(1)} %get-tuple-element.24), channel_id=1, source_target_pairs={{0,4},{4,0},{8,12},{12,8},{1,5},{5,1},{9,13},{13,9},{2,6},{6,2},{1... | collective-permute-start | bytes 184328 | tf_op jit(solution)/shard_map/ppermute | solution.py:128
  71.7 0.9 %collective-permute-done.20.refs_2_ = bf16[16,1920]{1,0:T(8,128)(2,1)S(1)} collective-permute-done((bf16[16,1920]{1,0:T(8,128)(2,1)S(1)}, bf16[16,1920]{1,0:T(8,128)(2,1)S(1)}, u32[]{:S(2)}, u32[]{:S(2)}) %collective-permute-start.20) | collective-permute-done | bytes 61472 | tf_op jit(solution)/shard_map/ppermute | solution.py:128
  72.6 1.6 %collective-permute-done.17.refs_1_ = bf16[16,1920]{1,0:T(8,128)(2,1)S(1)} collective-permute-done((bf16[16,1920]{1,0:T(8,128)(2,1)S(1)}, bf16[16,1920]{1,0:T(8,128)(2,1)S(1)}, u32[]{:S(2)}, u32[]{:S(2)}) %collective-permute-start.17) | collective-permute-done | bytes 61472 | tf_op jit(solution)/shard_map/ppermute | solution.py:128
  74.2 0.7 finish.1
  (21 shorter events, 0.4 us)
Async XLA Ops:
  2.2 10.0 %collective-permute-start.1 = (bf16[16,3712]{1,0:T(8,128)(2,1)S(1)}, bf16[16,3712]{1,0:T(8,128)(2,1)S(1)}, u32[]{:S(2)}, u32[]{:S(2)}) collective-permute-start(bf16[16,3712]{1,0:T(8,128)(2,1)S(1)} %pack.1.refs_0_), channel_id=1, source_target_pairs={{0,8},{4,12},{8,0},{12,4},{1,9},{5,13},{9,1},{13,5},{2,10},{6,14},... | collective-permute-start | bytes 356360 | tf_op jit(solution)/shard_map/ppermute | solution.py:128
  6.3 8.0 %collective-permute-start.3 = (bf16[16,3712]{1,0:T(8,128)(2,1)S(1)}, bf16[16,3712]{1,0:T(8,128)(2,1)S(1)}, u32[]{:S(2)}, u32[]{:S(2)}) collective-permute-start(bf16[16,3712]{1,0:T(8,128)(2,1)S(1)} %pack.1.refs_0_), channel_id=1, source_target_pairs={{0,2},{1,3},{2,0},{3,1},{4,6},{5,7},{6,4},{7,5},{8,10},{9,11},{10,... | collective-permute-start | bytes 356360 | tf_op jit(solution)/shard_map/ppermute | solution.py:128
  7.8 7.0 %collective-permute-start = (bf16[16,3712]{1,0:T(8,128)(2,1)S(1)}, bf16[16,3712]{1,0:T(8,128)(2,1)S(1)}, u32[]{:S(2)}, u32[]{:S(2)}) collective-permute-start(bf16[16,3712]{1,0:T(8,128)(2,1)S(1)} %pack.1.refs_0_), channel_id=1, source_target_pairs={{0,4},{4,0},{8,12},{12,8},{1,5},{5,1},{9,13},{13,9},{2,6},{6,2},{1... | collective-permute-start | bytes 356360 | tf_op jit(solution)/shard_map/ppermute | solution.py:128
  12.2 4.8 %collective-permute-start.5 = (bf16[16,3712]{1,0:T(8,128)(2,1)S(1)}, bf16[16,3712]{1,0:T(8,128)(2,1)S(1)}, u32[]{:S(2)}, u32[]{:S(2)}) collective-permute-start(bf16[16,3712]{1,0:T(8,128)(2,1)S(1)} %collective-permute-done.1.refs_2_), channel_id=1, source_target_pairs={{0,2},{1,3},{2,0},{3,1},{4,6},{5,7},{6,4},{7,5},{8,10},{9,11},{10,... | collective-permute-start | bytes 356360 | tf_op jit(solution)/shard_map/ppermute | solution.py:128
  13.7 4.9 %collective-permute-start.2 = (bf16[16,3712]{1,0:T(8,128)(2,1)S(1)}, bf16[16,3712]{1,0:T(8,128)(2,1)S(1)}, u32[]{:S(2)}, u32[]{:S(2)}) collective-permute-start(bf16[16,3712]{1,0:T(8,128)(2,1)S(1)} %collective-permute-done.1.refs_2_), channel_id=1, source_target_pairs={{0,4},{4,0},{8,12},{12,8},{1,5},{5,1},{9,13},{13,9},{2,6},{6,2},{1... | collective-permute-start | bytes 356360 | tf_op jit(solution)/shard_map/ppermute | solution.py:128
  14.3 6.9 %collective-permute-start.7 = (bf16[16,3712]{1,0:T(8,128)(2,1)S(1)}, bf16[16,3712]{1,0:T(8,128)(2,1)S(1)}, u32[]{:S(2)}, u32[]{:S(2)}) collective-permute-start(bf16[16,3712]{1,0:T(8,128)(2,1)S(1)} %pack.1.refs_0_), channel_id=1, source_target_pairs={{0,1},{1,0},{2,3},{3,2},{4,5},{5,4},{6,7},{7,6},{8,9},{9,8},{10,11... | collective-permute-start | bytes 356360 | tf_op jit(solution)/shard_map/ppermute | solution.py:128
  14.3 7.0 %collective-permute-start.11 = (bf16[16,3712]{1,0:T(8,128)(2,1)S(1)}, bf16[16,3712]{1,0:T(8,128)(2,1)S(1)}, u32[]{:S(2)}, u32[]{:S(2)}) collective-permute-start(bf16[16,3712]{1,0:T(8,128)(2,1)S(1)} %collective-permute-done.3.refs_4_), channel_id=1, source_target_pairs={{0,1},{1,0},{2,3},{3,2},{4,5},{5,4},{6,7},{7,6},{8,9},{9,8},{10,11... | collective-permute-start | bytes 356360 | tf_op jit(solution)/shard_map/ppermute | solution.py:128
  14.8 7.0 %collective-permute-start.9 = (bf16[16,3712]{1,0:T(8,128)(2,1)S(1)}, bf16[16,3712]{1,0:T(8,128)(2,1)S(1)}, u32[]{:S(2)}, u32[]{:S(2)}) collective-permute-start(bf16[16,3712]{1,0:T(8,128)(2,1)S(1)} %collective-permute-done.1.refs_2_), channel_id=1, source_target_pairs={{0,1},{1,0},{2,3},{3,2},{4,5},{5,4},{6,7},{7,6},{8,9},{9,8},{10,11... | collective-permute-start | bytes 356360 | tf_op jit(solution)/shard_map/ppermute | solution.py:128
  17.0 4.8 %collective-permute-start.4 = (bf16[16,3712]{1,0:T(8,128)(2,1)S(1)}, bf16[16,3712]{1,0:T(8,128)(2,1)S(1)}, u32[]{:S(2)}, u32[]{:S(2)}) collective-permute-start(bf16[16,3712]{1,0:T(8,128)(2,1)S(1)} %collective-permute-done.refs_1_), channel_id=1, source_target_pairs={{0,2},{1,3},{2,0},{3,1},{4,6},{5,7},{6,4},{7,5},{8,10},{9,11},{10,... | collective-permute-start | bytes 356360 | tf_op jit(solution)/shard_map/ppermute | solution.py:128
  18.6 4.8 %collective-permute-start.6 = (bf16[16,3712]{1,0:T(8,128)(2,1)S(1)}, bf16[16,3712]{1,0:T(8,128)(2,1)S(1)}, u32[]{:S(2)}, u32[]{:S(2)}) collective-permute-start(bf16[16,3712]{1,0:T(8,128)(2,1)S(1)} %collective-permute-done.5.refs_6_), channel_id=1, source_target_pairs={{0,4},{4,0},{8,12},{12,8},{1,5},{5,1},{9,13},{13,9},{2,6},{6,2},{1... | collective-permute-start | bytes 356360 | tf_op jit(solution)/shard_map/ppermute | solution.py:128
  21.2 2.2 %collective-permute-start.8 = (bf16[16,3712]{1,0:T(8,128)(2,1)S(1)}, bf16[16,3712]{1,0:T(8,128)(2,1)S(1)}, u32[]{:S(2)}, u32[]{:S(2)}) collective-permute-start(bf16[16,3712]{1,0:T(8,128)(2,1)S(1)} %collective-permute-done.refs_1_), channel_id=1, source_target_pairs={{0,1},{1,0},{2,3},{3,2},{4,5},{5,4},{6,7},{7,6},{8,9},{9,8},{10,11... | collective-permute-start | bytes 356360 | tf_op jit(solution)/shard_map/ppermute | solution.py:128
  21.3 2.2 %collective-permute-start.10 = (bf16[16,3712]{1,0:T(8,128)(2,1)S(1)}, bf16[16,3712]{1,0:T(8,128)(2,1)S(1)}, u32[]{:S(2)}, u32[]{:S(2)}) collective-permute-start(bf16[16,3712]{1,0:T(8,128)(2,1)S(1)} %collective-permute-done.2.refs_3_), channel_id=1, source_target_pairs={{0,1},{1,0},{2,3},{3,2},{4,5},{5,4},{6,7},{7,6},{8,9},{9,8},{10,11... | collective-permute-start | bytes 356360 | tf_op jit(solution)/shard_map/ppermute | solution.py:128
  21.8 1.7 %collective-permute-start.13 = (bf16[16,3712]{1,0:T(8,128)(2,1)S(1)}, bf16[16,3712]{1,0:T(8,128)(2,1)S(1)}, u32[]{:S(2)}, u32[]{:S(2)}) collective-permute-start(bf16[16,3712]{1,0:T(8,128)(2,1)S(1)} %collective-permute-done.5.refs_6_), channel_id=1, source_target_pairs={{0,1},{1,0},{2,3},{3,2},{4,5},{5,4},{6,7},{7,6},{8,9},{9,8},{10,11... | collective-permute-start | bytes 356360 | tf_op jit(solution)/shard_map/ppermute | solution.py:128
  21.9 1.6 %collective-permute-start.12 = (bf16[16,3712]{1,0:T(8,128)(2,1)S(1)}, bf16[16,3712]{1,0:T(8,128)(2,1)S(1)}, u32[]{:S(2)}, u32[]{:S(2)}) collective-permute-start(bf16[16,3712]{1,0:T(8,128)(2,1)S(1)} %collective-permute-done.4.refs_5_), channel_id=1, source_target_pairs={{0,1},{1,0},{2,3},{3,2},{4,5},{5,4},{6,7},{7,6},{8,9},{9,8},{10,11... | collective-permute-start | bytes 356360 | tf_op jit(solution)/shard_map/ppermute | solution.py:128
  23.4 1.3 %collective-permute-start.14 = (bf16[16,3712]{1,0:T(8,128)(2,1)S(1)}, bf16[16,3712]{1,0:T(8,128)(2,1)S(1)}, u32[]{:S(2)}, u32[]{:S(2)}) collective-permute-start(bf16[16,3712]{1,0:T(8,128)(2,1)S(1)} %collective-permute-done.6.refs_7_), channel_id=1, source_target_pairs={{0,1},{1,0},{2,3},{3,2},{4,5},{5,4},{6,7},{7,6},{8,9},{9,8},{10,11... | collective-permute-start | bytes 356360 | tf_op jit(solution)/shard_map/ppermute | solution.py:128
  55.5 1.9 %collective-permute-start.15 = (bf16[128,1920]{1,0:T(8,128)(2,1)S(1)}, bf16[128,1920]{1,0:T(8,128)(2,1)S(1)}, u32[]{:S(2)}, u32[]{:S(2)}) collective-permute-start(bf16[128,1920]{1,0:T(8,128)(2,1)S(1)} %get-tuple-element.18), channel_id=1, source_target_pairs={{0,1},{1,0},{2,3},{3,2},{4,5},{5,4},{6,7},{7,6},{8,9},{9,8},{10,11... | collective-permute-start | bytes 1474568 | tf_op jit(solution)/shard_map/ppermute | solution.py:128
  57.6 5.4 %collective-permute-start.18 = (bf16[32,1920]{1,0:T(8,128)(2,1)S(1)}, bf16[32,1920]{1,0:T(8,128)(2,1)S(1)}, u32[]{:S(2)}, u32[]{:S(2)}) collective-permute-start(bf16[32,1920]{1,0:T(8,128)(2,1)S(1)} %pad_maximum_fusion), channel_id=1, source_target_pairs={{0,4},{4,0},{8,12},{12,8},{1,5},{5,1},{9,13},{13,9},{2,6},{6,2},{1... | collective-permute-start | bytes 368648 | tf_op jit(solution)/shard_map/ppermute | solution.py:128
  58.6 5.2 %collective-permute-start.16 = (bf16[32,1920]{1,0:T(8,128)(2,1)S(1)}, bf16[32,1920]{1,0:T(8,128)(2,1)S(1)}, u32[]{:S(2)}, u32[]{:S(2)}) collective-permute-start(bf16[32,1920]{1,0:T(8,128)(2,1)S(1)} %slice.36), channel_id=1, source_target_pairs={{0,2},{1,3},{2,0},{3,1},{4,6},{5,7},{6,4},{7,5},{8,10},{9,11},{10,... | collective-permute-start | bytes 368648 | tf_op jit(solution)/shard_map/ppermute | solution.py:128
  63.1 4.3 %collective-permute-start.19 = (bf16[16,1920]{1,0:T(8,128)(2,1)S(1)}, bf16[16,1920]{1,0:T(8,128)(2,1)S(1)}, u32[]{:S(2)}, u32[]{:S(2)}) collective-permute-start(bf16[16,1920]{1,0:T(8,128)(2,1)S(1)} %add_convert_fusion.2), channel_id=1, source_target_pairs={{0,2},{1,3},{2,0},{3,1},{4,6},{5,7},{6,4},{7,5},{8,10},{9,11},{10,... | collective-permute-start | bytes 184328 | tf_op jit(solution)/shard_map/ppermute | solution.py:128
  67.4 5.2 %collective-permute-start.20 = (bf16[16,1920]{1,0:T(8,128)(2,1)S(1)}, bf16[16,1920]{1,0:T(8,128)(2,1)S(1)}, u32[]{:S(2)}, u32[]{:S(2)}) collective-permute-start(bf16[16,1920]{1,0:T(8,128)(2,1)S(1)} %get-tuple-element.23), channel_id=1, source_target_pairs={{0,8},{4,12},{8,0},{12,4},{1,9},{5,13},{9,1},{13,5},{2,10},{6,14},... | collective-permute-start | bytes 184328 | tf_op jit(solution)/shard_map/ppermute | solution.py:128
  70.0 4.2 %collective-permute-start.17 = (bf16[16,1920]{1,0:T(8,128)(2,1)S(1)}, bf16[16,1920]{1,0:T(8,128)(2,1)S(1)}, u32[]{:S(2)}, u32[]{:S(2)}) collective-permute-start(bf16[16,1920]{1,0:T(8,128)(2,1)S(1)} %get-tuple-element.24), channel_id=1, source_target_pairs={{0,4},{4,0},{8,12},{12,8},{1,5},{5,1},{9,13},{13,9},{2,6},{6,2},{1... | collective-permute-start | bytes 184328 | tf_op jit(solution)/shard_map/ppermute | solution.py:128

commit v7 on v6

--- a/solution.py
+++ b/solution.py
@@ -201,9 +201,11 @@
                 hidden_grad * up_pre * logistic * (1.0 + gate_pre * (1.0 - logistic))
             ).astype(BF16)
             up_diff = (hidden_grad * swish).astype(BF16)
-            first_part = dot(gate_diff, gates[base + k], NT)
-            second_part = dot(ups[base + k], up_diff, NT).T
-            backs[heres[k]] = (first_part + second_part).astype(BF16)
+            for left in range(0, features, 512):
+                cut = slice(left, min(left + 512, features))
+                first_part = dot(gate_diff, gates[base + k, cut], NT)
+                second_part = dot(ups[base + k, cut], up_diff, NT).T
+                backs[heres[k], cut] = (first_part + second_part).astype(BF16)
             score = jnp.sum(swish * up_pre * hidden_grad, axis=1, keepdims=True)
             by_token = jnp.sum(spread[heres[k]].astype(F32) * score, axis=0, keepdims=True)
             here = (turn * group + k).astype(F32)

time: 75.3 us -> 73.5 us (0.976)
  Pallas kernels: 34.1 us -> 32.4 us
    pallas_call x1, Pallas kernels: 30.8 us -> 29 us  [run_experts(): pl.pallas_call(functools.partial(experts_kernel, features, rows, blocks,...]
where the time goes in v7:
time: 73.5 us; the launch traced here: 73.2 us
  Pallas kernels  32.4 us (44%)
  starting transfers between devices  20 us (27%)
  waiting for transfers between devices  19.2 us (26%)
  between operations  0.75 us (1%)
    pallas_call x1, Pallas kernels, run_experts(): pl.pallas_call(functools.partial(experts_kernel, features, rows, blocks,...  29 us
    ppermute x21, starting transfers between devices, swap(): return lax.ppermute(value, axis, [(i, i ^ distance) for i in range(size)])  20 us
    ppermute x21, waiting for transfers between devices, swap(): return lax.ppermute(value, axis, [(i, i ^ distance) for i in range(size)])  19.2 us
    pallas_call x1, Pallas kernels, pack(): pl.pallas_call(pack_kernel, in_specs=[away, away, near, near], out_specs=...  1.56 us
  transfers between devices with their start and end apart: 21, of which 10 were waited for; matrix products, arithmetic and copies ran while one was open for 1% of the time, Pallas kernels for 1%

profile of v7, /device:TPU:0, one launch (start us, length us, event | category | flops | bytes accessed | tf_op | source)
XLA Modules:
  0.0 73.2 jit_solution(15704386823287031264)
XLA Ops:
  0.6 1.6 %pack.1.refs_0_ = bf16[16,3712]{1,0:T(8,128)(2,1)S(1)} custom-call(bf16[16,1792]{1,0:T(8,128)(2,1)} %norm_ref.3, bf16[16,1792]{1,0:T(8,128)(2,1)} %grad_ref.3, s32[8,16]{1,0:T(8,128)} %bitcast.4, bf16[8,16]{1,0:T(8,128)(2,1)} %bitcast.5), custom_call_target="tpu_custom_call" | custom-call | tf_op jit(solution)/shard_map/pack/pallas_call | solution.py:299
  2.2 4.1 %collective-permute-start.1 = (bf16[16,3712]{1,0:T(8,128)(2,1)S(1)}, bf16[16,3712]{1,0:T(8,128)(2,1)S(1)}, u32[]{:S(2)}, u32[]{:S(2)}) collective-permute-start(bf16[16,3712]{1,0:T(8,128)(2,1)S(1)} %pack.1.refs_0_), channel_id=1, source_target_pairs={{0,8},{4,12},{8,0},{12,4},{1,9},{5,13},{9,1},{13,5},{2,10},{6,14},... | collective-permute-start | bytes 356360 | tf_op jit(solution)/shard_map/ppermute | solution.py:128
  6.3 1.5 %collective-permute-start.3 = (bf16[16,3712]{1,0:T(8,128)(2,1)S(1)}, bf16[16,3712]{1,0:T(8,128)(2,1)S(1)}, u32[]{:S(2)}, u32[]{:S(2)}) collective-permute-start(bf16[16,3712]{1,0:T(8,128)(2,1)S(1)} %pack.1.refs_0_), channel_id=1, source_target_pairs={{0,2},{1,3},{2,0},{3,1},{4,6},{5,7},{6,4},{7,5},{8,10},{9,11},{10,... | collective-permute-start | bytes 356360 | tf_op jit(solution)/shard_map/ppermute | solution.py:128
  7.8 1.6 %collective-permute-start = (bf16[16,3712]{1,0:T(8,128)(2,1)S(1)}, bf16[16,3712]{1,0:T(8,128)(2,1)S(1)}, u32[]{:S(2)}, u32[]{:S(2)}) collective-permute-start(bf16[16,3712]{1,0:T(8,128)(2,1)S(1)} %pack.1.refs_0_), channel_id=1, source_target_pairs={{0,4},{4,0},{8,12},{12,8},{1,5},{5,1},{9,13},{13,9},{2,6},{6,2},{1... | collective-permute-start | bytes 356360 | tf_op jit(solution)/shard_map/ppermute | solution.py:128
  9.4 2.8 %collective-permute-done.1.refs_2_ = bf16[16,3712]{1,0:T(8,128)(2,1)S(1)} collective-permute-done((bf16[16,3712]{1,0:T(8,128)(2,1)S(1)}, bf16[16,3712]{1,0:T(8,128)(2,1)S(1)}, u32[]{:S(2)}, u32[]{:S(2)}) %collective-permute-start.1) | collective-permute-done | bytes 118816 | tf_op jit(solution)/shard_map/ppermute | solution.py:128
  12.2 1.5 %collective-permute-start.5 = (bf16[16,3712]{1,0:T(8,128)(2,1)S(1)}, bf16[16,3712]{1,0:T(8,128)(2,1)S(1)}, u32[]{:S(2)}, u32[]{:S(2)}) collective-permute-start(bf16[16,3712]{1,0:T(8,128)(2,1)S(1)} %collective-permute-done.1.refs_2_), channel_id=1, source_target_pairs={{0,2},{1,3},{2,0},{3,1},{4,6},{5,7},{6,4},{7,5},{8,10},{9,11},{10,... | collective-permute-start | bytes 356360 | tf_op jit(solution)/shard_map/ppermute | solution.py:128
  13.7 0.6 collective-permute-start.2
  14.3 0.5 collective-permute-start.11
  14.9 2.1 %collective-permute-done.5.refs_6_ = bf16[16,3712]{1,0:T(8,128)(2,1)S(1)} collective-permute-done((bf16[16,3712]{1,0:T(8,128)(2,1)S(1)}, bf16[16,3712]{1,0:T(8,128)(2,1)S(1)}, u32[]{:S(2)}, u32[]{:S(2)}) %collective-permute-start.5) | collective-permute-done | bytes 118816 | tf_op jit(solution)/shard_map/ppermute | solution.py:128
  17.0 1.6 %collective-permute-start.4 = (bf16[16,3712]{1,0:T(8,128)(2,1)S(1)}, bf16[16,3712]{1,0:T(8,128)(2,1)S(1)}, u32[]{:S(2)}, u32[]{:S(2)}) collective-permute-start(bf16[16,3712]{1,0:T(8,128)(2,1)S(1)} %collective-permute-done.refs_1_), channel_id=1, source_target_pairs={{0,2},{1,3},{2,0},{3,1},{4,6},{5,7},{6,4},{7,5},{8,10},{9,11},{10,... | collective-permute-start | bytes 356360 | tf_op jit(solution)/shard_map/ppermute | solution.py:128
  18.6 0.9 %collective-permute-start.6 = (bf16[16,3712]{1,0:T(8,128)(2,1)S(1)}, bf16[16,3712]{1,0:T(8,128)(2,1)S(1)}, u32[]{:S(2)}, u32[]{:S(2)}) collective-permute-start(bf16[16,3712]{1,0:T(8,128)(2,1)S(1)} %collective-permute-done.5.refs_6_), channel_id=1, source_target_pairs={{0,4},{4,0},{8,12},{12,8},{1,5},{5,1},{9,13},{13,9},{2,6},{6,2},{1... | collective-permute-start | bytes 356360 | tf_op jit(solution)/shard_map/ppermute | solution.py:128
  19.5 0.7 broadcast_in_dim.3.gate_ref
  20.2 1.0 %shared.1 = (f32[16,128]{1,0:T(8,128)S(1)}, f32[16,1792]{1,0:T(8,128)S(1)}) custom-call(bf16[16,1792]{1,0:T(8,128)(2,1)} %norm_ref.3, bf16[16,1792]{1,0:T(8,128)(2,1)} %grad_ref.3, bf16[16,1792]{1,0:T(8,128)(2,1)} %shared_ref.1, bf16[1,1792]{1,0:T(2,128)(2,1)S(1)} %broadcast_in_dim.3.gate_ref), custom_call_target="tpu_custom_call" | custom-call | tf_op jit(solution)/shard_map/shared/pallas_call | solution.py:336
  21.3 0.5 collective-permute-start.10
  21.9 0.4 collective-permute-start.12
  22.3 1.1 %collective-permute-done.6.refs_7_ = bf16[16,3712]{1,0:T(8,128)(2,1)S(1)} collective-permute-done((bf16[16,3712]{1,0:T(8,128)(2,1)S(1)}, bf16[16,3712]{1,0:T(8,128)(2,1)S(1)}, u32[]{:S(2)}, u32[]{:S(2)}) %collective-permute-start.6) | collective-permute-done | bytes 118816 | tf_op jit(solution)/shard_map/ppermute | solution.py:128
  23.5 1.3 %collective-permute-done.14.refs_15_ = bf16[16,3712]{1,0:T(8,128)(2,1)S(1)} collective-permute-done((bf16[16,3712]{1,0:T(8,128)(2,1)S(1)}, bf16[16,3712]{1,0:T(8,128)(2,1)S(1)}, u32[]{:S(2)}, u32[]{:S(2)}) %collective-permute-start.14) | collective-permute-done | bytes 118816 | tf_op jit(solution)/shard_map/ppermute | solution.py:128
  24.8 29.0 %experts.1 = (bf16[128,1920]{1,0:T(8,128)(2,1)S(1)}, bf16[128,1920]{1,0:T(8,128)(2,1)S(1)}) custom-call(bf16[16,3712]{1,0:T(8,128)(2,1)S(1)} %pack.1.refs_0_, bf16[16,3712]{1,0:T(8,128)(2,1)S(1)} %collective-permute-done.refs_1_, bf16[16,3712]{1,0:T(8,128)(2,1)S(1)} %collective-permute-done.1.refs_2_, bf16[16,3712]{1,0:T(8,128)(2,1)S(1)} %collective-permute-done.2.refs_3_, ...), custom_call_target="tpu_custom_call" | custom-call | tf_op jit(solution)/shard_map/experts/pallas_call | solution.py:249
  53.8 0.2 collective-permute-start.15
  54.0 1.7 %collective-permute-done.15 = bf16[128,1920]{1,0:T(8,128)(2,1)S(1)} collective-permute-done((bf16[128,1920]{1,0:T(8,128)(2,1)S(1)}, bf16[128,1920]{1,0:T(8,128)(2,1)S(1)}, u32[]{:S(2)}, u32[]{:S(2)}) %collective-permute-start.15) | collective-permute-done | bytes 491552 | tf_op jit(solution)/shard_map/ppermute | solution.py:128
  55.7 0.1 add_convert_fusion.total_ref
  55.9 0.9 %collective-permute-start.18 = (bf16[32,1920]{1,0:T(8,128)(2,1)S(1)}, bf16[32,1920]{1,0:T(8,128)(2,1)S(1)}, u32[]{:S(2)}, u32[]{:S(2)}) collective-permute-start(bf16[32,1920]{1,0:T(8,128)(2,1)S(1)} %pad_maximum_fusion), channel_id=1, source_target_pairs={{0,4},{4,0},{8,12},{12,8},{1,5},{5,1},{9,13},{13,9},{2,6},{6,2},{1... | collective-permute-start | bytes 368648 | tf_op jit(solution)/shard_map/ppermute | solution.py:128
  56.8 0.7 collective-permute-start.16
  57.5 3.9 %collective-permute-done.18 = bf16[32,1920]{1,0:T(8,128)(2,1)S(1)} collective-permute-done((bf16[32,1920]{1,0:T(8,128)(2,1)S(1)}, bf16[32,1920]{1,0:T(8,128)(2,1)S(1)}, u32[]{:S(2)}, u32[]{:S(2)}) %collective-permute-start.18) | collective-permute-done | bytes 122912 | tf_op jit(solution)/shard_map/ppermute | solution.py:128
  61.4 0.5 collective-permute-start.19
  61.9 0.1 collective-permute-done.16.refs_0_
  62.0 3.7 %collective-permute-done.19 = bf16[16,1920]{1,0:T(8,128)(2,1)S(1)} collective-permute-done((bf16[16,1920]{1,0:T(8,128)(2,1)S(1)}, bf16[16,1920]{1,0:T(8,128)(2,1)S(1)}, u32[]{:S(2)}, u32[]{:S(2)}) %collective-permute-start.19) | collective-permute-done | bytes 61472 | tf_op jit(solution)/shard_map/ppermute | solution.py:128
  65.7 2.6 %collective-permute-start.20 = (bf16[16,1920]{1,0:T(8,128)(2,1)S(1)}, bf16[16,1920]{1,0:T(8,128)(2,1)S(1)}, u32[]{:S(2)}, u32[]{:S(2)}) collective-permute-start(bf16[16,1920]{1,0:T(8,128)(2,1)S(1)} %get-tuple-element.23), channel_id=1, source_target_pairs={{0,8},{4,12},{8,0},{12,4},{1,9},{5,13},{9,1},{13,5},{2,10},{6,14},... | collective-permute-start | bytes 184328 | tf_op jit(solution)/shard_map/ppermute | solution.py:128
  68.3 1.7 %collective-permute-start.17 = (bf16[16,1920]{1,0:T(8,128)(2,1)S(1)}, bf16[16,1920]{1,0:T(8,128)(2,1)S(1)}, u32[]{:S(2)}, u32[]{:S(2)}) collective-permute-start(bf16[16,1920]{1,0:T(8,128)(2,1)S(1)} %get-tuple-element.24), channel_id=1, source_target_pairs={{0,4},{4,0},{8,12},{12,8},{1,5},{5,1},{9,13},{13,9},{2,6},{6,2},{1... | collective-permute-start | bytes 184328 | tf_op jit(solution)/shard_map/ppermute | solution.py:128
  70.0 0.9 %collective-permute-done.20.refs_2_ = bf16[16,1920]{1,0:T(8,128)(2,1)S(1)} collective-permute-done((bf16[16,1920]{1,0:T(8,128)(2,1)S(1)}, bf16[16,1920]{1,0:T(8,128)(2,1)S(1)}, u32[]{:S(2)}, u32[]{:S(2)}) %collective-permute-start.20) | collective-permute-done | bytes 61472 | tf_op jit(solution)/shard_map/ppermute | solution.py:128
  70.9 1.6 %collective-permute-done.17.refs_1_ = bf16[16,1920]{1,0:T(8,128)(2,1)S(1)} collective-permute-done((bf16[16,1920]{1,0:T(8,128)(2,1)S(1)}, bf16[16,1920]{1,0:T(8,128)(2,1)S(1)}, u32[]{:S(2)}, u32[]{:S(2)}) %collective-permute-start.17) | collective-permute-done | bytes 61472 | tf_op jit(solution)/shard_map/ppermute | solution.py:128
  72.5 0.7 %finish.1 = (bf16[16,1792]{1,0:T(8,128)(2,1)}, f32[8,16]{1,0:T(8,128)}, f32[14,128]{1,0:T(8,128)}) custom-call(bf16[128,1920]{1,0:T(8,128)(2,1)S(1)} %add_convert_fusion.total_ref, bf16[32,1920]{1,0:T(8,128)(2,1)S(1)} %collective-permute-done.16.refs_0_, bf16[16,1920]{1,0:T(8,128)(2,1)S(1)} %collective-permute-done.17.refs_1_, ...), custom_call_target="tpu_custom_call" | custom-call | tf_op jit(solution)/shard_map/finish/pallas_call | solution.py:374
  (21 shorter events, 0.4 us)
Async XLA Ops:
  2.2 10.0 %collective-permute-start.1 = (bf16[16,3712]{1,0:T(8,128)(2,1)S(1)}, bf16[16,3712]{1,0:T(8,128)(2,1)S(1)}, u32[]{:S(2)}, u32[]{:S(2)}) collective-permute-start(bf16[16,3712]{1,0:T(8,128)(2,1)S(1)} %pack.1.refs_0_), channel_id=1, source_target_pairs={{0,8},{4,12},{8,0},{12,4},{1,9},{5,13},{9,1},{13,5},{2,10},{6,14},... | collective-permute-start | bytes 356360 | tf_op jit(solution)/shard_map/ppermute | solution.py:128
  6.3 8.0 %collective-permute-start.3 = (bf16[16,3712]{1,0:T(8,128)(2,1)S(1)}, bf16[16,3712]{1,0:T(8,128)(2,1)S(1)}, u32[]{:S(2)}, u32[]{:S(2)}) collective-permute-start(bf16[16,3712]{1,0:T(8,128)(2,1)S(1)} %pack.1.refs_0_), channel_id=1, source_target_pairs={{0,2},{1,3},{2,0},{3,1},{4,6},{5,7},{6,4},{7,5},{8,10},{9,11},{10,... | collective-permute-start | bytes 356360 | tf_op jit(solution)/shard_map/ppermute | solution.py:128
  7.8 7.0 %collective-permute-start = (bf16[16,3712]{1,0:T(8,128)(2,1)S(1)}, bf16[16,3712]{1,0:T(8,128)(2,1)S(1)}, u32[]{:S(2)}, u32[]{:S(2)}) collective-permute-start(bf16[16,3712]{1,0:T(8,128)(2,1)S(1)} %pack.1.refs_0_), channel_id=1, source_target_pairs={{0,4},{4,0},{8,12},{12,8},{1,5},{5,1},{9,13},{13,9},{2,6},{6,2},{1... | collective-permute-start | bytes 356360 | tf_op jit(solution)/shard_map/ppermute | solution.py:128
  12.2 4.8 %collective-permute-start.5 = (bf16[16,3712]{1,0:T(8,128)(2,1)S(1)}, bf16[16,3712]{1,0:T(8,128)(2,1)S(1)}, u32[]{:S(2)}, u32[]{:S(2)}) collective-permute-start(bf16[16,3712]{1,0:T(8,128)(2,1)S(1)} %collective-permute-done.1.refs_2_), channel_id=1, source_target_pairs={{0,2},{1,3},{2,0},{3,1},{4,6},{5,7},{6,4},{7,5},{8,10},{9,11},{10,... | collective-permute-start | bytes 356360 | tf_op jit(solution)/shard_map/ppermute | solution.py:128
  13.7 4.9 %collective-permute-start.2 = (bf16[16,3712]{1,0:T(8,128)(2,1)S(1)}, bf16[16,3712]{1,0:T(8,128)(2,1)S(1)}, u32[]{:S(2)}, u32[]{:S(2)}) collective-permute-start(bf16[16,3712]{1,0:T(8,128)(2,1)S(1)} %collective-permute-done.1.refs_2_), channel_id=1, source_target_pairs={{0,4},{4,0},{8,12},{12,8},{1,5},{5,1},{9,13},{13,9},{2,6},{6,2},{1... | collective-permute-start | bytes 356360 | tf_op jit(solution)/shard_map/ppermute | solution.py:128
  14.3 6.9 %collective-permute-start.7 = (bf16[16,3712]{1,0:T(8,128)(2,1)S(1)}, bf16[16,3712]{1,0:T(8,128)(2,1)S(1)}, u32[]{:S(2)}, u32[]{:S(2)}) collective-permute-start(bf16[16,3712]{1,0:T(8,128)(2,1)S(1)} %pack.1.refs_0_), channel_id=1, source_target_pairs={{0,1},{1,0},{2,3},{3,2},{4,5},{5,4},{6,7},{7,6},{8,9},{9,8},{10,11... | collective-permute-start | bytes 356360 | tf_op jit(solution)/shard_map/ppermute | solution.py:128
  14.3 7.0 %collective-permute-start.11 = (bf16[16,3712]{1,0:T(8,128)(2,1)S(1)}, bf16[16,3712]{1,0:T(8,128)(2,1)S(1)}, u32[]{:S(2)}, u32[]{:S(2)}) collective-permute-start(bf16[16,3712]{1,0:T(8,128)(2,1)S(1)} %collective-permute-done.3.refs_4_), channel_id=1, source_target_pairs={{0,1},{1,0},{2,3},{3,2},{4,5},{5,4},{6,7},{7,6},{8,9},{9,8},{10,11... | collective-permute-start | bytes 356360 | tf_op jit(solution)/shard_map/ppermute | solution.py:128
  14.8 7.0 %collective-permute-start.9 = (bf16[16,3712]{1,0:T(8,128)(2,1)S(1)}, bf16[16,3712]{1,0:T(8,128)(2,1)S(1)}, u32[]{:S(2)}, u32[]{:S(2)}) collective-permute-start(bf16[16,3712]{1,0:T(8,128)(2,1)S(1)} %collective-permute-done.1.refs_2_), channel_id=1, source_target_pairs={{0,1},{1,0},{2,3},{3,2},{4,5},{5,4},{6,7},{7,6},{8,9},{9,8},{10,11... | collective-permute-start | bytes 356360 | tf_op jit(solution)/shard_map/ppermute | solution.py:128
  17.0 4.8 %collective-permute-start.4 = (bf16[16,3712]{1,0:T(8,128)(2,1)S(1)}, bf16[16,3712]{1,0:T(8,128)(2,1)S(1)}, u32[]{:S(2)}, u32[]{:S(2)}) collective-permute-start(bf16[16,3712]{1,0:T(8,128)(2,1)S(1)} %collective-permute-done.refs_1_), channel_id=1, source_target_pairs={{0,2},{1,3},{2,0},{3,1},{4,6},{5,7},{6,4},{7,5},{8,10},{9,11},{10,... | collective-permute-start | bytes 356360 | tf_op jit(solution)/shard_map/ppermute | solution.py:128
  18.6 4.8 %collective-permute-start.6 = (bf16[16,3712]{1,0:T(8,128)(2,1)S(1)}, bf16[16,3712]{1,0:T(8,128)(2,1)S(1)}, u32[]{:S(2)}, u32[]{:S(2)}) collective-permute-start(bf16[16,3712]{1,0:T(8,128)(2,1)S(1)} %collective-permute-done.5.refs_6_), channel_id=1, source_target_pairs={{0,4},{4,0},{8,12},{12,8},{1,5},{5,1},{9,13},{13,9},{2,6},{6,2},{1... | collective-permute-start | bytes 356360 | tf_op jit(solution)/shard_map/ppermute | solution.py:128
  21.2 2.2 %collective-permute-start.8 = (bf16[16,3712]{1,0:T(8,128)(2,1)S(1)}, bf16[16,3712]{1,0:T(8,128)(2,1)S(1)}, u32[]{:S(2)}, u32[]{:S(2)}) collective-permute-start(bf16[16,3712]{1,0:T(8,128)(2,1)S(1)} %collective-permute-done.refs_1_), channel_id=1, source_target_pairs={{0,1},{1,0},{2,3},{3,2},{4,5},{5,4},{6,7},{7,6},{8,9},{9,8},{10,11... | collective-permute-start | bytes 356360 | tf_op jit(solution)/shard_map/ppermute | solution.py:128
  21.3 2.2 %collective-permute-start.10 = (bf16[16,3712]{1,0:T(8,128)(2,1)S(1)}, bf16[16,3712]{1,0:T(8,128)(2,1)S(1)}, u32[]{:S(2)}, u32[]{:S(2)}) collective-permute-start(bf16[16,3712]{1,0:T(8,128)(2,1)S(1)} %collective-permute-done.2.refs_3_), channel_id=1, source_target_pairs={{0,1},{1,0},{2,3},{3,2},{4,5},{5,4},{6,7},{7,6},{8,9},{9,8},{10,11... | collective-permute-start | bytes 356360 | tf_op jit(solution)/shard_map/ppermute | solution.py:128
  21.8 1.7 %collective-permute-start.13 = (bf16[16,3712]{1,0:T(8,128)(2,1)S(1)}, bf16[16,3712]{1,0:T(8,128)(2,1)S(1)}, u32[]{:S(2)}, u32[]{:S(2)}) collective-permute-start(bf16[16,3712]{1,0:T(8,128)(2,1)S(1)} %collective-permute-done.5.refs_6_), channel_id=1, source_target_pairs={{0,1},{1,0},{2,3},{3,2},{4,5},{5,4},{6,7},{7,6},{8,9},{9,8},{10,11... | collective-permute-start | bytes 356360 | tf_op jit(solution)/shard_map/ppermute | solution.py:128
  21.9 1.6 %collective-permute-start.12 = (bf16[16,3712]{1,0:T(8,128)(2,1)S(1)}, bf16[16,3712]{1,0:T(8,128)(2,1)S(1)}, u32[]{:S(2)}, u32[]{:S(2)}) collective-permute-start(bf16[16,3712]{1,0:T(8,128)(2,1)S(1)} %collective-permute-done.4.refs_5_), channel_id=1, source_target_pairs={{0,1},{1,0},{2,3},{3,2},{4,5},{5,4},{6,7},{7,6},{8,9},{9,8},{10,11... | collective-permute-start | bytes 356360 | tf_op jit(solution)/shard_map/ppermute | solution.py:128
  23.4 1.3 %collective-permute-start.14 = (bf16[16,3712]{1,0:T(8,128)(2,1)S(1)}, bf16[16,3712]{1,0:T(8,128)(2,1)S(1)}, u32[]{:S(2)}, u32[]{:S(2)}) collective-permute-start(bf16[16,3712]{1,0:T(8,128)(2,1)S(1)} %collective-permute-done.6.refs_7_), channel_id=1, source_target_pairs={{0,1},{1,0},{2,3},{3,2},{4,5},{5,4},{6,7},{7,6},{8,9},{9,8},{10,11... | collective-permute-start | bytes 356360 | tf_op jit(solution)/shard_map/ppermute | solution.py:128
  53.8 1.9 %collective-permute-start.15 = (bf16[128,1920]{1,0:T(8,128)(2,1)S(1)}, bf16[128,1920]{1,0:T(8,128)(2,1)S(1)}, u32[]{:S(2)}, u32[]{:S(2)}) collective-permute-start(bf16[128,1920]{1,0:T(8,128)(2,1)S(1)} %get-tuple-element.18), channel_id=1, source_target_pairs={{0,1},{1,0},{2,3},{3,2},{4,5},{5,4},{6,7},{7,6},{8,9},{9,8},{10,11... | collective-permute-start | bytes 1474568 | tf_op jit(solution)/shard_map/ppermute | solution.py:128
  55.9 5.4 %collective-permute-start.18 = (bf16[32,1920]{1,0:T(8,128)(2,1)S(1)}, bf16[32,1920]{1,0:T(8,128)(2,1)S(1)}, u32[]{:S(2)}, u32[]{:S(2)}) collective-permute-start(bf16[32,1920]{1,0:T(8,128)(2,1)S(1)} %pad_maximum_fusion), channel_id=1, source_target_pairs={{0,4},{4,0},{8,12},{12,8},{1,5},{5,1},{9,13},{13,9},{2,6},{6,2},{1... | collective-permute-start | bytes 368648 | tf_op jit(solution)/shard_map/ppermute | solution.py:128
  56.8 5.2 %collective-permute-start.16 = (bf16[32,1920]{1,0:T(8,128)(2,1)S(1)}, bf16[32,1920]{1,0:T(8,128)(2,1)S(1)}, u32[]{:S(2)}, u32[]{:S(2)}) collective-permute-start(bf16[32,1920]{1,0:T(8,128)(2,1)S(1)} %slice.36), channel_id=1, source_target_pairs={{0,2},{1,3},{2,0},{3,1},{4,6},{5,7},{6,4},{7,5},{8,10},{9,11},{10,... | collective-permute-start | bytes 368648 | tf_op jit(solution)/shard_map/ppermute | solution.py:128
  61.4 4.3 %collective-permute-start.19 = (bf16[16,1920]{1,0:T(8,128)(2,1)S(1)}, bf16[16,1920]{1,0:T(8,128)(2,1)S(1)}, u32[]{:S(2)}, u32[]{:S(2)}) collective-permute-start(bf16[16,1920]{1,0:T(8,128)(2,1)S(1)} %add_convert_fusion.2), channel_id=1, source_target_pairs={{0,2},{1,3},{2,0},{3,1},{4,6},{5,7},{6,4},{7,5},{8,10},{9,11},{10,... | collective-permute-start | bytes 184328 | tf_op jit(solution)/shard_map/ppermute | solution.py:128
  65.7 5.2 %collective-permute-start.20 = (bf16[16,1920]{1,0:T(8,128)(2,1)S(1)}, bf16[16,1920]{1,0:T(8,128)(2,1)S(1)}, u32[]{:S(2)}, u32[]{:S(2)}) collective-permute-start(bf16[16,1920]{1,0:T(8,128)(2,1)S(1)} %get-tuple-element.23), channel_id=1, source_target_pairs={{0,8},{4,12},{8,0},{12,4},{1,9},{5,13},{9,1},{13,5},{2,10},{6,14},... | collective-permute-start | bytes 184328 | tf_op jit(solution)/shard_map/ppermute | solution.py:128
  68.3 4.2 %collective-permute-start.17 = (bf16[16,1920]{1,0:T(8,128)(2,1)S(1)}, bf16[16,1920]{1,0:T(8,128)(2,1)S(1)}, u32[]{:S(2)}, u32[]{:S(2)}) collective-permute-start(bf16[16,1920]{1,0:T(8,128)(2,1)S(1)} %get-tuple-element.24), channel_id=1, source_target_pairs={{0,4},{4,0},{8,12},{12,8},{1,5},{5,1},{9,13},{13,9},{2,6},{6,2},{1... | collective-permute-start | bytes 184328 | tf_op jit(solution)/shard_map/ppermute | solution.py:128

commit v8 on v7

--- a/solution.py
+++ b/solution.py
@@ -171,8 +171,11 @@
     for k in range(group):
         for copy in loads(1, k):
             copy.start()
-    norms[...] = dot(spread[...], together(slice(0, features))).astype(BF16)
-    grads[...] = dot(spread[...], together(slice(features, 2 * features))).astype(BF16)
+    for target, first in ((norms, 0), (grads, features)):
+        for left in range(0, features, 512):
+            right = min(left + 512, features)
+            piece = together(slice(first + left, first + right))
+            target[:, left:right] = dot(spread[...], piece).astype(BF16)
     routes[...] = jnp.zeros_like(routes)
 
     def run(turn, _):

time: 73.5 us -> 73.5 us (level)
  no operation moved by 1% of the time
where the time goes in v8:
time: 73.5 us; the launch traced here: 73.2 us
  Pallas kernels  32.4 us (44%)
  starting transfers between devices  20 us (27%)
  waiting for transfers between devices  19.2 us (26%)
  between operations  0.75 us (1%)
    pallas_call x1, Pallas kernels, run_experts(): pl.pallas_call(functools.partial(experts_kernel, features, rows, blocks,...  29 us
    ppermute x21, starting transfers between devices, swap(): return lax.ppermute(value, axis, [(i, i ^ distance) for i in range(size)])  20 us
    ppermute x21, waiting for transfers between devices, swap(): return lax.ppermute(value, axis, [(i, i ^ distance) for i in range(size)])  19.2 us
    pallas_call x1, Pallas kernels, pack(): pl.pallas_call(pack_kernel, in_specs=[away, away, near, near], out_specs=...  1.56 us
  transfers between devices with their start and end apart: 21, of which 10 were waited for; matrix products, arithmetic and copies ran while one was open for 1% of the time, Pallas kernels for 1%

profile of v8, /device:TPU:0, one launch (start us, length us, event | category | flops | bytes accessed | tf_op | source)
XLA Modules:
  0.0 73.2 jit_solution(1761399485394045054)
XLA Ops:
  0.6 1.6 %pack.1.refs_0_ = bf16[16,3712]{1,0:T(8,128)(2,1)S(1)} custom-call(bf16[16,1792]{1,0:T(8,128)(2,1)} %norm_ref.3, bf16[16,1792]{1,0:T(8,128)(2,1)} %grad_ref.3, s32[8,16]{1,0:T(8,128)} %bitcast.4, bf16[8,16]{1,0:T(8,128)(2,1)} %bitcast.5), custom_call_target="tpu_custom_call" | custom-call | tf_op jit(solution)/shard_map/pack/pallas_call | solution.py:302
  2.2 4.1 %collective-permute-start.1 = (bf16[16,3712]{1,0:T(8,128)(2,1)S(1)}, bf16[16,3712]{1,0:T(8,128)(2,1)S(1)}, u32[]{:S(2)}, u32[]{:S(2)}) collective-permute-start(bf16[16,3712]{1,0:T(8,128)(2,1)S(1)} %pack.1.refs_0_), channel_id=1, source_target_pairs={{0,8},{4,12},{8,0},{12,4},{1,9},{5,13},{9,1},{13,5},{2,10},{6,14},... | collective-permute-start | bytes 356360 | tf_op jit(solution)/shard_map/ppermute | solution.py:128
  6.3 1.5 %collective-permute-start.3 = (bf16[16,3712]{1,0:T(8,128)(2,1)S(1)}, bf16[16,3712]{1,0:T(8,128)(2,1)S(1)}, u32[]{:S(2)}, u32[]{:S(2)}) collective-permute-start(bf16[16,3712]{1,0:T(8,128)(2,1)S(1)} %pack.1.refs_0_), channel_id=1, source_target_pairs={{0,2},{1,3},{2,0},{3,1},{4,6},{5,7},{6,4},{7,5},{8,10},{9,11},{10,... | collective-permute-start | bytes 356360 | tf_op jit(solution)/shard_map/ppermute | solution.py:128
  7.8 1.6 %collective-permute-start = (bf16[16,3712]{1,0:T(8,128)(2,1)S(1)}, bf16[16,3712]{1,0:T(8,128)(2,1)S(1)}, u32[]{:S(2)}, u32[]{:S(2)}) collective-permute-start(bf16[16,3712]{1,0:T(8,128)(2,1)S(1)} %pack.1.refs_0_), channel_id=1, source_target_pairs={{0,4},{4,0},{8,12},{12,8},{1,5},{5,1},{9,13},{13,9},{2,6},{6,2},{1... | collective-permute-start | bytes 356360 | tf_op jit(solution)/shard_map/ppermute | solution.py:128
  9.4 2.8 %collective-permute-done.1.refs_2_ = bf16[16,3712]{1,0:T(8,128)(2,1)S(1)} collective-permute-done((bf16[16,3712]{1,0:T(8,128)(2,1)S(1)}, bf16[16,3712]{1,0:T(8,128)(2,1)S(1)}, u32[]{:S(2)}, u32[]{:S(2)}) %collective-permute-start.1) | collective-permute-done | bytes 118816 | tf_op jit(solution)/shard_map/ppermute | solution.py:128
  12.2 1.5 %collective-permute-start.5 = (bf16[16,3712]{1,0:T(8,128)(2,1)S(1)}, bf16[16,3712]{1,0:T(8,128)(2,1)S(1)}, u32[]{:S(2)}, u32[]{:S(2)}) collective-permute-start(bf16[16,3712]{1,0:T(8,128)(2,1)S(1)} %collective-permute-done.1.refs_2_), channel_id=1, source_target_pairs={{0,2},{1,3},{2,0},{3,1},{4,6},{5,7},{6,4},{7,5},{8,10},{9,11},{10,... | collective-permute-start | bytes 356360 | tf_op jit(solution)/shard_map/ppermute | solution.py:128
  13.7 0.6 collective-permute-start.2
  14.3 0.5 collective-permute-start.11
  14.9 2.1 %collective-permute-done.5.refs_6_ = bf16[16,3712]{1,0:T(8,128)(2,1)S(1)} collective-permute-done((bf16[16,3712]{1,0:T(8,128)(2,1)S(1)}, bf16[16,3712]{1,0:T(8,128)(2,1)S(1)}, u32[]{:S(2)}, u32[]{:S(2)}) %collective-permute-start.5) | collective-permute-done | bytes 118816 | tf_op jit(solution)/shard_map/ppermute | solution.py:128
  17.0 1.6 %collective-permute-start.4 = (bf16[16,3712]{1,0:T(8,128)(2,1)S(1)}, bf16[16,3712]{1,0:T(8,128)(2,1)S(1)}, u32[]{:S(2)}, u32[]{:S(2)}) collective-permute-start(bf16[16,3712]{1,0:T(8,128)(2,1)S(1)} %collective-permute-done.refs_1_), channel_id=1, source_target_pairs={{0,2},{1,3},{2,0},{3,1},{4,6},{5,7},{6,4},{7,5},{8,10},{9,11},{10,... | collective-permute-start | bytes 356360 | tf_op jit(solution)/shard_map/ppermute | solution.py:128
  18.6 0.9 %collective-permute-start.6 = (bf16[16,3712]{1,0:T(8,128)(2,1)S(1)}, bf16[16,3712]{1,0:T(8,128)(2,1)S(1)}, u32[]{:S(2)}, u32[]{:S(2)}) collective-permute-start(bf16[16,3712]{1,0:T(8,128)(2,1)S(1)} %collective-permute-done.5.refs_6_), channel_id=1, source_target_pairs={{0,4},{4,0},{8,12},{12,8},{1,5},{5,1},{9,13},{13,9},{2,6},{6,2},{1... | collective-permute-start | bytes 356360 | tf_op jit(solution)/shard_map/ppermute | solution.py:128
  19.5 0.7 broadcast_in_dim.3.gate_ref
  20.2 1.0 %shared.1 = (f32[16,128]{1,0:T(8,128)S(1)}, f32[16,1792]{1,0:T(8,128)S(1)}) custom-call(bf16[16,1792]{1,0:T(8,128)(2,1)} %norm_ref.3, bf16[16,1792]{1,0:T(8,128)(2,1)} %grad_ref.3, bf16[16,1792]{1,0:T(8,128)(2,1)} %shared_ref.1, bf16[1,1792]{1,0:T(2,128)(2,1)S(1)} %broadcast_in_dim.3.gate_ref), custom_call_target="tpu_custom_call" | custom-call | tf_op jit(solution)/shard_map/shared/pallas_call | solution.py:339
  21.3 0.5 collective-permute-start.10
  21.9 0.4 collective-permute-start.12
  22.3 1.1 %collective-permute-done.6.refs_7_ = bf16[16,3712]{1,0:T(8,128)(2,1)S(1)} collective-permute-done((bf16[16,3712]{1,0:T(8,128)(2,1)S(1)}, bf16[16,3712]{1,0:T(8,128)(2,1)S(1)}, u32[]{:S(2)}, u32[]{:S(2)}) %collective-permute-start.6) | collective-permute-done | bytes 118816 | tf_op jit(solution)/shard_map/ppermute | solution.py:128
  23.5 1.3 %collective-permute-done.14.refs_15_ = bf16[16,3712]{1,0:T(8,128)(2,1)S(1)} collective-permute-done((bf16[16,3712]{1,0:T(8,128)(2,1)S(1)}, bf16[16,3712]{1,0:T(8,128)(2,1)S(1)}, u32[]{:S(2)}, u32[]{:S(2)}) %collective-permute-start.14) | collective-permute-done | bytes 118816 | tf_op jit(solution)/shard_map/ppermute | solution.py:128
  24.8 29.0 %experts.1 = (bf16[128,1920]{1,0:T(8,128)(2,1)S(1)}, bf16[128,1920]{1,0:T(8,128)(2,1)S(1)}) custom-call(bf16[16,3712]{1,0:T(8,128)(2,1)S(1)} %pack.1.refs_0_, bf16[16,3712]{1,0:T(8,128)(2,1)S(1)} %collective-permute-done.refs_1_, bf16[16,3712]{1,0:T(8,128)(2,1)S(1)} %collective-permute-done.1.refs_2_, bf16[16,3712]{1,0:T(8,128)(2,1)S(1)} %collective-permute-done.2.refs_3_, ...), custom_call_target="tpu_custom_call" | custom-call | tf_op jit(solution)/shard_map/experts/pallas_call | solution.py:252
  53.8 0.2 collective-permute-start.15
  54.0 1.7 %collective-permute-done.15 = bf16[128,1920]{1,0:T(8,128)(2,1)S(1)} collective-permute-done((bf16[128,1920]{1,0:T(8,128)(2,1)S(1)}, bf16[128,1920]{1,0:T(8,128)(2,1)S(1)}, u32[]{:S(2)}, u32[]{:S(2)}) %collective-permute-start.15) | collective-permute-done | bytes 491552 | tf_op jit(solution)/shard_map/ppermute | solution.py:128
  55.7 0.1 add_convert_fusion.total_ref
  55.9 0.9 %collective-permute-start.18 = (bf16[32,1920]{1,0:T(8,128)(2,1)S(1)}, bf16[32,1920]{1,0:T(8,128)(2,1)S(1)}, u32[]{:S(2)}, u32[]{:S(2)}) collective-permute-start(bf16[32,1920]{1,0:T(8,128)(2,1)S(1)} %pad_maximum_fusion), channel_id=1, source_target_pairs={{0,4},{4,0},{8,12},{12,8},{1,5},{5,1},{9,13},{13,9},{2,6},{6,2},{1... | collective-permute-start | bytes 368648 | tf_op jit(solution)/shard_map/ppermute | solution.py:128
  56.8 0.6 collective-permute-start.16
  57.5 3.9 %collective-permute-done.18 = bf16[32,1920]{1,0:T(8,128)(2,1)S(1)} collective-permute-done((bf16[32,1920]{1,0:T(8,128)(2,1)S(1)}, bf16[32,1920]{1,0:T(8,128)(2,1)S(1)}, u32[]{:S(2)}, u32[]{:S(2)}) %collective-permute-start.18) | collective-permute-done | bytes 122912 | tf_op jit(solution)/shard_map/ppermute | solution.py:128
  61.4 0.5 collective-permute-start.19
  61.9 0.1 collective-permute-done.16.refs_0_
  62.0 3.7 %collective-permute-done.19 = bf16[16,1920]{1,0:T(8,128)(2,1)S(1)} collective-permute-done((bf16[16,1920]{1,0:T(8,128)(2,1)S(1)}, bf16[16,1920]{1,0:T(8,128)(2,1)S(1)}, u32[]{:S(2)}, u32[]{:S(2)}) %collective-permute-start.19) | collective-permute-done | bytes 61472 | tf_op jit(solution)/shard_map/ppermute | solution.py:128
  65.7 2.6 %collective-permute-start.20 = (bf16[16,1920]{1,0:T(8,128)(2,1)S(1)}, bf16[16,1920]{1,0:T(8,128)(2,1)S(1)}, u32[]{:S(2)}, u32[]{:S(2)}) collective-permute-start(bf16[16,1920]{1,0:T(8,128)(2,1)S(1)} %get-tuple-element.23), channel_id=1, source_target_pairs={{0,8},{4,12},{8,0},{12,4},{1,9},{5,13},{9,1},{13,5},{2,10},{6,14},... | collective-permute-start | bytes 184328 | tf_op jit(solution)/shard_map/ppermute | solution.py:128
  68.3 1.7 %collective-permute-start.17 = (bf16[16,1920]{1,0:T(8,128)(2,1)S(1)}, bf16[16,1920]{1,0:T(8,128)(2,1)S(1)}, u32[]{:S(2)}, u32[]{:S(2)}) collective-permute-start(bf16[16,1920]{1,0:T(8,128)(2,1)S(1)} %get-tuple-element.24), channel_id=1, source_target_pairs={{0,4},{4,0},{8,12},{12,8},{1,5},{5,1},{9,13},{13,9},{2,6},{6,2},{1... | collective-permute-start | bytes 184328 | tf_op jit(solution)/shard_map/ppermute | solution.py:128
  70.0 0.9 %collective-permute-done.20.refs_2_ = bf16[16,1920]{1,0:T(8,128)(2,1)S(1)} collective-permute-done((bf16[16,1920]{1,0:T(8,128)(2,1)S(1)}, bf16[16,1920]{1,0:T(8,128)(2,1)S(1)}, u32[]{:S(2)}, u32[]{:S(2)}) %collective-permute-start.20) | collective-permute-done | bytes 61472 | tf_op jit(solution)/shard_map/ppermute | solution.py:128
  70.9 1.6 %collective-permute-done.17.refs_1_ = bf16[16,1920]{1,0:T(8,128)(2,1)S(1)} collective-permute-done((bf16[16,1920]{1,0:T(8,128)(2,1)S(1)}, bf16[16,1920]{1,0:T(8,128)(2,1)S(1)}, u32[]{:S(2)}, u32[]{:S(2)}) %collective-permute-start.17) | collective-permute-done | bytes 61472 | tf_op jit(solution)/shard_map/ppermute | solution.py:128
  72.5 0.7 %finish.1 = (bf16[16,1792]{1,0:T(8,128)(2,1)}, f32[8,16]{1,0:T(8,128)}, f32[14,128]{1,0:T(8,128)}) custom-call(bf16[128,1920]{1,0:T(8,128)(2,1)S(1)} %add_convert_fusion.total_ref, bf16[32,1920]{1,0:T(8,128)(2,1)S(1)} %collective-permute-done.16.refs_0_, bf16[16,1920]{1,0:T(8,128)(2,1)S(1)} %collective-permute-done.17.refs_1_, ...), custom_call_target="tpu_custom_call" | custom-call | tf_op jit(solution)/shard_map/finish/pallas_call | solution.py:377
  (21 shorter events, 0.4 us)
Async XLA Ops:
  2.2 10.0 %collective-permute-start.1 = (bf16[16,3712]{1,0:T(8,128)(2,1)S(1)}, bf16[16,3712]{1,0:T(8,128)(2,1)S(1)}, u32[]{:S(2)}, u32[]{:S(2)}) collective-permute-start(bf16[16,3712]{1,0:T(8,128)(2,1)S(1)} %pack.1.refs_0_), channel_id=1, source_target_pairs={{0,8},{4,12},{8,0},{12,4},{1,9},{5,13},{9,1},{13,5},{2,10},{6,14},... | collective-permute-start | bytes 356360 | tf_op jit(solution)/shard_map/ppermute | solution.py:128
  6.3 8.0 %collective-permute-start.3 = (bf16[16,3712]{1,0:T(8,128)(2,1)S(1)}, bf16[16,3712]{1,0:T(8,128)(2,1)S(1)}, u32[]{:S(2)}, u32[]{:S(2)}) collective-permute-start(bf16[16,3712]{1,0:T(8,128)(2,1)S(1)} %pack.1.refs_0_), channel_id=1, source_target_pairs={{0,2},{1,3},{2,0},{3,1},{4,6},{5,7},{6,4},{7,5},{8,10},{9,11},{10,... | collective-permute-start | bytes 356360 | tf_op jit(solution)/shard_map/ppermute | solution.py:128
  7.8 7.0 %collective-permute-start = (bf16[16,3712]{1,0:T(8,128)(2,1)S(1)}, bf16[16,3712]{1,0:T(8,128)(2,1)S(1)}, u32[]{:S(2)}, u32[]{:S(2)}) collective-permute-start(bf16[16,3712]{1,0:T(8,128)(2,1)S(1)} %pack.1.refs_0_), channel_id=1, source_target_pairs={{0,4},{4,0},{8,12},{12,8},{1,5},{5,1},{9,13},{13,9},{2,6},{6,2},{1... | collective-permute-start | bytes 356360 | tf_op jit(solution)/shard_map/ppermute | solution.py:128
  12.2 4.8 %collective-permute-start.5 = (bf16[16,3712]{1,0:T(8,128)(2,1)S(1)}, bf16[16,3712]{1,0:T(8,128)(2,1)S(1)}, u32[]{:S(2)}, u32[]{:S(2)}) collective-permute-start(bf16[16,3712]{1,0:T(8,128)(2,1)S(1)} %collective-permute-done.1.refs_2_), channel_id=1, source_target_pairs={{0,2},{1,3},{2,0},{3,1},{4,6},{5,7},{6,4},{7,5},{8,10},{9,11},{10,... | collective-permute-start | bytes 356360 | tf_op jit(solution)/shard_map/ppermute | solution.py:128
  13.7 4.9 %collective-permute-start.2 = (bf16[16,3712]{1,0:T(8,128)(2,1)S(1)}, bf16[16,3712]{1,0:T(8,128)(2,1)S(1)}, u32[]{:S(2)}, u32[]{:S(2)}) collective-permute-start(bf16[16,3712]{1,0:T(8,128)(2,1)S(1)} %collective-permute-done.1.refs_2_), channel_id=1, source_target_pairs={{0,4},{4,0},{8,12},{12,8},{1,5},{5,1},{9,13},{13,9},{2,6},{6,2},{1... | collective-permute-start | bytes 356360 | tf_op jit(solution)/shard_map/ppermute | solution.py:128
  14.3 6.9 %collective-permute-start.7 = (bf16[16,3712]{1,0:T(8,128)(2,1)S(1)}, bf16[16,3712]{1,0:T(8,128)(2,1)S(1)}, u32[]{:S(2)}, u32[]{:S(2)}) collective-permute-start(bf16[16,3712]{1,0:T(8,128)(2,1)S(1)} %pack.1.refs_0_), channel_id=1, source_target_pairs={{0,1},{1,0},{2,3},{3,2},{4,5},{5,4},{6,7},{7,6},{8,9},{9,8},{10,11... | collective-permute-start | bytes 356360 | tf_op jit(solution)/shard_map/ppermute | solution.py:128
  14.3 7.0 %collective-permute-start.11 = (bf16[16,3712]{1,0:T(8,128)(2,1)S(1)}, bf16[16,3712]{1,0:T(8,128)(2,1)S(1)}, u32[]{:S(2)}, u32[]{:S(2)}) collective-permute-start(bf16[16,3712]{1,0:T(8,128)(2,1)S(1)} %collective-permute-done.3.refs_4_), channel_id=1, source_target_pairs={{0,1},{1,0},{2,3},{3,2},{4,5},{5,4},{6,7},{7,6},{8,9},{9,8},{10,11... | collective-permute-start | bytes 356360 | tf_op jit(solution)/shard_map/ppermute | solution.py:128
  14.8 7.0 %collective-permute-start.9 = (bf16[16,3712]{1,0:T(8,128)(2,1)S(1)}, bf16[16,3712]{1,0:T(8,128)(2,1)S(1)}, u32[]{:S(2)}, u32[]{:S(2)}) collective-permute-start(bf16[16,3712]{1,0:T(8,128)(2,1)S(1)} %collective-permute-done.1.refs_2_), channel_id=1, source_target_pairs={{0,1},{1,0},{2,3},{3,2},{4,5},{5,4},{6,7},{7,6},{8,9},{9,8},{10,11... | collective-permute-start | bytes 356360 | tf_op jit(solution)/shard_map/ppermute | solution.py:128
  17.0 4.8 %collective-permute-start.4 = (bf16[16,3712]{1,0:T(8,128)(2,1)S(1)}, bf16[16,3712]{1,0:T(8,128)(2,1)S(1)}, u32[]{:S(2)}, u32[]{:S(2)}) collective-permute-start(bf16[16,3712]{1,0:T(8,128)(2,1)S(1)} %collective-permute-done.refs_1_), channel_id=1, source_target_pairs={{0,2},{1,3},{2,0},{3,1},{4,6},{5,7},{6,4},{7,5},{8,10},{9,11},{10,... | collective-permute-start | bytes 356360 | tf_op jit(solution)/shard_map/ppermute | solution.py:128
  18.6 4.8 %collective-permute-start.6 = (bf16[16,3712]{1,0:T(8,128)(2,1)S(1)}, bf16[16,3712]{1,0:T(8,128)(2,1)S(1)}, u32[]{:S(2)}, u32[]{:S(2)}) collective-permute-start(bf16[16,3712]{1,0:T(8,128)(2,1)S(1)} %collective-permute-done.5.refs_6_), channel_id=1, source_target_pairs={{0,4},{4,0},{8,12},{12,8},{1,5},{5,1},{9,13},{13,9},{2,6},{6,2},{1... | collective-permute-start | bytes 356360 | tf_op jit(solution)/shard_map/ppermute | solution.py:128
  21.2 2.2 %collective-permute-start.8 = (bf16[16,3712]{1,0:T(8,128)(2,1)S(1)}, bf16[16,3712]{1,0:T(8,128)(2,1)S(1)}, u32[]{:S(2)}, u32[]{:S(2)}) collective-permute-start(bf16[16,3712]{1,0:T(8,128)(2,1)S(1)} %collective-permute-done.refs_1_), channel_id=1, source_target_pairs={{0,1},{1,0},{2,3},{3,2},{4,5},{5,4},{6,7},{7,6},{8,9},{9,8},{10,11... | collective-permute-start | bytes 356360 | tf_op jit(solution)/shard_map/ppermute | solution.py:128
  21.3 2.2 %collective-permute-start.10 = (bf16[16,3712]{1,0:T(8,128)(2,1)S(1)}, bf16[16,3712]{1,0:T(8,128)(2,1)S(1)}, u32[]{:S(2)}, u32[]{:S(2)}) collective-permute-start(bf16[16,3712]{1,0:T(8,128)(2,1)S(1)} %collective-permute-done.2.refs_3_), channel_id=1, source_target_pairs={{0,1},{1,0},{2,3},{3,2},{4,5},{5,4},{6,7},{7,6},{8,9},{9,8},{10,11... | collective-permute-start | bytes 356360 | tf_op jit(solution)/shard_map/ppermute | solution.py:128
  21.8 1.7 %collective-permute-start.13 = (bf16[16,3712]{1,0:T(8,128)(2,1)S(1)}, bf16[16,3712]{1,0:T(8,128)(2,1)S(1)}, u32[]{:S(2)}, u32[]{:S(2)}) collective-permute-start(bf16[16,3712]{1,0:T(8,128)(2,1)S(1)} %collective-permute-done.5.refs_6_), channel_id=1, source_target_pairs={{0,1},{1,0},{2,3},{3,2},{4,5},{5,4},{6,7},{7,6},{8,9},{9,8},{10,11... | collective-permute-start | bytes 356360 | tf_op jit(solution)/shard_map/ppermute | solution.py:128
  21.9 1.6 %collective-permute-start.12 = (bf16[16,3712]{1,0:T(8,128)(2,1)S(1)}, bf16[16,3712]{1,0:T(8,128)(2,1)S(1)}, u32[]{:S(2)}, u32[]{:S(2)}) collective-permute-start(bf16[16,3712]{1,0:T(8,128)(2,1)S(1)} %collective-permute-done.4.refs_5_), channel_id=1, source_target_pairs={{0,1},{1,0},{2,3},{3,2},{4,5},{5,4},{6,7},{7,6},{8,9},{9,8},{10,11... | collective-permute-start | bytes 356360 | tf_op jit(solution)/shard_map/ppermute | solution.py:128
  23.4 1.3 %collective-permute-start.14 = (bf16[16,3712]{1,0:T(8,128)(2,1)S(1)}, bf16[16,3712]{1,0:T(8,128)(2,1)S(1)}, u32[]{:S(2)}, u32[]{:S(2)}) collective-permute-start(bf16[16,3712]{1,0:T(8,128)(2,1)S(1)} %collective-permute-done.6.refs_7_), channel_id=1, source_target_pairs={{0,1},{1,0},{2,3},{3,2},{4,5},{5,4},{6,7},{7,6},{8,9},{9,8},{10,11... | collective-permute-start | bytes 356360 | tf_op jit(solution)/shard_map/ppermute | solution.py:128
  53.8 1.9 %collective-permute-start.15 = (bf16[128,1920]{1,0:T(8,128)(2,1)S(1)}, bf16[128,1920]{1,0:T(8,128)(2,1)S(1)}, u32[]{:S(2)}, u32[]{:S(2)}) collective-permute-start(bf16[128,1920]{1,0:T(8,128)(2,1)S(1)} %get-tuple-element.18), channel_id=1, source_target_pairs={{0,1},{1,0},{2,3},{3,2},{4,5},{5,4},{6,7},{7,6},{8,9},{9,8},{10,11... | collective-permute-start | bytes 1474568 | tf_op jit(solution)/shard_map/ppermute | solution.py:128
  55.9 5.4 %collective-permute-start.18 = (bf16[32,1920]{1,0:T(8,128)(2,1)S(1)}, bf16[32,1920]{1,0:T(8,128)(2,1)S(1)}, u32[]{:S(2)}, u32[]{:S(2)}) collective-permute-start(bf16[32,1920]{1,0:T(8,128)(2,1)S(1)} %pad_maximum_fusion), channel_id=1, source_target_pairs={{0,4},{4,0},{8,12},{12,8},{1,5},{5,1},{9,13},{13,9},{2,6},{6,2},{1... | collective-permute-start | bytes 368648 | tf_op jit(solution)/shard_map/ppermute | solution.py:128
  56.8 5.2 %collective-permute-start.16 = (bf16[32,1920]{1,0:T(8,128)(2,1)S(1)}, bf16[32,1920]{1,0:T(8,128)(2,1)S(1)}, u32[]{:S(2)}, u32[]{:S(2)}) collective-permute-start(bf16[32,1920]{1,0:T(8,128)(2,1)S(1)} %slice.36), channel_id=1, source_target_pairs={{0,2},{1,3},{2,0},{3,1},{4,6},{5,7},{6,4},{7,5},{8,10},{9,11},{10,... | collective-permute-start | bytes 368648 | tf_op jit(solution)/shard_map/ppermute | solution.py:128
  61.4 4.3 %collective-permute-start.19 = (bf16[16,1920]{1,0:T(8,128)(2,1)S(1)}, bf16[16,1920]{1,0:T(8,128)(2,1)S(1)}, u32[]{:S(2)}, u32[]{:S(2)}) collective-permute-start(bf16[16,1920]{1,0:T(8,128)(2,1)S(1)} %add_convert_fusion.2), channel_id=1, source_target_pairs={{0,2},{1,3},{2,0},{3,1},{4,6},{5,7},{6,4},{7,5},{8,10},{9,11},{10,... | collective-permute-start | bytes 184328 | tf_op jit(solution)/shard_map/ppermute | solution.py:128
  65.7 5.2 %collective-permute-start.20 = (bf16[16,1920]{1,0:T(8,128)(2,1)S(1)}, bf16[16,1920]{1,0:T(8,128)(2,1)S(1)}, u32[]{:S(2)}, u32[]{:S(2)}) collective-permute-start(bf16[16,1920]{1,0:T(8,128)(2,1)S(1)} %get-tuple-element.23), channel_id=1, source_target_pairs={{0,8},{4,12},{8,0},{12,4},{1,9},{5,13},{9,1},{13,5},{2,10},{6,14},... | collective-permute-start | bytes 184328 | tf_op jit(solution)/shard_map/ppermute | solution.py:128
  68.3 4.2 %collective-permute-start.17 = (bf16[16,1920]{1,0:T(8,128)(2,1)S(1)}, bf16[16,1920]{1,0:T(8,128)(2,1)S(1)}, u32[]{:S(2)}, u32[]{:S(2)}) collective-permute-start(bf16[16,1920]{1,0:T(8,128)(2,1)S(1)} %get-tuple-element.24), channel_id=1, source_target_pairs={{0,4},{4,0},{8,12},{12,8},{1,5},{5,1},{9,13},{13,9},{2,6},{6,2},{1... | collective-permute-start | bytes 184328 | tf_op jit(solution)/shard_map/ppermute | solution.py:128
